TPU v7x, 128 devices: a whole 4x4x4 slice. The times are simulated.
128 devices in a mesh: fsdp: 8 (over x_hi, y), ctx: 8 (over z, x_lo), tp: 2 (over core).
Axes of the slice: x: 4 (x_hi: 2, x_lo: 2; x = x_hi * 2 + x_lo), y: 4, z: 4, core: 2. Of those that a mesh axis runs over, the one named last changes fastest.
Arguments:
- tokens: float32 [8192, 1536], P(('fsdp', 'ctx')), may hold values from -6 to 6
- cotangent: float32 [8192, 1536], P(('fsdp', 'ctx')), may hold values from -6 to 6
- norm_attn: bfloat16 [1536], P('fsdp'), may hold values from 0.5 to 1.5
- qkv_weight: bfloat16 [1536, 2048], P('fsdp', 'tp'), may hold values from -0.15625 to 0.15625
- qkv_bias: bfloat16 [2, 1024], P('tp', 'fsdp'), may hold values from -3 to 3
- out_weight: bfloat16 [1536, 1536], P('tp', 'fsdp'), may hold values from -0.875 to 0.875
- norm_mlp: bfloat16 [1536], P('fsdp'), may hold values from 0.5 to 1.5
- gate_up_weight: bfloat16 [1536, 2, 8960], P('fsdp', None, 'tp'), may hold values from -0.15625 to 0.15625
- down_weight: bfloat16 [8960, 1536], P('tp', 'fsdp'), may hold values from -0.125 to 0.125
- lengths: int32 [8, 4], P('fsdp'), may hold values from 1 to 512, 1024 in all within a row
- deal: int32 [8, 1024], P('fsdp'), may hold values from 0 to 1023, as said below
Outputs:
- output: float32 [8192, 1536], P(('fsdp', 'ctx'))
- grad_tokens: float32 [8192, 1536], P(('fsdp', 'ctx'))
- grad_norm_attn: float32 [1536], P('fsdp')
- grad_qkv_weight: float32 [1536, 2048], P('fsdp', 'tp')
- grad_qkv_bias: float32 [2, 896], P('tp', 'fsdp')
- grad_value_bias: float32 [2, 128], P('tp', 'fsdp')
- grad_out_weight: float32 [1536, 1536], P('tp', 'fsdp')
- grad_norm_mlp: float32 [1536], P('fsdp')
- grad_gate_up_weight: float32 [1536, 2, 8960], P('fsdp', None, 'tp')
- grad_down_weight: float32 [8960, 1536], P('tp', 'fsdp')
Inputs may be any that keep to these rules, and one draw needn't show every extreme that they name: `lengths`: each row sums to 1024; its largest entry is 512. `deal`: each row is a permutation of the places of the pack; entry c * 128 + r lies between r * 8 and r * 8 + 7.
All inputs are finite; a program needn't handle non-finite values.
Results may differ from a plain program's by a relative error of at most 0.035.
Values may be sent and summed in bfloat16 or wider, within the bound.
No kernel may reach another device: no remote copies, remote signals or barrier semaphores. Data moves between devices by JAX's collectives and lax.ppermute only.
A program may use at most 256 MiB of HBM per device.

v0:
```python
import jax
import jax.numpy as jnp
from jax import lax
from jax.sharding import PartitionSpec as P

HEAD = 128
HEADS = 12
KV_HEADS = 2


EPS = 1e-06
THETA = 1000000.0


def contract(left, right, left_dim, right_dim):
    return lax.dot_general(
        left, right, (((left_dim,), (right_dim,)), ((), ())), preferred_element_type=jnp.float32
    )


def segment_of(places, seq_lengths):
    ends = jnp.cumsum(seq_lengths)
    starts = ends - seq_lengths
    inside = ((places[:, None] >= starts[None, :]) & (places[:, None] < ends[None, :])).astype(
        jnp.int32
    )
    segment = jnp.sum(inside * jnp.arange(seq_lengths.shape[0], dtype=jnp.int32)[None, :], axis=1)
    offset = places - jnp.sum(inside * starts[None, :], axis=1)
    return (segment, offset)


def rotary(offset, width):
    half = width // 2
    freqs = THETA ** (-(2.0 * jnp.arange(half, dtype=jnp.float32)) / width)
    angle = offset.astype(jnp.float32)[:, None] * freqs[None, :]
    cosine = jnp.concatenate([jnp.cos(angle), jnp.cos(angle)], axis=1)
    sine = jnp.concatenate([jnp.sin(angle), jnp.sin(angle)], axis=1)
    return (cosine, sine)


def rope_apply(values, cosine, sine):
    half = values.shape[-1] // 2
    turned = jnp.concatenate([-values[..., half:], values[..., :half]], axis=-1)
    return values * cosine + turned * sine


def rope_back(grads, cosine, sine):
    half = grads.shape[-1] // 2
    scaled = grads * sine
    turned = jnp.concatenate([scaled[..., half:], -scaled[..., :half]], axis=-1)
    return grads * cosine + turned


def rms_scale(values):
    return lax.rsqrt(jnp.mean(values * values, axis=-1, keepdims=True) + EPS)


def norm_back(values, scale, gain, incoming):
    weighted = incoming * gain
    gain_grad = jnp.sum(incoming * values * scale, axis=0)
    value_grad = scale * weighted - values * scale**3 * jnp.mean(
        weighted * values, axis=-1, keepdims=True
    )
    return (value_grad, gain_grad)


def score_block(query_low, keys_all, allowed_rows, factor):
    scores = contract(query_low, keys_all, 1, 1) * factor
    return jnp.where(allowed_rows, scores, -1e30)


def on_device(
    tokens,
    cotangent,
    norm_attn,
    qkv_weight,
    qkv_bias,
    out_weight,
    norm_mlp,
    gate_up_weight,
    down_weight,
    lengths,
    deal,
):
    count = tokens.shape[0]
    group_q = HEADS // KV_HEADS
    qcols = group_q * HEAD
    split_at = qcols + HEAD
    factor = HEAD ** (-0.5)
    places_all = deal[0]
    pack = places_all.shape[0]
    places = lax.dynamic_slice_in_dim(places_all, lax.axis_index("ctx") * count, count)
    seq_lengths = lengths[0]
    segment, offset = segment_of(places, seq_lengths)
    key_segment, _ = segment_of(places_all, seq_lengths)
    cosine, sine = rotary(offset, HEAD)
    allowed = (segment[:, None] == key_segment[None, :]) & (places_all[None, :] <= places[:, None])
    allowed_rows = jnp.broadcast_to(allowed[:, None, :], (count, group_q, pack)).reshape(
        count * group_q, pack
    )
    gain_a, w_qkv, b_qkv, w_out = (
        lax.all_gather(norm_attn, "fsdp", axis=0, tiled=True),
        lax.all_gather(qkv_weight, "fsdp", axis=0, tiled=True),
        lax.all_gather(qkv_bias, "fsdp", axis=1, tiled=True),
        lax.all_gather(out_weight, "fsdp", axis=1, tiled=True),
    )
    gain_m, w_gu, w_down = (
        lax.all_gather(norm_mlp, "fsdp", axis=0, tiled=True),
        lax.all_gather(gate_up_weight, "fsdp", axis=0, tiled=True),
        lax.all_gather(down_weight, "fsdp", axis=1, tiled=True),
    )
    scale_a = rms_scale(tokens)
    normed_low = (tokens * scale_a * gain_a.astype(jnp.float32)).astype(jnp.bfloat16)
    qkv = jnp.dot(normed_low, w_qkv, preferred_element_type=jnp.float32) + b_qkv[0].astype(
        jnp.float32
    )
    query = qkv[:, :qcols].reshape(count, group_q, HEAD)
    key = qkv[:, qcols : qcols + HEAD]
    value = qkv[:, qcols + HEAD :]
    query_low = (
        rope_apply(query, cosine[:, None, :], sine[:, None, :])
        .astype(jnp.bfloat16)
        .reshape(count * group_q, HEAD)
    )
    key_low = rope_apply(key, cosine, sine).astype(jnp.bfloat16)
    value_low = value.astype(jnp.bfloat16)
    keys_all, values_all = (
        lax.all_gather(key_low, "ctx", axis=0, tiled=True),
        lax.all_gather(value_low, "ctx", axis=0, tiled=True),
    )
    scores = score_block(query_low, keys_all, allowed_rows, factor)
    top = jnp.max(scores, axis=-1, keepdims=True)
    raised = jnp.exp(scores - top)
    total = jnp.sum(raised, axis=-1, keepdims=True)
    log_total = top + jnp.log(total)
    probs_low = (raised / total).astype(jnp.bfloat16)
    attended = jnp.dot(probs_low, values_all, preferred_element_type=jnp.float32)
    attended_low = attended.reshape(count, qcols).astype(jnp.bfloat16)
    branch = lax.psum(
        jnp.dot(attended_low, w_out, preferred_element_type=jnp.float32).astype(jnp.bfloat16), "tp"
    ).astype(jnp.float32)
    middle = tokens + branch
    scale_m = rms_scale(middle)
    normed2_low = (middle * scale_m * gain_m.astype(jnp.float32)).astype(jnp.bfloat16)
    width = w_gu.shape[0]
    gate_up = jnp.dot(
        normed2_low, w_gu.reshape(width, -1), preferred_element_type=jnp.float32
    ).reshape(count, 2, -1)
    gate = gate_up[:, 0]
    upward = gate_up[:, 1]
    sigmoid_gate = jax.nn.sigmoid(gate)
    activated = gate * sigmoid_gate
    hidden_low = (activated * upward).astype(jnp.bfloat16)
    mlp_out = lax.psum(
        jnp.dot(hidden_low, w_down, preferred_element_type=jnp.float32).astype(jnp.bfloat16), "tp"
    ).astype(jnp.float32)
    output = middle + mlp_out
    grad_low = cotangent.astype(jnp.bfloat16)
    held = lax.optimization_barrier((grad_low, norm_mlp, gate_up_weight, down_weight))
    gain_m, w_gu, w_down = (
        lax.all_gather(held[1], "fsdp", axis=0, tiled=True),
        lax.all_gather(held[2], "fsdp", axis=0, tiled=True),
        lax.all_gather(held[3], "fsdp", axis=1, tiled=True),
    )
    grad_hidden = contract(grad_low, w_down, 1, 1)
    grad_gate = grad_hidden * upward * sigmoid_gate * (1.0 + gate * (1.0 - sigmoid_gate))
    grad_up = grad_hidden * activated
    grad_gu_low = jnp.stack([grad_gate, grad_up], axis=1).astype(jnp.bfloat16).reshape(count, -1)
    grad_normed2 = lax.psum(
        contract(grad_gu_low, w_gu.reshape(width, -1), 1, 1).astype(jnp.bfloat16), "tp"
    ).astype(jnp.float32)
    middle_part, grad_gain_m = norm_back(middle, scale_m, gain_m.astype(jnp.float32), grad_normed2)
    grad_middle = cotangent + middle_part
    grad_branch_low = grad_middle.astype(jnp.bfloat16)
    held = lax.optimization_barrier((grad_branch_low, norm_attn, qkv_weight, qkv_bias, out_weight))
    gain_a, w_qkv, b_qkv, w_out = (
        lax.all_gather(held[1], "fsdp", axis=0, tiled=True),
        lax.all_gather(held[2], "fsdp", axis=0, tiled=True),
        lax.all_gather(held[3], "fsdp", axis=1, tiled=True),
        lax.all_gather(held[4], "fsdp", axis=1, tiled=True),
    )
    grad_att_low = (
        contract(grad_branch_low, w_out, 1, 1).astype(jnp.bfloat16).reshape(count * group_q, HEAD)
    )
    probs = jnp.exp(score_block(query_low, keys_all, allowed_rows, factor) - log_total)
    probs_again = probs.astype(jnp.bfloat16)
    grad_probs = contract(grad_att_low, values_all, 1, 1)
    grad_values = contract(probs_again, grad_att_low, 0, 0)
    grad_scores_low = (
        probs * (grad_probs - jnp.sum(probs * grad_probs, axis=-1, keepdims=True))
    ).astype(jnp.bfloat16)
    grad_query = jnp.dot(grad_scores_low, keys_all, preferred_element_type=jnp.float32) * factor
    grad_keys = contract(grad_scores_low, query_low, 0, 0) * factor
    grad_key_own, grad_value_own = (
        lax.psum_scatter(
            grad_keys.astype(jnp.bfloat16), "ctx", scatter_dimension=0, tiled=True
        ).astype(jnp.float32),
        lax.psum_scatter(
            grad_values.astype(jnp.bfloat16), "ctx", scatter_dimension=0, tiled=True
        ).astype(jnp.float32),
    )
    grad_query_pre = rope_back(
        grad_query.reshape(count, group_q, HEAD), cosine[:, None, :], sine[:, None, :]
    ).reshape(count, qcols)
    grad_key_pre = rope_back(grad_key_own, cosine, sine)
    grad_qkv_low = jnp.concatenate([grad_query_pre, grad_key_pre, grad_value_own], axis=1).astype(
        jnp.bfloat16
    )
    grad_normed = lax.psum(contract(grad_qkv_low, w_qkv, 1, 1).astype(jnp.bfloat16), "tp").astype(
        jnp.float32
    )
    token_part, grad_gain_a = norm_back(tokens, scale_a, gain_a.astype(jnp.float32), grad_normed)
    grad_tokens = grad_middle + token_part
    grad_down = contract(hidden_low, grad_low, 0, 0)
    grad_gu = contract(normed2_low, grad_gu_low, 0, 0).reshape(width, 2, -1)
    grad_out = contract(attended_low, grad_branch_low, 0, 0)
    grad_qkv = contract(normed_low, grad_qkv_low, 0, 0)
    bias_whole = jnp.sum(grad_qkv_low.astype(jnp.float32), axis=0)[None, :]
    grad_bias = bias_whole[:, :split_at]
    value_bias_grad = bias_whole[:, split_at:]
    shares = (
        lax.psum_scatter(grad_gain_a, ("fsdp", "ctx"), scatter_dimension=0, tiled=True),
        lax.psum_scatter(grad_qkv, ("fsdp", "ctx"), scatter_dimension=0, tiled=True),
        lax.psum_scatter(grad_bias, ("fsdp", "ctx"), scatter_dimension=1, tiled=True),
        lax.psum_scatter(value_bias_grad, ("fsdp", "ctx"), scatter_dimension=1, tiled=True),
        lax.psum_scatter(grad_out, ("fsdp", "ctx"), scatter_dimension=1, tiled=True),
        lax.psum_scatter(grad_gain_m, ("fsdp", "ctx"), scatter_dimension=0, tiled=True),
        lax.psum_scatter(grad_gu, ("fsdp", "ctx"), scatter_dimension=0, tiled=True),
        lax.psum_scatter(grad_down, ("fsdp", "ctx"), scatter_dimension=1, tiled=True),
    )
    shares = (
        lax.all_gather(shares[0].astype(jnp.bfloat16), "ctx", axis=0, tiled=True).astype(
            jnp.float32
        ),
        lax.all_gather(shares[1].astype(jnp.bfloat16), "ctx", axis=0, tiled=True).astype(
            jnp.float32
        ),
        lax.all_gather(shares[2].astype(jnp.bfloat16), "ctx", axis=1, tiled=True).astype(
            jnp.float32
        ),
        lax.all_gather(shares[3].astype(jnp.bfloat16), "ctx", axis=1, tiled=True).astype(
            jnp.float32
        ),
        lax.all_gather(shares[4].astype(jnp.bfloat16), "ctx", axis=1, tiled=True).astype(
            jnp.float32
        ),
        lax.all_gather(shares[5].astype(jnp.bfloat16), "ctx", axis=0, tiled=True).astype(
            jnp.float32
        ),
        lax.all_gather(shares[6].astype(jnp.bfloat16), "ctx", axis=0, tiled=True).astype(
            jnp.float32
        ),
        lax.all_gather(shares[7].astype(jnp.bfloat16), "ctx", axis=1, tiled=True).astype(
            jnp.float32
        ),
    )
    return (
        output,
        grad_tokens,
        shares[0],
        shares[1],
        shares[2],
        shares[3],
        shares[4],
        shares[5],
        shares[6],
        shares[7],
    )


def solution(mesh):
    in_specs = (
        P(("fsdp", "ctx"), None),
        P(("fsdp", "ctx"), None),
        P("fsdp"),
        P("fsdp", "tp"),
        P("tp", "fsdp"),
        P("tp", "fsdp"),
        P("fsdp"),
        P("fsdp", None, "tp"),
        P("tp", "fsdp"),
        P("fsdp", None),
        P("fsdp", None),
    )
    out_specs = (
        P(("fsdp", "ctx"), None),
        P(("fsdp", "ctx"), None),
        P("fsdp"),
        P("fsdp", "tp"),
        P("tp", "fsdp"),
        P("tp", "fsdp"),
        P("tp", "fsdp"),
        P("fsdp"),
        P("fsdp", None, "tp"),
        P("tp", "fsdp"),
    )
    return jax.shard_map(
        on_device, mesh=mesh, in_specs=in_specs, out_specs=out_specs, check_vma=False
    )
```

profile of v0, /device:TPU:1, one launch (start us, length us, event | category | flops | bytes accessed | tf_op | source)
XLA Modules:
  0.0 3957.2 jit_solution(4584169564995800849)
XLA Ops:
  10.2 20.7 all_gather.71
  37.3 30.1 all-reduce.15
  80.7 23.4 all_gather.73
  104.1 25.1 all_gather.72
  145.2 33.4 all-reduce.21.cloned.1.call-done
  181.3 279.8 %all-gather.15.cloned.1.call-done = bf16[1536,2,4480]{2,1,0:T(2,128)(2,1)} async-done(((bf16[192,2,4480]{2,1,0:T(2,128)(2,1)}), bf16[1536,2,4480]{2,1,0:T(2,128)(2,1)}) %all-gather.15.cloned.1.call-update) | async-done | bytes 27525136 | tf_op jit(solution)/shard_map/all_gather | solution.py:109
  461.2 67.3 %copy.73 = bf16[1536,2,4480]{0,2,1:T(8,128)(2,1)} copy(bf16[1536,2,4480]{2,1,0:T(2,128)(2,1)} %all-gather.15.cloned.1.call-done) | data formatting | bytes 55050240 | tf_op jit(solution)/shard_map/reshape | solution.py:147
  528.4 15.6 fusion
  544.0 73.0 %all-gather.19.cloned.1.call-done = bf16[4480,1536]{0,1:T(8,128)(2,1)} async-done(((bf16[4480,192]{0,1:T(8,128)(2,1)}), bf16[4480,1536]{0,1:T(8,128)(2,1)}) %all-gather.19.cloned.1.call-update) | async-done | bytes 13762576 | tf_op jit(solution)/shard_map/all_gather | solution.py:163
  617.0 10.4 multiply_bitcast_fusion.1
  627.4 270.1 %all-gather.21.cloned.1.call-done = bf16[1536,2,4480]{2,0,1:T(8,128)(2,1)} async-done(((bf16[192,2,4480]{2,0,1:T(8,128)(2,1)}), bf16[1536,2,4480]{2,0,1:T(8,128)(2,1)}) %all-gather.21.cloned.1.call-update) | async-done | bytes 27525136 | tf_op jit(solution)/shard_map/all_gather | solution.py:162
  897.6 15.3 fusion.3
  912.9 22.9 all-reduce.23.cloned.1.call-done
  942.6 54.5 %all-gather.23.cloned.1.call-done = bf16[768,1536]{0,1:T(8,128)(2,1)} async-done(((bf16[768,192]{0,1:T(8,128)(2,1)}), bf16[768,1536]{0,1:T(8,128)(2,1)}) %all-gather.23.cloned.1.call-update) | async-done | bytes 2359312 | tf_op jit(solution)/shard_map/all_gather | solution.py:180
  1014.6 11.2 fusion.53
  1033.3 24.7 fusion.5
  1058.9 94.0 %all-gather.17.cloned.1.call-done = bf16[4480,1536]{0,1:T(8,128)(2,1)} async-done(((bf16[4480,192]{0,1:T(8,128)(2,1)}), bf16[4480,1536]{0,1:T(8,128)(2,1)}) %all-gather.17.cloned.1.call-update) | async-done | bytes 13762576 | tf_op jit(solution)/shard_map/all_gather | solution.py:110
  1152.9 10.5 convolution_convert_fusion.1
  1165.1 20.8 reduce-scatter.12.cloned.1.call-done
  1187.8 36.5 reduce-scatter.14.cloned.1.call-done
  1225.2 66.9 %all-gather.25.cloned.1.call-done = bf16[1536,1024]{1,0:T(8,128)(2,1)} async-done(((bf16[192,1024]{1,0:T(8,128)(2,1)}), bf16[1536,1024]{1,0:T(8,128)(2,1)}) %all-gather.25.cloned.1.call-update) | async-done | bytes 3145744 | tf_op jit(solution)/shard_map/all_gather | solution.py:178
  1304.3 586.3 %reduce-scatter.22.cloned.1.call-done = f32[4480,24]{0,1:T(8,128)} async-done(((f32[4480,1536]{0,1:T(8,128)}), f32[4480,24]{0,1:T(8,128)}) %reduce-scatter.22.cloned.1.call-update) | async-done | bytes 430096
  1892.3 1174.7 %reduce-scatter.20.cloned.1.call-done = f32[24,2,4480]{2,0,1:T(8,128)} async-done(((f32[1536,2,4480]{2,0,1:T(8,128)}), f32[24,2,4480]{2,0,1:T(8,128)}) %reduce-scatter.20.cloned.1.call-update) | async-done | bytes 860176 | tf_op jit(solution)/shard_map/reduce_scatter | solution.py:228
  3074.4 20.4 all-reduce.3
  3097.7 298.6 %all-reduce.13 = (bf16[1536]{0:T(1024)(128)(2,1)S(1)}, bf16[1,896]{1,0:T(2,128)(2,1)S(1)}, bf16[1,128]{1,0:T(2,128)(2,1)S(1)}, bf16[1536]{0:T(1024)(128)(2,1)S(1)}) all-reduce(f32[1536]{0:T(1024)S(1)} %get-tuple-element.64, f32[1,896]{1,0:T(1,128)S(1)} %slice.76, ...), channel_id=4, replica_groups=mesh['fsdp'=8,'ctx'=8,'tp'=2] {'fsdp','ctx'}, use_global_device_ids=true, to_apply=%region_18.19.clone | all-reduce | flops 4096 | bytes 24576
  3397.5 13.4 all-reduce.14
  3417.0 24.3 all_gather.88
  3442.1 330.8 %reduce-scatter.16.cloned.1.call-done = f32[24,1024]{1,0:T(8,128)} async-done(((f32[1536,1024]{1,0:T(8,128)}), f32[24,1024]{1,0:T(8,128)}) %reduce-scatter.16.cloned.1.call-update) | async-done | bytes 98320 | tf_op jit(solution)/shard_map/reduce_scatter | solution.py:223
  3773.9 24.5 all_gather.85
  3799.3 65.4 %all-gather.29.cloned.1.call-done = bf16[4480,192]{0,1:T(8,128)(2,1)} async-done(((bf16[4480,24]{0,1:T(8,128)(2,1)}), bf16[4480,192]{0,1:T(8,128)(2,1)}) %all-gather.29.cloned.1.call-update) | async-done | bytes 1720336 | tf_op jit(solution)/shard_map/all_gather | solution.py:253
  3868.2 73.6 %all-gather.27.cloned.1.call-done = bf16[192,2,4480]{2,0,1:T(8,128)(2,1)} async-done(((bf16[24,2,4480]{2,0,1:T(8,128)(2,1)}), bf16[192,2,4480]{2,0,1:T(8,128)(2,1)}) %all-gather.27.cloned.1.call-update) | async-done | bytes 3440656 | tf_op jit(solution)/shard_map/all_gather | solution.py:250
  3941.8 8.4 copy.70
  (242 shorter events, 111.0 us)
Async XLA Ops:
  7.2 64.5 %copy-start = (f32[128,1536]{1,0:T(8,128)S(1)}, f32[128,1536]{1,0:T(8,128)}, u32[]{:S(2)}) copy-start(f32[128,1536]{1,0:T(8,128)} %param.11) | copy-start | bytes 2359300
  7.2 69.0 %all-gather.11.cloned.1.call-start = ((), (), s32[]{:S(2)}) async-start(), calls=%async_computation.6 | async-start | bytes 3538944 | tf_op jit(solution)/shard_map/all_gather | solution.py:103
  7.9 127.9 %all-gather.13.cloned.1.call-start = ((), (), s32[]{:S(2)}) async-start(), calls=%async_computation.7 | async-start | bytes 2654208 | tf_op jit(solution)/shard_map/all_gather | solution.py:105
  8.7 169.9 %all-reduce.21.cloned.1.call-start = ((), (), s32[]{:S(2)}) async-start(), calls=%async_computation.8 | async-start | bytes 786432 | tf_op jit(solution)/shard_map/psum | solution.py:139
  139.2 322.0 %all-gather.15.cloned.1.call-start = ((), (), s32[]{:S(2)}) async-start(), calls=%async_computation.9 | async-start | bytes 30965760 | tf_op jit(solution)/shard_map/all_gather | solution.py:109
  139.8 477.2 %all-gather.19.cloned.1.call-start = ((), (), s32[]{:S(2)}) async-start(), calls=%async_computation.11 | async-start | bytes 15482880 | tf_op jit(solution)/shard_map/all_gather | solution.py:163
  140.4 757.2 %all-gather.21.cloned.1.call-start = ((), (), s32[]{:S(2)}) async-start(), calls=%async_computation.12 | async-start | bytes 30965760 | tf_op jit(solution)/shard_map/all_gather | solution.py:162
  144.5 791.3 %all-reduce.23.cloned.1.call-start = ((), (), s32[]{:S(2)}) async-start(), calls=%async_computation.13 | async-start | bytes 786432 | tf_op jit(solution)/shard_map/psum | solution.py:169
  528.4 88.6 %copy-start.13 = (bf16[128,1536]{1,0:T(8,128)(2,1)S(1)}, bf16[128,1536]{1,0:T(8,128)(2,1)}, u32[]{:S(2)}) copy-start(bf16[128,1536]{1,0:T(8,128)(2,1)} %convert_element_type.172) | copy-start | bytes 1179652
  897.6 38.3 copy-start.31
  912.9 84.3 %all-gather.23.cloned.1.call-start = ((), (), s32[]{:S(2)}) async-start(), calls=%async_computation.14 | async-start | bytes 2654208 | tf_op jit(solution)/shard_map/all_gather | solution.py:180
  940.6 212.3 %all-gather.17.cloned.1.call-start = ((), (), s32[]{:S(2)}) async-start(), calls=%async_computation.10 | async-start | bytes 15482880 | tf_op jit(solution)/shard_map/all_gather | solution.py:110
  941.3 244.6 %reduce-scatter.12.cloned.1.call-start = ((), (), s32[]{:S(2)}) async-start(), calls=%async_computation.15 | async-start | bytes 294912 | tf_op jit(solution)/shard_map/reduce_scatter | solution.py:195
  1006.8 217.6 %reduce-scatter.14.cloned.1.call-start = ((), (), s32[]{:S(2)}) async-start(), calls=%async_computation.16 | async-start | bytes 294912 | tf_op jit(solution)/shard_map/reduce_scatter | solution.py:198
  1009.3 282.8 %all-gather.25.cloned.1.call-start = ((), (), s32[]{:S(2)}) async-start(), calls=%async_computation.17 | async-start | bytes 3538944 | tf_op jit(solution)/shard_map/all_gather | solution.py:178
  1009.9 880.6 %reduce-scatter.22.cloned.1.call-start = ((), (), s32[]{:S(2)}) async-start(), calls=%async_computation.23 | async-start | bytes 27955200
  1025.8 2041.2 %reduce-scatter.20.cloned.1.call-start = ((), (), s32[]{:S(2)}) async-start(), calls=%async_computation.20 | async-start | bytes 55910400 | tf_op jit(solution)/shard_map/reduce_scatter | solution.py:228
  1058.0 2038.4 %all-reduce.25.cloned.1.call-start = ((), (), s32[]{:S(2)}) async-start(), calls=%async_computation.24 | async-start | bytes 1572864 | tf_op jit(solution)/shard_map/psum | solution.py:154
  1058.9 104.5 %copy-start.4 = (bf16[768,1024]{1,0:T(8,128)(2,1)S(1)}, bf16[768,1024]{1,0:T(8,128)(2,1)}, u32[]{:S(2)}) copy-start(bf16[768,1024]{1,0:T(8,128)(2,1)} %copy-done.3) | copy-start | bytes 4718596
  1058.9 104.4 %copy-start.10 = (bf16[1024,128]{1,0:T(8,128)(2,1)S(1)}, bf16[1024,128]{1,0:T(8,128)(2,1)}, u32[]{:S(2)}) copy-start(bf16[1024,128]{1,0:T(8,128)(2,1)} %copy-done.9) | copy-start | bytes 786436
  1165.1 131.2 %copy-start.8 = (bf16[128,768]{1,0:T(8,128)(2,1)S(1)}, bf16[128,768]{1,0:T(8,128)(2,1)}, u32[]{:S(2)}) copy-start(bf16[128,768]{1,0:T(8,128)(2,1)} %copy-done.7) | copy-start | bytes 589828
  1296.0 2120.1 %reduce-scatter.18.cloned.1.call-start = ((), (), s32[]{:S(2)}) async-start(), calls=%async_computation.19 | async-start | bytes 4792320 | tf_op jit(solution)/shard_map/reduce_scatter | solution.py:226
  1299.3 2473.7 %reduce-scatter.16.cloned.1.call-start = ((), (), s32[]{:S(2)}) async-start(), calls=%async_computation.18 | async-start | bytes 6389760 | tf_op jit(solution)/shard_map/reduce_scatter | solution.py:223
  1304.2 1764.9 %copy-start.41 = (u32[128]{0:T(128)S(1)}, u32[128]{0:T(128)}, u32[]{:S(2)}) copy-start(u32[128]{0:T(128)} %constant.72) | copy-start | bytes 1540
  1304.2 1765.5 %copy-start.40 = (u32[128]{0:T(128)S(1)}, u32[128]{0:T(128)}, u32[]{:S(2)}) copy-start(u32[128]{0:T(128)} %constant.100) | copy-start | bytes 1540
  1304.2 1770.0 %copy-start.39 = (bf16[192]{0:T(256)(128)(2,1)S(1)}, bf16[192]{0:T(256)(128)(2,1)}, u32[]{:S(2)}) copy-start(bf16[192]{0:T(256)(128)(2,1)} %param.13) | copy-start | bytes 1156
  1304.2 1793.5 %copy-start.30 = (f32[1536]{0:T(1024)S(1)}, f32[1536]{0:T(1024)}, u32[]{:S(2)}) copy-start(f32[1536]{0:T(1024)} %get-tuple-element.62) | copy-start | bytes 18436
  1304.2 2110.7 %copy-start.6 = (f32[128,1536]{1,0:T(8,128)S(1)}, f32[128,1536]{1,0:T(8,128)}, u32[]{:S(2)}) copy-start(f32[128,1536]{1,0:T(8,128)} %get-tuple-element.82) | copy-start | bytes 2359300
  1304.2 2110.7 %copy-start.38 = (f32[128]{0:T(128)S(1)}, f32[128]{0:T(128)}, u32[]{:S(2)}) copy-start(f32[128]{0:T(128)} %get-tuple-element.100) | copy-start | bytes 1540
  1304.2 2560.5 %all-gather.29.cloned.1.call-start = ((), (), s32[]{:S(2)}) async-start(), calls=%async_computation.22 | async-start | bytes 1935360 | tf_op jit(solution)/shard_map/all_gather | solution.py:253
  1892.3 2049.5 %all-gather.27.cloned.1.call-start = ((), (), s32[]{:S(2)}) async-start(), calls=%async_computation.21 | async-start | bytes 3870720 | tf_op jit(solution)/shard_map/all_gather | solution.py:250
  3096.4 318.6 %copy-start.15 = (bf16[128,1536]{1,0:T(8,128)(2,1)S(1)}, bf16[128,1536]{1,0:T(8,128)(2,1)}, u32[]{:S(2)}) copy-start(bf16[128,1536]{1,0:T(8,128)(2,1)} %get-tuple-element.80) | copy-start | bytes 1179652
  (29 other events, 171.1 us)
Sparse Core Ops, SparseCore 0:
  10.3 65.8 all-gather.10
  78.5 57.3 all-gather.12
  139.3 39.1 all-reduce.20
  181.0 280.1 all-gather.14
  463.6 153.3 all-gather.18
  620.0 277.5 all-gather.20
  913.0 22.8 all-reduce.22
  940.7 56.4 all-gather.22
  999.5 153.3 all-gather.16
  1155.1 30.7 reduce-scatter.11
  1188.4 35.9 reduce-scatter.13
  1226.5 65.5 all-gather.24
  1294.6 595.9 reduce-scatter.21
  1893.0 1174.0 reduce-scatter.19
  3070.1 26.2 all-reduce.24
  3098.6 312.7 reduce-scatter.17
  3414.2 358.7 reduce-scatter.15
  3775.1 89.5 all-gather.28
  3866.5 75.2 all-gather.26
where the time goes:
time: 3970 us; the launch traced here: 3960 us
  waiting for transfers between devices  3190 us (80%)
  blocking collectives  480 us (12%)
  matrix products  116 us (3%)
  local copies, waits for them, and re-layouts  105 us (3%)
  other arithmetic  42.3 us (1%)
    reduce_scatter x1, waiting for transfers between devices, on_device(): lax.psum_scatter(grad_gu, ('fsdp', 'ctx'), scatter_dimension=0, tiled=True)  1170 us
    unnamed x20, waiting for transfers between devices  590 us
    unnamed x4, blocking collectives  362 us
    all_gather x2, waiting for transfers between devices, on_device(): lax.all_gather(held[2], 'fsdp', axis=0, tiled=True)  337 us
    reduce_scatter x1, waiting for transfers between devices, on_device(): lax.psum_scatter(grad_qkv, ('fsdp', 'ctx'), scatter_dimension=0, tiled=True)  331 us
    all_gather x1, waiting for transfers between devices, on_device(): lax.all_gather(gate_up_weight, 'fsdp', axis=0, tiled=True)  280 us
    all_gather x1, waiting for transfers between devices, on_device(): lax.all_gather(down_weight, 'fsdp', axis=1, tiled=True)  94 us
    dot_general x12, matrix products, contract(): lax.dot_general(left, right, (((left_dim,), (right_dim,)), ((), ())), pre...  82.5 us
  transfers between devices with their start and end apart: 19, of which 18 were waited for; matrix products, arithmetic and copies ran while one was open for 6% of the time, Pallas kernels for 0%

commit v1 on v0

v1 whole, which is shorter than its diff:
```python
import jax
import jax.numpy as jnp
from jax import lax
from jax.sharding import PartitionSpec as P

HEAD = 128
GROUP_Q = 6
EPS = 1e-06
THETA = 1000000.0

bf16 = jnp.bfloat16
f32 = jnp.float32

TP_SWAP = [(0, 1), (1, 0)]
BLOCK = 128


def contract(left, right, left_dim, right_dim):
    return lax.dot_general(
        left, right, (((left_dim,), (right_dim,)), ((), ())), preferred_element_type=f32
    )


def after(value, *others):
    return lax.optimization_barrier((value,) + others)[0]


def gather(own, axis):
    copies = jnp.broadcast_to(own[None], (8,) + own.shape)
    return lax.all_to_all(copies, axis, 0, 0, tiled=True)


def reduce(part, axis):
    return jnp.sum(lax.all_to_all(part, axis, 0, 0, tiled=True).astype(f32), axis=0)


def gather_rows(own):
    mine = gather(own, "ctx").reshape(-1, own.shape[1])
    other = lax.ppermute(mine, "tp", TP_SWAP)
    return jnp.concatenate([mine, other], axis=0)


def reduce_rows(part):
    rows, width = part.shape
    part = part.astype(bf16)
    half = rows // 2
    got = lax.ppermute(part[half:], "tp", TP_SWAP)
    both = (part[:half].astype(f32) + got.astype(f32)).astype(bf16)
    return reduce(both.reshape(8, -1, width), "ctx")


def both_halves(own):
    t = lax.axis_index("tp")
    other = lax.ppermute(own, "tp", TP_SWAP)
    first = jnp.where(t == 0, own, other)
    second = jnp.where(t == 0, other, own)
    return jnp.concatenate([first, second], axis=0)


def segment_of(places, seq_lengths):
    ends = jnp.cumsum(seq_lengths)
    starts = ends - seq_lengths
    inside = ((places[:, None] >= starts[None, :]) & (places[:, None] < ends[None, :])).astype(
        jnp.int32
    )
    segment = jnp.sum(inside * jnp.arange(seq_lengths.shape[0], dtype=jnp.int32)[None, :], axis=1)
    offset = places - jnp.sum(inside * starts[None, :], axis=1)
    return (segment, offset)


def rotary(offset, width):
    half = width // 2
    freqs = THETA ** (-(2.0 * jnp.arange(half, dtype=f32)) / width)
    angle = offset.astype(f32)[:, None] * freqs[None, :]
    cosine = jnp.concatenate([jnp.cos(angle), jnp.cos(angle)], axis=1)
    sine = jnp.concatenate([jnp.sin(angle), jnp.sin(angle)], axis=1)
    return (cosine, sine)


def rope_apply(values, cosine, sine):
    half = values.shape[-1] // 2
    turned = jnp.concatenate([-values[..., half:], values[..., :half]], axis=-1)
    return values * cosine + turned * sine


def rope_back(grads, cosine, sine):
    half = grads.shape[-1] // 2
    scaled = grads * sine
    turned = jnp.concatenate([scaled[..., half:], -scaled[..., :half]], axis=-1)
    return grads * cosine + turned


def rms_scale(values):
    return lax.rsqrt(jnp.mean(values * values, axis=-1, keepdims=True) + EPS)


def norm_back(values, scale, gain, incoming):
    weighted = incoming * gain
    return scale * weighted - values * scale**3 * jnp.mean(
        weighted * values, axis=-1, keepdims=True
    )


def on_device(
    tokens,
    cotangent,
    norm_attn,
    qkv_weight,
    qkv_bias,
    out_weight,
    norm_mlp,
    gate_up_weight,
    down_weight,
    lengths,
    deal,
):
    f = lax.axis_index("fsdp")
    c = lax.axis_index("ctx")
    t = lax.axis_index("tp")
    count, width = tokens.shape
    own = count // 2
    shard = qkv_weight.shape[0]
    qcols = GROUP_Q * HEAD
    factor = HEAD ** (-0.5)
    has_head = c < GROUP_Q
    head = jnp.minimum(c, GROUP_Q - 1)

    tok = lax.dynamic_slice_in_dim(tokens, t * own, own)
    cot = lax.dynamic_slice_in_dim(cotangent, t * own, own)
    scale_a = rms_scale(tok)
    unit_own = (tok * scale_a).astype(bf16)
    grad_own = cot.astype(bf16)

    w_out_own = lax.dynamic_slice_in_dim(out_weight, head * HEAD, HEAD).T
    w_out_own = jnp.where(has_head, w_out_own, jnp.zeros_like(w_out_own))
    att_own = jnp.concatenate(
        [
            lax.dynamic_slice_in_dim(qkv_weight, head * HEAD, HEAD, axis=1),
            qkv_weight[:, qcols:],
            w_out_own,
        ],
        axis=1,
    )
    row = jnp.concatenate([norm_attn, norm_mlp, qkv_bias[0]])[None]
    att_own = jnp.concatenate([att_own, row, jnp.zeros((15, row.shape[1]), bf16)], axis=0)
    att_all = gather(att_own, "fsdp")
    w_att = att_all[:, :shard].reshape(width, -1)
    w_qkv = w_att[:, : 3 * HEAD]
    w_out = w_att[:, 3 * HEAD :]
    extra = att_all[:, shard].astype(f32)
    gain_a = extra[:, :shard].reshape(width)
    gain_m = extra[:, shard : 2 * shard].reshape(width)
    bias_all = extra[:, 2 * shard :].reshape(-1)
    bias = jnp.concatenate([lax.dynamic_slice_in_dim(bias_all, head * HEAD, HEAD), bias_all[qcols:]])

    start = jnp.maximum(4 * c, 5 * c - 5) * BLOCK
    units = 5 * BLOCK
    gu_own = lax.dynamic_slice_in_dim(gate_up_weight, start, units, axis=2)
    inside = (jnp.arange(units) < 4 * BLOCK) | (c >= 5)
    gu_own = jnp.where(inside, gu_own, jnp.zeros_like(gu_own))
    down_own = lax.dynamic_slice_in_dim(down_weight, start, units).T
    w_ffn = lax.all_gather(
        jnp.concatenate([gu_own[:, 0], gu_own[:, 1], down_own], axis=1), "fsdp", axis=0, tiled=True
    )
    w_gu = w_ffn[:, : 2 * units]
    w_down = w_ffn[:, 2 * units :]

    deal_all = deal[0].reshape(8, 2, own)[:, t ^ jnp.arange(2)]
    places = jnp.transpose(deal_all, (1, 0, 2)).reshape(-1)
    segment, offset = segment_of(places, lengths[0])
    cosine, sine = rotary(offset, HEAD)
    allowed = (segment[:, None] == segment[None, :]) & (places[None, :] <= places[:, None])

    unit_all = gather_rows(unit_own)
    normed = (unit_all.astype(f32) * gain_a).astype(bf16)
    grad_all = gather_rows(after(grad_own, unit_all))
    qkv = contract(normed, w_qkv, 1, 0) + bias
    query = rope_apply(qkv[:, :HEAD], cosine, sine).astype(bf16)
    key = rope_apply(qkv[:, HEAD : 2 * HEAD], cosine, sine).astype(bf16)
    value = qkv[:, 2 * HEAD :].astype(bf16)
    scores = jnp.where(allowed, contract(query, key, 1, 1) * factor, -1e30)
    raised = jnp.exp(scores - jnp.max(scores, axis=-1, keepdims=True))
    probs = raised / jnp.sum(raised, axis=-1, keepdims=True)
    probs_low = probs.astype(bf16)
    attended = contract(probs_low, value, 1, 0).astype(bf16)
    branch = reduce_rows(contract(attended, w_out, 1, 1))
    middle = tok + branch
    scale_m = rms_scale(middle)
    normed2 = gather_rows((middle * scale_m * gain_m).astype(bf16))

    gate_up = contract(normed2, w_gu, 1, 0)
    gate, upward = gate_up[:, :units], gate_up[:, units:]
    sigmoid = jax.nn.sigmoid(gate)
    activated = gate * sigmoid
    hidden = (activated * upward).astype(bf16)
    grad_hidden = contract(grad_all, w_down, 1, 0)
    grad_gate = grad_hidden * upward * sigmoid * (1.0 + gate * (1.0 - sigmoid))
    grad_up = grad_hidden * activated
    grad_gu = jnp.concatenate([grad_gate, grad_up], axis=1).astype(bf16)
    grad_normed2 = reduce_rows(contract(grad_gu, w_gu, 1, 1))
    mlp = reduce_rows(contract(hidden, w_down, 1, 1))
    output = both_halves(middle + mlp)

    def share(grad):
        mine = lax.psum_scatter(grad.astype(bf16), "fsdp", scatter_dimension=0, tiled=True)
        return gather(mine, "ctx")

    down_part = share(contract(grad_all, hidden, 0, 0))
    gu_part = share(contract(normed2, grad_gu, 0, 0))

    grad_middle = cot + norm_back(middle, scale_m, gain_m, grad_normed2)
    grad_branch = gather_rows(grad_middle.astype(bf16))
    grad_att = contract(grad_branch, w_out, 1, 0).astype(bf16)
    grad_probs = contract(grad_att, value, 1, 1)
    grad_value = contract(probs_low, grad_att, 0, 0)
    grad_scores = (
        probs * (grad_probs - jnp.sum(probs * grad_probs, axis=-1, keepdims=True))
    ).astype(bf16)
    grad_query = contract(grad_scores, key, 1, 0) * factor
    grad_key = contract(grad_scores, query, 0, 0) * factor
    grad_qkv = jnp.concatenate(
        [rope_back(grad_query, cosine, sine), rope_back(grad_key, cosine, sine), grad_value],
        axis=1,
    ).astype(bf16)
    grad_normed = reduce_rows(contract(grad_qkv, w_qkv, 1, 1))
    grad_tokens = both_halves(grad_middle + norm_back(tok, scale_a, gain_a, grad_normed))

    att_grads = jnp.concatenate(
        [contract(normed, grad_qkv, 0, 0), contract(grad_branch, attended, 0, 0)], axis=1
    ).reshape(8, shard, 4 * HEAD)
    sums = jnp.sum(grad_qkv.astype(f32), axis=0)
    sums = jnp.concatenate([sums, jnp.zeros((HEAD,), f32)])
    sums = jnp.broadcast_to(sums, (8, 1, 4 * HEAD))
    pad = jnp.zeros((8, 15, 4 * HEAD), f32)
    att_part = reduce(jnp.concatenate([att_grads, sums, pad], axis=1).astype(bf16), "fsdp")
    att_part = gather(att_part.astype(bf16), "ctx").astype(f32)
    heads = att_part[:GROUP_Q]
    kv_sum = jnp.sum(heads[:, : shard + 1, HEAD : 3 * HEAD], axis=0)
    q_cols = jnp.transpose(heads[:, : shard + 1, :HEAD], (1, 0, 2)).reshape(shard + 1, qcols)
    all_cols = jnp.concatenate([q_cols, kv_sum], axis=1)
    grad_qkv_weight = all_cols[:shard]
    bias_grad = all_cols[shard]
    split_at = qcols + HEAD
    own_bias = lax.dynamic_slice_in_dim(bias_grad, f * (split_at // 8), split_at // 8)[None]
    own_value = lax.dynamic_slice_in_dim(bias_grad, split_at + f * (HEAD // 8), HEAD // 8)[None]
    grad_out_weight = jnp.transpose(heads[:, :shard, 3 * HEAD :], (0, 2, 1)).reshape(qcols, shard)

    def joined(parts):
        return jnp.concatenate(
            [parts[i, :, : (4 if i < 5 else 5) * BLOCK] for i in range(8)], axis=1
        ).astype(f32)

    grad_gu_weight = jnp.stack([joined(gu_part[..., :units]), joined(gu_part[..., units:])], axis=1)
    grad_down_weight = joined(down_part).T

    gain_sums = jnp.stack(
        [
            jnp.sum(grad_qkv_weight * qkv_weight.astype(f32), axis=1) / norm_attn.astype(f32),
            jnp.sum(grad_gu_weight * gate_up_weight.astype(f32), axis=(1, 2))
            / norm_mlp.astype(f32),
        ]
    )
    gain_sums = gain_sums + lax.ppermute(gain_sums, "tp", TP_SWAP)

    return (
        output,
        grad_tokens,
        gain_sums[0],
        grad_qkv_weight,
        own_bias,
        own_value,
        grad_out_weight,
        gain_sums[1],
        grad_gu_weight,
        grad_down_weight,
    )


def solution(mesh):
    in_specs = (
        P(("fsdp", "ctx"), None),
        P(("fsdp", "ctx"), None),
        P("fsdp"),
        P("fsdp", "tp"),
        P("tp", "fsdp"),
        P("tp", "fsdp"),
        P("fsdp"),
        P("fsdp", None, "tp"),
        P("tp", "fsdp"),
        P("fsdp", None),
        P("fsdp", None),
    )
    out_specs = (
        P(("fsdp", "ctx"), None),
        P(("fsdp", "ctx"), None),
        P("fsdp"),
        P("fsdp", "tp"),
        P("tp", "fsdp"),
        P("tp", "fsdp"),
        P("tp", "fsdp"),
        P("fsdp"),
        P("fsdp", None, "tp"),
        P("tp", "fsdp"),
    )
    return jax.shard_map(
        on_device, mesh=mesh, in_specs=in_specs, out_specs=out_specs, check_vma=False
    )
```

time: 3970 us -> 545 us (0.14)
  the two profiles are of different devices: /device:TPU:1 before, /device:TPU:13 now
where the time goes in v1:
time: 545 us; the launch traced here: 534 us
  waiting for transfers between devices  241 us (44%)
  starting transfers between devices  79.3 us (15%)
  local copies, waits for them, and re-layouts  70 us (13%)
  matrix products  53.6 us (10%)
  other arithmetic  45.5 us (8%)
  blocking collectives  29.8 us (5%)
  between operations  15.4 us (3%)
    all_to_all x7, waiting for transfers between devices, gather(): return lax.all_to_all(copies, axis, 0, 0, tiled=True)  113 us
    all_to_all x5, waiting for transfers between devices, reduce(): lax.all_to_all(part, axis, 0, 0, tiled=True).astype(f32)  101 us
    dot_general x18, matrix products, contract(): lax.dot_general(left, right, (((left_dim,), (right_dim,)), ((), ())), pre...  53.6 us
    unnamed x132, local copies, waits for them, and re-layouts  44.3 us
    all_to_all x7, starting transfers between devices, gather(): return lax.all_to_all(copies, axis, 0, 0, tiled=True)  34.1 us
    all_to_all x1, blocking collectives, gather(): return lax.all_to_all(copies, axis, 0, 0, tiled=True)  29.8 us
    reduce_scatter x2, waiting for transfers between devices, share(): lax.psum_scatter(grad.astype(bf16), 'fsdp', scatter_dimension=0, tiled=True)  23.6 us
    all_to_all x5, starting transfers between devices, reduce(): lax.all_to_all(part, axis, 0, 0, tiled=True).astype(f32)  20.9 us
  transfers between devices with their start and end apart: 26, of which 15 were waited for; matrix products, arithmetic and copies ran while one was open for 25% of the time, Pallas kernels for 0%

profile of v1, /device:TPU:13, one launch (start us, length us, event | category | flops | bytes accessed | tf_op | source)
XLA Modules:
  0.0 534.5 jit_solution(10487694960224361917)
XLA Ops:
  11.9 5.8 %all-to-all-start = ((bf16[8,64,1536]{2,1,0:T(8,128)(2,1)}), bf16[8,64,1536]{2,1,0:T(8,128)(2,1)S(1)}, u32[]{:S(2)}, u32[]{:S(2)}) async-start(bf16[8,64,1536]{2,1,0:T(8,128)(2,1)} %broadcast_in_dim.36), calls=%async_computation | async-start | bytes 3145728 | tf_op jit(solution)/shard_map/all_to_all | solution.py:30
  19.3 4.1 copy.55
  28.1 10.1 %all-to-all-done = bf16[8,64,1536]{2,1,0:T(8,128)(2,1)S(1)} async-done(((bf16[8,64,1536]{2,1,0:T(8,128)(2,1)}), bf16[8,64,1536]{2,1,0:T(8,128)(2,1)S(1)}, u32[]{:S(2)}, u32[]{:S(2)}) %all-to-all-start) | async-done | bytes 1572896 | tf_op jit(solution)/shard_map/all_to_all | solution.py:30
  39.9 6.8 %all-to-all-start.1 = ((bf16[8,208,512]{2,1,0:T(8,128)(2,1)}), bf16[8,208,512]{2,1,0:T(8,128)(2,1)S(1)}, u32[]{:S(2)}, u32[]{:S(2)}) async-start(bf16[8,208,512]{2,1,0:T(8,128)(2,1)} %broadcast_in_dim.40), calls=%async_computation.1 | async-start | bytes 3407872 | tf_op jit(solution)/shard_map/all_to_all | solution.py:30
  55.4 14.8 %all-to-all-done.1 = bf16[8,208,512]{2,1,0:T(8,128)(2,1)S(1)} async-done(((bf16[8,208,512]{2,1,0:T(8,128)(2,1)}), bf16[8,208,512]{2,1,0:T(8,128)(2,1)S(1)}, u32[]{:S(2)}, u32[]{:S(2)}) %all-to-all-start.1) | async-done | bytes 1703968 | tf_op jit(solution)/shard_map/all_to_all | solution.py:30
  89.3 3.8 all-to-all-start.2
  93.2 38.3 %all-to-all-done.2 = bf16[8,64,1536]{2,1,0:T(8,128)(2,1)S(1)} async-done(((bf16[8,64,1536]{2,1,0:T(8,128)(2,1)}), bf16[8,64,1536]{2,1,0:T(8,128)(2,1)S(1)}, u32[]{:S(2)}, u32[]{:S(2)}) %all-to-all-start.2) | async-done | bytes 1572896 | tf_op jit(solution)/shard_map/all_to_all | solution.py:34
  133.2 3.6 all-to-all-start.3
  137.8 22.6 %all-to-all-done.3 = bf16[8,64,1536]{2,1,0:T(8,128)(2,1)S(1)} async-done(((bf16[8,64,1536]{2,1,0:T(8,128)(2,1)}), bf16[8,64,1536]{2,1,0:T(8,128)(2,1)S(1)}, u32[]{:S(2)}, u32[]{:S(2)}) %all-to-all-start.3) | async-done | bytes 1572896 | tf_op jit(solution)/shard_map/all_to_all | solution.py:30
  161.9 3.6 all-to-all-start.5
  166.5 19.4 %all-to-all-done.5 = bf16[8,64,1536]{2,1,0:T(8,128)(2,1)S(1)} async-done(((bf16[8,64,1536]{2,1,0:T(8,128)(2,1)}), bf16[8,64,1536]{2,1,0:T(8,128)(2,1)S(1)}, u32[]{:S(2)}, u32[]{:S(2)}) %all-to-all-start.5) | async-done | bytes 1572896 | tf_op jit(solution)/shard_map/all_to_all | solution.py:30
  188.2 7.0 %fusion.3 = f32[1024,1280]{1,0:T(8,128)S(1)} fusion(bf16[1536,1920]{1,0:T(8,128)(2,1)} %all-gather.2.cloned.1.call-done, bf16[512,1536]{1,0:T(8,128)(2,1)} %collective-permute-done.2, bf16[512,1536]{1,0:T(8,128)(2,1)S(1)} %bitcast.174), kind=kOutput, calls=%fused_computation.15 | convolution fusion | flops 4032823296 | bytes 12320768 | tf_op jit(solution)/shard_map/dot_general | solution.py:19
  195.2 4.7 multiply_convert_fusion.5
  199.9 4.5 convolution_convert_fusion.4
  216.9 17.6 %all-to-all-done.6 = bf16[8,64,1536]{2,1,0:T(8,128)(2,1)S(1)} async-done(((bf16[8,64,1536]{2,1,0:T(8,128)(2,1)}), bf16[8,64,1536]{2,1,0:T(8,128)(2,1)S(1)}, u32[]{:S(2)}, u32[]{:S(2)}) %all-to-all-start.6) | async-done | bytes 1572896 | tf_op jit(solution)/shard_map/all_to_all | solution.py:34
  238.3 6.2 %convolution_convert_fusion.5 = bf16[1536,640]{1,0:T(8,128)(2,1)} fusion(bf16[1024,640]{1,0:T(8,128)(2,1)} %copy-done.51, bf16[512,1536]{1,0:T(8,128)(2,1)} %collective-permute-done.5, bf16[512,1536]{1,0:T(8,128)(2,1)} %bitcast.178), kind=kOutput, calls=%fused_computation.19 | convolution fusion | flops 2020540416 | bytes 6422528 | tf_op jit(solution)/shard_map/dot_general | solution.py:19
  246.7 11.4 %all-to-all-done.4 = bf16[8,64,1536]{2,1,0:T(8,128)(2,1)S(1)} async-done(((bf16[8,64,1536]{2,1,0:T(8,128)(2,1)}), bf16[8,64,1536]{2,1,0:T(8,128)(2,1)S(1)}, u32[]{:S(2)}, u32[]{:S(2)}) %all-to-all-start.4) | async-done | bytes 1572896 | tf_op jit(solution)/shard_map/all_to_all | solution.py:34
  260.5 29.8 %all_to_all.65 = bf16[8,64,1536]{2,1,0:T(8,128)(2,1)} all-to-all(bf16[8,64,1536]{2,1,0:T(8,128)(2,1)S(1)} %broadcast_in_dim.46), channel_id=1, replica_groups=mesh['fsdp'=8,'ctx'=8,'tp'=2] {'ctx'}, dimensions={0} | all-to-all | bytes 3145728 | tf_op jit(solution)/shard_map/all_to_all | solution.py:30
  293.4 8.3 %convolution_convert_fusion = bf16[1536,1280]{1,0:T(8,128)(2,1)} fusion(bf16[512,1536]{1,0:T(8,128)(2,1)} %collective-permute-done.2, bf16[512,1536]{1,0:T(8,128)(2,1)S(1)} %bitcast.175, bf16[1024,640]{1,0:T(8,128)(2,1)S(1)} %copy-done.55, bf16[1024,640]{1,0:T(8,128)(2,1)S(1)} %copy-done.53), kind=kOutput, calls=%fused_computation.1 | convolution fusion | flops 4040032256 | bytes 9699328 | tf_op jit(solution)/shard_map/dot_general | solution.py:19
  301.7 18.1 %reduce-scatter.5.cloned.1.call-done = bf16[192,640]{1,0:T(8,128)(2,1)} async-done(((bf16[1536,640]{1,0:T(8,128)(2,1)}), bf16[192,640]{1,0:T(8,128)(2,1)}) %reduce-scatter.5.cloned.1.call-update) | async-done | bytes 245776 | tf_op jit(solution)/shard_map/reduce_scatter | solution.py:205
  322.1 6.0 %all-to-all-start.12 = ((bf16[8,192,640]{2,1,0:T(8,128)(2,1)}), bf16[8,192,640]{2,1,0:T(8,128)(2,1)}, u32[]{:S(2)}, u32[]{:S(2)}) async-start(bf16[8,192,640]{2,1,0:T(8,128)(2,1)} %broadcast_in_dim.51), calls=%async_computation.14 | async-start | bytes 3932160 | tf_op jit(solution)/shard_map/all_to_all | solution.py:30
  352.6 3.8 all-to-all-done.12
  356.4 6.3 %all-to-all-start.9 = ((bf16[8,208,512]{2,1,0:T(8,128)(2,1)}), bf16[8,208,512]{2,1,0:T(8,128)(2,1)S(1)}, u32[]{:S(2)}, u32[]{:S(2)}) async-start(bf16[8,208,512]{2,1,0:T(8,128)(2,1)} %maximum_maximum_fusion), calls=%async_computation.9 | async-start | bytes 3407872 | tf_op jit(solution)/shard_map/all_to_all | solution.py:34
  362.7 6.6 %collective-permute-start.4 = (f32[64,1536]{1,0:T(8,128)}, f32[64,1536]{1,0:T(8,128)}, u32[]{:S(2)}, u32[]{:S(2)}) collective-permute-start(f32[64,1536]{1,0:T(8,128)} %get-tuple-element.95), channel_id=1, source_target_pairs={{0,1},{1,0},{2,3},{3,2},{4,5},{5,4},{6,7},{7,6},{8,9},{9,8},{10,11... | collective-permute-start | bytes 1179656 | tf_op jit(solution)/shard_map/ppermute | solution.py:54
  372.8 13.8 %all-to-all-done.9 = bf16[8,208,512]{2,1,0:T(8,128)(2,1)S(1)} async-done(((bf16[8,208,512]{2,1,0:T(8,128)(2,1)}), bf16[8,208,512]{2,1,0:T(8,128)(2,1)S(1)}, u32[]{:S(2)}, u32[]{:S(2)}) %all-to-all-start.9) | async-done | bytes 1703968 | tf_op jit(solution)/shard_map/all_to_all | solution.py:34
  394.9 20.0 %all-to-all-done.8 = bf16[8,64,1536]{2,1,0:T(8,128)(2,1)S(1)} async-done(((bf16[8,64,1536]{2,1,0:T(8,128)(2,1)}), bf16[8,64,1536]{2,1,0:T(8,128)(2,1)S(1)}, u32[]{:S(2)}, u32[]{:S(2)}) %all-to-all-start.8) | async-done | bytes 1572896 | tf_op jit(solution)/shard_map/all_to_all | solution.py:34
  417.2 3.6 all-to-all-start.10
  432.5 5.6 %reduce-scatter.3.cloned.1.call-done = bf16[192,1280]{1,0:T(8,128)(2,1)} async-done(((bf16[1536,1280]{1,0:T(8,128)(2,1)}), bf16[192,1280]{1,0:T(8,128)(2,1)}) %reduce-scatter.3.cloned.1.call-update) | async-done | bytes 491536 | tf_op jit(solution)/shard_map/reduce_scatter | solution.py:205
  438.1 8.7 %all-to-all-done.10 = bf16[8,208,512]{2,1,0:T(8,128)(2,1)S(1)} async-done(((bf16[8,208,512]{2,1,0:T(8,128)(2,1)}), bf16[8,208,512]{2,1,0:T(8,128)(2,1)S(1)}, u32[]{:S(2)}, u32[]{:S(2)}) %all-to-all-start.10) | async-done | bytes 1703968 | tf_op jit(solution)/shard_map/all_to_all | solution.py:30
  450.0 4.8 all-to-all-start.11
  466.7 33.8 %all-to-all-done.11 = bf16[8,192,1280]{2,1,0:T(8,128)(2,1)} async-done(((bf16[8,192,1280]{2,1,0:T(8,128)(2,1)}), bf16[8,192,1280]{2,1,0:T(8,128)(2,1)}, u32[]{:S(2)}, u32[]{:S(2)}) %all-to-all-start.11) | async-done | bytes 3932192 | tf_op jit(solution)/shard_map/all_to_all | solution.py:30
  515.6 11.3 %copy.62 = f32[192,2,4480]{2,1,0:T(2,128)} copy(f32[192,2,4480]{2,0,1:T(8,128)} %maximum_convert_fusion) | data formatting | bytes 13762560
  (279 shorter events, 154.6 us)
Async XLA Ops:
  7.2 39.5 %copy-start = (bf16[4480,192]{0,1:T(8,128)(2,1)S(1)}, bf16[4480,192]{0,1:T(8,128)(2,1)}, u32[]{:S(2)}) copy-start(bf16[4480,192]{0,1:T(8,128)(2,1)} %param.19) | copy-start | bytes 5160964
  11.9 26.2 %all-to-all-start = ((bf16[8,64,1536]{2,1,0:T(8,128)(2,1)}), bf16[8,64,1536]{2,1,0:T(8,128)(2,1)S(1)}, u32[]{:S(2)}, u32[]{:S(2)}) async-start(bf16[8,64,1536]{2,1,0:T(8,128)(2,1)} %broadcast_in_dim.36), calls=%async_computation | async-start | bytes 3145728 | tf_op jit(solution)/shard_map/all_to_all | solution.py:30
  39.9 30.3 %all-to-all-start.1 = ((bf16[8,208,512]{2,1,0:T(8,128)(2,1)}), bf16[8,208,512]{2,1,0:T(8,128)(2,1)S(1)}, u32[]{:S(2)}, u32[]{:S(2)}) async-start(bf16[8,208,512]{2,1,0:T(8,128)(2,1)} %broadcast_in_dim.40), calls=%async_computation.1 | async-start | bytes 3407872 | tf_op jit(solution)/shard_map/all_to_all | solution.py:30
  46.6 141.6 %all-gather.2.cloned.1.call-start = ((), (), s32[]{:S(2)}) async-start(), calls=%async_computation.15 | async-start | bytes 6635520 | tf_op jit(solution)/shard_map/all_gather | solution.py:162
  51.1 19.5 %collective-permute-start = (bf16[512,1536]{1,0:T(8,128)(2,1)S(1)}, bf16[512,1536]{1,0:T(8,128)(2,1)}, u32[]{:S(2)}, u32[]{:S(2)}) collective-permute-start(bf16[512,1536]{1,0:T(8,128)(2,1)S(1)} %bitcast.170), channel_id=1, source_target_pairs={{0,1},{1,0},{2,3},{3,2},{4,5},{5,4},{6,7},{7,6},{8,9},{9,8},{10,11... | collective-permute-start | bytes 4718600 | tf_op jit(solution)/shard_map/ppermute | solution.py:39
  82.3 5.4 %collective-permute-start.1 = (bf16[512,1536]{1,0:T(8,128)(2,1)S(1)}, bf16[512,1536]{1,0:T(8,128)(2,1)S(1)}, u32[]{:S(2)}, u32[]{:S(2)}) collective-permute-start(bf16[512,1536]{1,0:T(8,128)(2,1)S(1)} %slice.309), channel_id=1, source_target_pairs={{0,1},{1,0},{2,3},{3,2},{4,5},{5,4},{6,7},{7,6},{8,9},{9,8},{10,11... | collective-permute-start | bytes 4718600 | tf_op jit(solution)/shard_map/ppermute | solution.py:47
  89.3 42.4 %copy-start.6 = (f32[128,1536]{1,0:T(8,128)S(1)}, f32[128,1536]{1,0:T(8,128)}, u32[]{:S(2)}) copy-start(f32[128,1536]{1,0:T(8,128)} %param.11) | copy-start | bytes 2359300
  89.3 42.2 %all-to-all-start.2 = ((bf16[8,64,1536]{2,1,0:T(8,128)(2,1)}), bf16[8,64,1536]{2,1,0:T(8,128)(2,1)S(1)}, u32[]{:S(2)}, u32[]{:S(2)}) async-start(bf16[8,64,1536]{2,1,0:T(8,128)(2,1)} %bitcast.11), calls=%async_computation.2 | async-start | bytes 3145728 | tf_op jit(solution)/shard_map/all_to_all | solution.py:34
  133.2 27.3 %all-to-all-start.3 = ((bf16[8,64,1536]{2,1,0:T(8,128)(2,1)}), bf16[8,64,1536]{2,1,0:T(8,128)(2,1)S(1)}, u32[]{:S(2)}, u32[]{:S(2)}) async-start(bf16[8,64,1536]{2,1,0:T(8,128)(2,1)} %broadcast_in_dim.42), calls=%async_computation.3 | async-start | bytes 3145728 | tf_op jit(solution)/shard_map/all_to_all | solution.py:30
  160.5 27.7 %copy-start.22 = (bf16[8,64,1536]{2,1,0:T(8,128)(2,1)}, bf16[8,64,1536]{2,1,0:T(8,128)(2,1)S(1)}, u32[]{:S(2)}) copy-start(bf16[8,64,1536]{2,1,0:T(8,128)(2,1)S(1)} %all-to-all-done.3) | copy-start | bytes 4718596
  161.9 24.0 %all-to-all-start.5 = ((bf16[8,64,1536]{2,1,0:T(8,128)(2,1)}), bf16[8,64,1536]{2,1,0:T(8,128)(2,1)S(1)}, u32[]{:S(2)}, u32[]{:S(2)}) async-start(bf16[8,64,1536]{2,1,0:T(8,128)(2,1)} %broadcast_in_dim.45), calls=%async_computation.5 | async-start | bytes 3145728 | tf_op jit(solution)/shard_map/all_to_all | solution.py:30
  165.5 22.7 %collective-permute-start.2 = (bf16[512,1536]{1,0:T(8,128)(2,1)S(1)}, bf16[512,1536]{1,0:T(8,128)(2,1)}, u32[]{:S(2)}, u32[]{:S(2)}) collective-permute-start(bf16[512,1536]{1,0:T(8,128)(2,1)S(1)} %bitcast.173), channel_id=1, source_target_pairs={{0,1},{1,0},{2,3},{3,2},{4,5},{5,4},{6,7},{7,6},{8,9},{9,8},{10,11... | collective-permute-start | bytes 4718600 | tf_op jit(solution)/shard_map/ppermute | solution.py:39
  185.9 9.3 %collective-permute-start.5 = (bf16[512,1536]{1,0:T(8,128)(2,1)S(1)}, bf16[512,1536]{1,0:T(8,128)(2,1)}, u32[]{:S(2)}, u32[]{:S(2)}) collective-permute-start(bf16[512,1536]{1,0:T(8,128)(2,1)S(1)} %bitcast.176), channel_id=1, source_target_pairs={{0,1},{1,0},{2,3},{3,2},{4,5},{5,4},{6,7},{7,6},{8,9},{9,8},{10,11... | collective-permute-start | bytes 4718600 | tf_op jit(solution)/shard_map/ppermute | solution.py:39
  204.6 3.7 collective-permute-start.6
  207.8 5.7 %collective-permute-start.3 = (bf16[512,1536]{1,0:T(8,128)(2,1)S(1)}, bf16[512,1536]{1,0:T(8,128)(2,1)}, u32[]{:S(2)}, u32[]{:S(2)}) collective-permute-start(bf16[512,1536]{1,0:T(8,128)(2,1)S(1)} %slice.318), channel_id=1, source_target_pairs={{0,1},{1,0},{2,3},{3,2},{4,5},{5,4},{6,7},{7,6},{8,9},{9,8},{10,11... | collective-permute-start | bytes 4718600 | tf_op jit(solution)/shard_map/ppermute | solution.py:47
  209.9 24.6 %all-to-all-start.6 = ((bf16[8,64,1536]{2,1,0:T(8,128)(2,1)}), bf16[8,64,1536]{2,1,0:T(8,128)(2,1)S(1)}, u32[]{:S(2)}, u32[]{:S(2)}) async-start(bf16[8,64,1536]{2,1,0:T(8,128)(2,1)} %bitcast.18), calls=%async_computation.6 | async-start | bytes 3145728 | tf_op jit(solution)/shard_map/all_to_all | solution.py:34
  234.4 23.6 %all-to-all-start.4 = ((bf16[8,64,1536]{2,1,0:T(8,128)(2,1)}), bf16[8,64,1536]{2,1,0:T(8,128)(2,1)S(1)}, u32[]{:S(2)}, u32[]{:S(2)}) async-start(bf16[8,64,1536]{2,1,0:T(8,128)(2,1)} %bitcast.16), calls=%async_computation.4 | async-start | bytes 3145728 | tf_op jit(solution)/shard_map/all_to_all | solution.py:34
  238.0 81.7 %reduce-scatter.5.cloned.1.call-start = ((), (), s32[]{:S(2)}) async-start(), calls=%async_computation.17 | async-start | bytes 2211840 | tf_op jit(solution)/shard_map/reduce_scatter | solution.py:205
  244.5 193.6 %reduce-scatter.3.cloned.1.call-start = ((), (), s32[]{:S(2)}) async-start(), calls=%async_computation.16 | async-start | bytes 4423680 | tf_op jit(solution)/shard_map/reduce_scatter | solution.py:205
  260.4 33.0 %copy-start.55 = (bf16[1024,640]{1,0:T(8,128)(2,1)S(1)}, bf16[1024,640]{1,0:T(8,128)(2,1)}, u32[]{:S(2)}) copy-start(bf16[1024,640]{1,0:T(8,128)(2,1)} %copy-done.54) | copy-start | bytes 3932164
  260.5 32.9 %copy-start.23 = (bf16[8,64,1536]{2,1,0:T(8,128)(2,1)S(1)}, bf16[8,64,1536]{2,1,0:T(8,128)(2,1)}, u32[]{:S(2)}) copy-start(bf16[8,64,1536]{2,1,0:T(8,128)(2,1)} %copy-done.22) | copy-start | bytes 4718596
  260.5 32.9 %copy-start.53 = (bf16[1024,640]{1,0:T(8,128)(2,1)S(1)}, bf16[1024,640]{1,0:T(8,128)(2,1)}, u32[]{:S(2)}) copy-start(bf16[1024,640]{1,0:T(8,128)(2,1)} %copy-done.52) | copy-start | bytes 3932164
  290.3 37.9 %collective-permute-start.7 = (bf16[512,1536]{1,0:T(8,128)(2,1)}, bf16[512,1536]{1,0:T(8,128)(2,1)S(1)}, u32[]{:S(2)}, u32[]{:S(2)}) collective-permute-start(bf16[512,1536]{1,0:T(8,128)(2,1)} %bitcast.19), channel_id=1, source_target_pairs={{0,1},{1,0},{2,3},{3,2},{4,5},{5,4},{6,7},{7,6},{8,9},{9,8},{10,11... | collective-permute-start | bytes 4718600 | tf_op jit(solution)/shard_map/ppermute | solution.py:39
  322.1 34.3 %all-to-all-start.12 = ((bf16[8,192,640]{2,1,0:T(8,128)(2,1)}), bf16[8,192,640]{2,1,0:T(8,128)(2,1)}, u32[]{:S(2)}, u32[]{:S(2)}) async-start(bf16[8,192,640]{2,1,0:T(8,128)(2,1)} %broadcast_in_dim.51), calls=%async_computation.14 | async-start | bytes 3932160 | tf_op jit(solution)/shard_map/all_to_all | solution.py:30
  341.5 27.8 %collective-permute-start.8 = (bf16[512,1536]{1,0:T(8,128)(2,1)}, bf16[512,1536]{1,0:T(8,128)(2,1)}, u32[]{:S(2)}, u32[]{:S(2)}) collective-permute-start(bf16[512,1536]{1,0:T(8,128)(2,1)} %slice.326), channel_id=1, source_target_pairs={{0,1},{1,0},{2,3},{3,2},{4,5},{5,4},{6,7},{7,6},{8,9},{9,8},{10,11... | collective-permute-start | bytes 4718600 | tf_op jit(solution)/shard_map/ppermute | solution.py:47
  356.4 30.2 %all-to-all-start.9 = ((bf16[8,208,512]{2,1,0:T(8,128)(2,1)}), bf16[8,208,512]{2,1,0:T(8,128)(2,1)S(1)}, u32[]{:S(2)}, u32[]{:S(2)}) async-start(bf16[8,208,512]{2,1,0:T(8,128)(2,1)} %maximum_maximum_fusion), calls=%async_computation.9 | async-start | bytes 3407872 | tf_op jit(solution)/shard_map/all_to_all | solution.py:34
  362.7 27.5 %collective-permute-start.4 = (f32[64,1536]{1,0:T(8,128)}, f32[64,1536]{1,0:T(8,128)}, u32[]{:S(2)}, u32[]{:S(2)}) collective-permute-start(f32[64,1536]{1,0:T(8,128)} %get-tuple-element.95), channel_id=1, source_target_pairs={{0,1},{1,0},{2,3},{3,2},{4,5},{5,4},{6,7},{7,6},{8,9},{9,8},{10,11... | collective-permute-start | bytes 1179656 | tf_op jit(solution)/shard_map/ppermute | solution.py:54
  386.6 28.3 %all-to-all-start.8 = ((bf16[8,64,1536]{2,1,0:T(8,128)(2,1)}), bf16[8,64,1536]{2,1,0:T(8,128)(2,1)S(1)}, u32[]{:S(2)}, u32[]{:S(2)}) async-start(bf16[8,64,1536]{2,1,0:T(8,128)(2,1)} %bitcast.161), calls=%async_computation.8 | async-start | bytes 3145728 | tf_op jit(solution)/shard_map/all_to_all | solution.py:34
  417.2 29.6 %all-to-all-start.10 = ((bf16[8,208,512]{2,1,0:T(8,128)(2,1)}), bf16[8,208,512]{2,1,0:T(8,128)(2,1)S(1)}, u32[]{:S(2)}, u32[]{:S(2)}) async-start(bf16[8,208,512]{2,1,0:T(8,128)(2,1)} %broadcast_in_dim.49), calls=%async_computation.10 | async-start | bytes 3407872 | tf_op jit(solution)/shard_map/all_to_all | solution.py:30
  450.0 50.4 %all-to-all-start.11 = ((bf16[8,192,1280]{2,1,0:T(8,128)(2,1)}), bf16[8,192,1280]{2,1,0:T(8,128)(2,1)}, u32[]{:S(2)}, u32[]{:S(2)}) async-start(bf16[8,192,1280]{2,1,0:T(8,128)(2,1)} %broadcast_in_dim.50), calls=%async_computation.12 | async-start | bytes 7864320 | tf_op jit(solution)/shard_map/all_to_all | solution.py:30
  459.7 5.9 %collective-permute-start.9 = (f32[64,1536]{1,0:T(8,128)S(1)}, f32[64,1536]{1,0:T(8,128)S(1)}, u32[]{:S(2)}, u32[]{:S(2)}) collective-permute-start(f32[64,1536]{1,0:T(8,128)S(1)} %subtract_add_fusion), channel_id=1, source_target_pairs={{0,1},{1,0},{2,3},{3,2},{4,5},{5,4},{6,7},{7,6},{8,9},{9,8},{10,11... | collective-permute-start | bytes 1179656 | tf_op jit(solution)/shard_map/ppermute | solution.py:54
  510.4 16.5 %collective-permute-start.10 = (f32[2,192]{1,0:T(2,128)S(1)}, f32[2,192]{1,0:T(2,128)S(1)}, u32[]{:S(2)}, u32[]{:S(2)}) collective-permute-start(f32[2,192]{1,0:T(2,128)S(1)} %pad_maximum_fusion.23), channel_id=1, source_target_pairs={{0,1},{1,0},{2,3},{3,2},{4,5},{5,4},{6,7},{7,6},{8,9},{9,8},{10,11... | collective-permute-start | bytes 4616 | tf_op jit(solution)/shard_map/ppermute | solution.py:263
  (50 other events, 190.7 us)
Sparse Core Ops, SparseCore 0:
  50.3 100.9 all-gather.1
  244.6 75.1 reduce-scatter.4
  324.2 113.8 reduce-scatter.2

commit v2 on v1

v2 whole, which is shorter than its diff:
```python
import jax
import jax.numpy as jnp
from jax import lax
from jax.experimental import pallas as pl
from jax.experimental.pallas import tpu as pltpu
from jax.sharding import PartitionSpec as P

HEAD = 128
GROUP_Q = 6
EPS = 1e-06
THETA = 1000000.0

bf16 = jnp.bfloat16
f32 = jnp.float32

BLOCK = 128
ROWS = 256
GRAD_ROWS = 64
VMEM_BYTES = 60 * 2**20
COST = pl.CostEstimate(flops=10**6, bytes_accessed=10**5, transcendentals=0)

TP_SWAP = [(0, 1), (1, 0)]
XH_SWAP = [(i, i ^ 4) for i in range(8)]
XL_SWAP = [(i, i ^ 1) for i in range(8)]
Y_GROUPS = [[0, 1, 2, 3], [4, 5, 6, 7]]
Z_GROUPS = [[0, 2, 4, 6], [1, 3, 5, 7]]


def y_shift(k):
    return [(h * 4 + y, h * 4 + (y + k) % 4) for h in range(2) for y in range(4)]


def contract(left, right, left_dim, right_dim):
    return lax.dot_general(
        left, right, (((left_dim,), (right_dim,)), ((), ())), preferred_element_type=f32
    )


def tie(*values):
    return lax.optimization_barrier(values)


def ordered(own, other, place):
    return jnp.stack([jnp.where(place == 0, own, other), jnp.where(place == 0, other, own)])


def gather(own, axis):
    copies = jnp.broadcast_to(own[None], (8,) + own.shape)
    return lax.all_to_all(copies, axis, 0, 0, tiled=True)


def reduce(part, axis):
    return jnp.sum(lax.all_to_all(part, axis, 0, 0, tiled=True).astype(f32), axis=0)


def gather_small(own, far):
    me = lax.axis_index("fsdp")
    hi, y = me // 4, me % 4
    out = jnp.zeros((8,) + own.shape, own.dtype)
    for d, base in ((0, own), (1, far)):
        out = lax.dynamic_update_index_in_dim(out, base, (hi ^ d) * 4 + y, 0)
        for k in (1, 3, 2):
            piece = lax.ppermute(base, "fsdp", y_shift(k))
            out = lax.dynamic_update_index_in_dim(out, piece, (hi ^ d) * 4 + (y - k + 4) % 4, 0)
    return out


def gather_along_y(own):
    return lax.all_gather(own, "fsdp", axis=0, axis_index_groups=Y_GROUPS, tiled=True)


def by_y(part):
    rows, width = part.shape
    return jnp.swapaxes(part.astype(bf16).reshape(2, 4, -1, width), 0, 1).reshape(rows, width)


def reduce_along_y(part):
    pair = lax.psum_scatter(
        part, "fsdp", scatter_dimension=0, axis_index_groups=Y_GROUPS, tiled=True
    )
    return pair.reshape(2, -1, part.shape[1])


def reduce_over_hi(pair):
    hi = lax.axis_index("fsdp") // 4
    kept = jnp.where(hi == 0, pair[0], pair[1])
    sent = jnp.where(hi == 0, pair[1], pair[0])
    return (kept.astype(f32) + lax.ppermute(sent, "fsdp", XH_SWAP).astype(f32)).astype(bf16)


def gather_along_z(own):
    return lax.all_gather(own, "ctx", axis=0, axis_index_groups=Z_GROUPS)


def reduce_along_z(part):
    pair = lax.psum_scatter(
        part, "ctx", scatter_dimension=0, axis_index_groups=Z_GROUPS, tiled=True
    )
    return pair.reshape(2, -1, part.shape[1])


def reduce_over_lo(pair):
    lo = lax.axis_index("ctx") % 2
    kept = jnp.where(lo == 0, pair[0], pair[1])
    sent = jnp.where(lo == 0, pair[1], pair[0])
    return kept.astype(f32) + lax.ppermute(sent, "ctx", XL_SWAP).astype(f32)


def gather_over_lo(own):
    return ordered(own, lax.ppermute(own, "ctx", XL_SWAP), lax.axis_index("ctx") % 2)


def both_cores(mine):
    mine = mine.reshape(-1, mine.shape[-1])
    return [mine, lax.ppermute(mine, "tp", TP_SWAP)]


def pair_sums(mine, other):
    got = lax.ppermute(other, "tp", TP_SWAP)
    total = (mine.astype(f32) + got.astype(f32)).astype(bf16)
    return total.reshape(8, -1, total.shape[1])


def over_rows(lefts, rights):
    return contract(lefts[0], rights[0], 0, 0) + contract(lefts[1], rights[1], 0, 0)


def both_halves(own):
    t = lax.axis_index("tp")
    other = lax.ppermute(own, "tp", TP_SWAP)
    first = jnp.where(t == 0, own, other)
    second = jnp.where(t == 0, other, own)
    return jnp.concatenate([first, second], axis=0)


def rope_in(values, cosine, sine):
    return values * cosine + pltpu.roll(values, HEAD // 2, 1) * sine


def rope_out(grads, cosine, sine):
    return grads * cosine - pltpu.roll(grads, HEAD // 2, 1) * sine


def masked_scores(query, key, first, last, places):
    scores = contract(query, key, 1, 1) * HEAD ** (-0.5)
    return jnp.where((places >= first) & (places <= last), scores, -1e30)


def attention_kernel(
    mine, other, gain, att, bias, cosine, sine, first, last, places,
    query, key, value, attended, log_total, branch_mine, branch_other, weight,
):
    shard = weight.shape[0] // 8
    for i in range(8):
        weight[i * shard : (i + 1) * shard, :] = att[i, :shard, :]
    for i in range(4):
        at = slice(i * ROWS, (i + 1) * ROWS)
        half = slice(i % 2 * ROWS, (i % 2 + 1) * ROWS)
        rows = (mine if i < 2 else other)[half, :]
        normed = (rows.astype(f32) * gain[...]).astype(bf16)
        qkv = contract(normed, weight[:, : 3 * HEAD], 1, 0) + bias[...]
        query[at, :] = rope_in(qkv[:, :HEAD], cosine[at, :], sine[at, :]).astype(bf16)
        key[at, :] = rope_in(qkv[:, HEAD : 2 * HEAD], cosine[at, :], sine[at, :]).astype(bf16)
        value[at, :] = qkv[:, 2 * HEAD :].astype(bf16)
    for i in range(4):
        at = slice(i * ROWS, (i + 1) * ROWS)
        half = slice(i % 2 * ROWS, (i % 2 + 1) * ROWS)
        scores = masked_scores(query[at, :], key[...], first[at, :], last[at, :], places[...])
        top = jnp.max(scores, axis=1, keepdims=True)
        raised = jnp.exp(scores - top)
        total = jnp.sum(raised, axis=1, keepdims=True)
        log_total[at, :] = top + jnp.log(total)
        probs = (raised / total).astype(bf16)
        rows = contract(probs, value[...], 1, 0).astype(bf16)
        attended[at, :] = rows
        branch = contract(rows, weight[:, 3 * HEAD :], 1, 1).astype(bf16)
        (branch_mine if i < 2 else branch_other)[half, :] = branch


def attention_grad_kernel(
    branch_mine, branch_other, mine, other, gain, att, query, key, value, attended, log_total,
    cosine, sine, first, last, places,
    normed_mine, normed_other, grads, weight, normed, grad_qkv, grad_key, grad_value,
):
    shard = weight.shape[0] // 8
    for i in range(8):
        weight[i * shard : (i + 1) * shard, :] = att[i, :shard, :]
    for i in range(4):
        at = slice(i * ROWS, (i + 1) * ROWS)
        half = slice(i % 2 * ROWS, (i % 2 + 1) * ROWS)
        rows = (mine if i < 2 else other)[half, :]
        normed[at, :] = (rows.astype(f32) * gain[...]).astype(bf16)
        branch = (branch_mine if i < 2 else branch_other)[half, :]
        grad_att = contract(branch, weight[:, 3 * HEAD :], 1, 0).astype(bf16)
        scores = masked_scores(query[at, :], key[...], first[at, :], last[at, :], places[...])
        probs = jnp.exp(scores - log_total[at, :])
        grad_probs = contract(grad_att, value[...], 1, 1)
        inner = jnp.sum(probs * grad_probs, axis=1, keepdims=True)
        grad_scores = (probs * (grad_probs - inner)).astype(bf16)
        grad_query = contract(grad_scores, key[...], 1, 0) * HEAD ** (-0.5)
        grad_qkv[at, :HEAD] = rope_out(grad_query, cosine[at, :], sine[at, :]).astype(bf16)
        key_part = contract(grad_scores, query[at, :], 0, 0)
        value_part = contract(probs.astype(bf16), grad_att, 0, 0)
        if i == 0:
            grad_key[...] = key_part
            grad_value[...] = value_part
        else:
            grad_key[...] += key_part
            grad_value[...] += value_part
    grad_key_pre = rope_out(grad_key[...] * HEAD ** (-0.5), cosine[...], sine[...])
    grad_qkv[:, HEAD : 2 * HEAD] = grad_key_pre.astype(bf16)
    grad_qkv[:, 2 * HEAD :] = grad_value[...].astype(bf16)
    for i in range(4):
        at = slice(i * ROWS, (i + 1) * ROWS)
        half = slice(i % 2 * ROWS, (i % 2 + 1) * ROWS)
        rows = contract(grad_qkv[at, :], weight[:, : 3 * HEAD], 1, 1).astype(bf16)
        (normed_mine if i < 2 else normed_other)[half, :] = rows
    sums = jnp.sum(grad_qkv[...].astype(f32), axis=0, keepdims=True)
    sums = jnp.concatenate([sums, jnp.zeros((1, HEAD), f32)], axis=1)
    pad = jnp.where(lax.broadcasted_iota(jnp.int32, (16, 4 * HEAD), 0) == 0, sums, 0.0).astype(bf16)
    top = attended[: 2 * ROWS, :]
    low = attended[2 * ROWS :, :]
    for i in range(4):
        cols = slice(2 * i * shard, 2 * (i + 1) * shard)
        qkv_part = contract(normed[:, cols], grad_qkv[...], 0, 0)
        out_part = contract(branch_mine[:, cols], top, 0, 0)
        out_part += contract(branch_other[:, cols], low, 0, 0)
        both = jnp.concatenate([qkv_part, out_part], axis=1).astype(bf16)
        for j in range(2):
            place = (2 * i + j) % 4 * 2 + (2 * i + j) // 4
            base = place * (shard + 16)
            grads[base : base + shard, :] = both[j * shard : (j + 1) * shard, :]
            grads[base + shard : base + shard + 16, :] = pad


def ffn_kernel(hi, rows, grad, weight_own, weight_far, hidden, grad_gu, grad_rows):
    width = weight_own.shape[0]
    units = weight_own.shape[1] // 3
    at_own = pl.ds(pl.multiple_of(hi[0] * width, HEAD), width)
    at_far = pl.ds(pl.multiple_of((1 - hi[0]) * width, HEAD), width)

    def product(left, cols):
        return contract(left[:, at_own], weight_own[:, cols], 1, 0) + contract(
            left[:, at_far], weight_far[:, cols], 1, 0
        )

    gate = product(rows, slice(0, units))
    upward = product(rows, slice(units, 2 * units))
    sigmoid = jax.nn.sigmoid(gate)
    activated = gate * sigmoid
    hidden[...] = (activated * upward).astype(bf16)
    grad_hidden = product(grad, slice(2 * units, 3 * units))
    grad_gu[:, :units] = (
        grad_hidden * upward * sigmoid * (1.0 + gate * (1.0 - sigmoid))
    ).astype(bf16)
    grad_gu[:, units:] = (grad_hidden * activated).astype(bf16)
    for at, weight in ((at_own, weight_own), (at_far, weight_far)):
        grad_rows[:, at] = contract(grad_gu[...], weight[:, : 2 * units], 1, 1).astype(bf16)


def down_grad_kernel(parts, out):
    start = 0
    for i in range(8):
        cols = (4 if i < 5 else 5) * BLOCK
        out[:, start : start + cols] = parts[i, :, :cols].astype(f32)
        start += cols


def gate_up_grad_kernel(parts, out):
    units = parts.shape[2] // 2
    start = 0
    for i in range(8):
        for j in range(4 if i < 5 else 5):
            for k in range(2):
                cols = slice(k * units + j * BLOCK, k * units + (j + 1) * BLOCK)
                out[:, k, start : start + BLOCK] = parts[i, :, cols].astype(f32)
            start += BLOCK


def attention_weight_grad_kernel(parts, grad_qkv, grad_out, sums):
    shard = grad_qkv.shape[0]
    qcols = GROUP_Q * HEAD
    pairs = 0.0
    tails = 0.0
    for i in range(GROUP_Q):
        cols = slice(i * HEAD, (i + 1) * HEAD)
        grad_qkv[:, cols] = parts[i, :shard, :HEAD].astype(f32)
        grad_out[:, cols] = parts[i, :shard, 3 * HEAD :].astype(f32)
        tail = parts[i, shard:, :].astype(f32)
        sums[:, cols] = tail[:, :HEAD]
        pairs += parts[i, :shard, HEAD : 3 * HEAD].astype(f32)
        tails += tail[:, HEAD : 3 * HEAD]
    grad_qkv[:, qcols:] = pairs
    sums[:, qcols:] = tails


def local_call(kernel, outs, scratch=()):
    return pl.pallas_call(
        kernel,
        out_shape=[jax.ShapeDtypeStruct(shape, dtype) for shape, dtype in outs],
        scratch_shapes=[pltpu.VMEM(shape, dtype) for shape, dtype in scratch],
        compiler_params=pltpu.CompilerParams(vmem_limit_bytes=VMEM_BYTES),
        cost_estimate=COST,
    )


def assemble(kernel, parts, outs):
    return local_call(kernel, outs)(parts)


def attention(mine, other, gain, att, bias, cosine, sine, first, last, places):
    half, width = mine.shape
    outs = [((2 * half, HEAD), bf16)] * 4 + [((2 * half, 1), f32)] + [((half, width), bf16)] * 2
    return local_call(attention_kernel, outs, [((width, 4 * HEAD), bf16)])(
        mine, other, gain, att, bias, cosine, sine, first, last, places
    )


def attention_grad(branch_mine, branch_other, mine, other, gain, att, *rest):
    half, width = mine.shape
    outs = [((half, width), bf16)] * 2 + [((width + 8 * 16, 4 * HEAD), bf16)]
    scratch = [
        ((width, 4 * HEAD), bf16),
        ((2 * half, width), bf16),
        ((2 * half, 3 * HEAD), bf16),
        ((2 * half, HEAD), f32),
        ((2 * half, HEAD), f32),
    ]
    return local_call(attention_grad_kernel, outs, scratch)(
        branch_mine, branch_other, mine, other, gain, att, *rest
    )


def feed_forward(hi, rows, grad, weight_own, weight_far):
    count, width = rows.shape
    units = weight_own.shape[1] // 3

    def by_rows(cols):
        return pl.BlockSpec((ROWS, cols), lambda i, hi: (i, 0))

    whole = pl.BlockSpec(weight_own.shape, lambda i, hi: (0, 0))
    return pl.pallas_call(
        ffn_kernel,
        grid_spec=pltpu.PrefetchScalarGridSpec(
            num_scalar_prefetch=1,
            grid=(count // ROWS,),
            in_specs=[by_rows(width), by_rows(width), whole, whole],
            out_specs=[by_rows(units), by_rows(2 * units), by_rows(width)],
        ),
        out_shape=[
            jax.ShapeDtypeStruct((count, cols), bf16) for cols in (units, 2 * units, width)
        ],
        compiler_params=pltpu.CompilerParams(vmem_limit_bytes=VMEM_BYTES),
        cost_estimate=COST,
    )(hi, rows, grad, weight_own, weight_far)


def sequence_of(places, seq_lengths):
    ends = jnp.cumsum(seq_lengths)
    starts = ends - seq_lengths
    inside = (places[:, None] >= starts[None, :]) & (places[:, None] < ends[None, :])
    return jnp.sum(inside.astype(jnp.int32) * starts[None, :], axis=1)


def rotary(offset):
    half = HEAD // 2
    freqs = THETA ** (-(2.0 * jnp.arange(half, dtype=f32)) / HEAD)
    angle = offset.astype(f32)[:, None] * freqs[None, :]
    cosine, sine = jnp.cos(angle), jnp.sin(angle)
    return jnp.concatenate([cosine, cosine], axis=1), jnp.concatenate([-sine, sine], axis=1)


def rms_scale(values):
    return lax.rsqrt(jnp.mean(values * values, axis=-1, keepdims=True) + EPS)


def norm_back(values, scale, gain, incoming):
    weighted = incoming * gain
    return scale * weighted - values * scale**3 * jnp.mean(
        weighted * values, axis=-1, keepdims=True
    )


def on_device(
    tokens,
    cotangent,
    norm_attn,
    qkv_weight,
    qkv_bias,
    out_weight,
    norm_mlp,
    gate_up_weight,
    down_weight,
    lengths,
    deal,
):
    f = lax.axis_index("fsdp")
    c = lax.axis_index("ctx")
    t = lax.axis_index("tp")
    count, width = tokens.shape
    own = count // 2
    shard = qkv_weight.shape[0]
    qcols = GROUP_Q * HEAD
    has_head = c < GROUP_Q
    head = jnp.minimum(c, GROUP_Q - 1)

    tok = lax.dynamic_slice_in_dim(tokens, t * own, own)
    cot = lax.dynamic_slice_in_dim(cotangent, t * own, own)
    scale_a = rms_scale(tok)
    unit_own = (tok * scale_a).astype(bf16)
    grad_own = cot.astype(bf16)

    w_out_own = lax.dynamic_slice_in_dim(out_weight, head * HEAD, HEAD).T
    w_out_own = jnp.where(has_head, w_out_own, jnp.zeros_like(w_out_own))
    att_own = jnp.concatenate(
        [
            lax.dynamic_slice_in_dim(qkv_weight, head * HEAD, HEAD, axis=1),
            qkv_weight[:, qcols:],
            w_out_own,
        ],
        axis=1,
    )
    row = jnp.concatenate([norm_attn, norm_mlp, qkv_bias[0]])[None]
    att_own = jnp.concatenate([att_own, row, jnp.zeros((15, row.shape[1]), bf16)], axis=0)
    att_far = lax.ppermute(att_own, "fsdp", XH_SWAP)

    start = jnp.maximum(4 * c, 5 * c - 5) * BLOCK
    units = 5 * BLOCK
    gu_own = lax.dynamic_slice_in_dim(gate_up_weight, start, units, axis=2)
    inside = (jnp.arange(units) < 4 * BLOCK) | (c >= 5)
    gu_own = jnp.where(inside, gu_own, jnp.zeros_like(gu_own))
    down_own = lax.dynamic_slice_in_dim(down_weight, start, units).T
    ffn_own = jnp.concatenate([gu_own[:, 0], gu_own[:, 1], down_own], axis=1)
    ffn_line = gather_along_y(ffn_own)
    ffn_far = lax.ppermute(ffn_own, "fsdp", XH_SWAP)

    att_all = gather_small(att_own, att_far)
    extra = att_all[:, shard].astype(f32)
    gain_a = extra[:, :shard].reshape(1, width)
    gain_m = extra[:, shard : 2 * shard].reshape(1, width)
    bias_all = extra[:, 2 * shard :].reshape(1, -1)
    bias = jnp.concatenate(
        [lax.dynamic_slice_in_dim(bias_all, head * HEAD, HEAD, axis=1), bias_all[:, qcols:]], axis=1
    )

    deal_all = deal[0].reshape(8, 2, own)[:, t ^ jnp.arange(2)]
    places = jnp.transpose(deal_all, (1, 0, 2)).reshape(-1)
    first = sequence_of(places, lengths[0])
    cosine, sine = rotary(places - first)
    order = (cosine, sine, first[:, None], places[:, None], places[None, :])

    unit_mine, grad_own = tie(gather(unit_own, "ctx"), grad_own)
    grad_mine = gather(grad_own, "ctx")
    units_all = both_cores(unit_mine)
    held = attention(*units_all, gain_a, att_all, bias, *order)
    *held, grad_mine, ffn_far = tie(*held, grad_mine, ffn_far)
    query, key, value, attended, log_total, branch_mine, branch_other = held
    ffn_far = gather_along_y(ffn_far)
    grads = both_cores(grad_mine)
    branch_parts = pair_sums(branch_mine, branch_other)
    branch = reduce(branch_parts, "ctx")
    middle = tok + branch
    scale_m = rms_scale(middle)
    normed2_mine = gather((middle * scale_m * gain_m).astype(bf16), "ctx")
    normed2 = both_cores(normed2_mine)

    hi = (f // 4)[None]
    hidden, grad_gu, parts = zip(
        *[feed_forward(hi, r, g, ffn_line, ffn_far) for r, g in zip(normed2, grads)]
    )
    parts = pair_sums(*parts)
    parts, *held = tie(parts, *normed2, *grad_gu, *hidden, *grads)
    normed2, grad_gu, hidden, grads = held[0:2], held[2:4], held[4:6], held[6:8]
    grad_normed2 = reduce(parts, "ctx")

    down_sums = reduce_along_y(by_y(over_rows(grads, hidden)))
    grad_normed2, gu_blocks = tie(grad_normed2, by_y(over_rows(normed2, grad_gu)))
    gu_sums = reduce_along_y(gu_blocks)

    def output_rows(rows):
        own_side = contract(rows, ffn_line[:, 2 * units :], 1, 1).astype(bf16)
        far_side = contract(rows, ffn_far[:, 2 * units :], 1, 1).astype(bf16)
        return jnp.concatenate(
            [jnp.where(f < 4, own_side, far_side), jnp.where(f < 4, far_side, own_side)], axis=1
        )

    grad_middle = cot + norm_back(middle, scale_m, gain_m, grad_normed2)
    branch_mine = gather(grad_middle.astype(bf16), "ctx")
    branch_mine, down_share = tie(branch_mine, reduce_over_hi(down_sums))
    grad_branch = both_cores(branch_mine)
    down_part = gather(down_share, "ctx")
    normed_mine, normed_other, att_grads = attention_grad(
        *grad_branch, *units_all, gain_a, att_all, query, key, value, attended, log_total, *order
    )
    att_grads, down_part = tie(att_grads, down_part)
    att_sums = reduce_along_y(att_grads)
    normed_parts = pair_sums(normed_mine, normed_other)
    grad_normed, gu_share, *hidden = tie(
        reduce(normed_parts, "ctx"), reduce_over_hi(gu_sums), *hidden
    )
    gu_part = gather(gu_share, "ctx")
    grad_tokens = both_halves(grad_middle + norm_back(tok, scale_a, gain_a, grad_normed))
    output_parts = pair_sums(*[output_rows(h) for h in hidden])
    grad_down_weight = assemble(
        down_grad_kernel, down_part, [((shard, down_weight.shape[0]), f32)]
    )[0]
    att_share, gu_part, output_parts, grad_down_weight, grad_tokens = tie(
        reduce_over_hi(att_sums), gu_part, output_parts, grad_down_weight, grad_tokens
    )
    att_part = gather(att_share, "ctx")
    output_pair = reduce_along_z(output_parts.reshape(-1, width))
    output = both_halves(middle + reduce_over_lo(output_pair))
    grad_gu_weight = pl.pallas_call(
        gate_up_grad_kernel,
        grid=(shard // GRAD_ROWS,),
        in_specs=[pl.BlockSpec((8, GRAD_ROWS, 2 * units), lambda i: (0, i, 0))],
        out_specs=pl.BlockSpec((GRAD_ROWS,) + gate_up_weight.shape[1:], lambda i: (i, 0, 0)),
        out_shape=jax.ShapeDtypeStruct(gate_up_weight.shape, f32),
        compiler_params=pltpu.CompilerParams(vmem_limit_bytes=VMEM_BYTES),
        cost_estimate=COST,
    )(gu_part)
    grad_qkv_weight, grad_out_weight, sums = assemble(
        attention_weight_grad_kernel,
        att_part,
        [(qkv_weight.shape, f32), ((shard, qcols), f32), ((16, qkv_weight.shape[1]), f32)],
    )
    split_at = qcols + HEAD
    own_bias = lax.dynamic_slice(sums, (0, f * (split_at // 8)), (1, split_at // 8))
    own_value = lax.dynamic_slice(sums, (0, split_at + f * (HEAD // 8)), (1, HEAD // 8))
    gain_sums = jnp.stack(
        [
            jnp.sum(grad_qkv_weight * qkv_weight.astype(f32), axis=1) / norm_attn.astype(f32),
            jnp.sum(grad_gu_weight * gate_up_weight.astype(f32), axis=(1, 2))
            / norm_mlp.astype(f32),
        ]
    )
    gain_sums = gain_sums + lax.ppermute(gain_sums, "tp", TP_SWAP)

    return (
        output,
        grad_tokens,
        gain_sums[0],
        grad_qkv_weight,
        own_bias,
        own_value,
        grad_out_weight.T,
        gain_sums[1],
        grad_gu_weight,
        grad_down_weight.T,
    )


def solution(mesh):
    in_specs = (
        P(("fsdp", "ctx"), None),
        P(("fsdp", "ctx"), None),
        P("fsdp"),
        P("fsdp", "tp"),
        P("tp", "fsdp"),
        P("tp", "fsdp"),
        P("fsdp"),
        P("fsdp", None, "tp"),
        P("tp", "fsdp"),
        P("fsdp", None),
        P("fsdp", None),
    )
    out_specs = (
        P(("fsdp", "ctx"), None),
        P(("fsdp", "ctx"), None),
        P("fsdp"),
        P("fsdp", "tp"),
        P("tp", "fsdp"),
        P("tp", "fsdp"),
        P("tp", "fsdp"),
        P("fsdp"),
        P("fsdp", None, "tp"),
        P("tp", "fsdp"),
    )
    return jax.shard_map(
        on_device, mesh=mesh, in_specs=in_specs, out_specs=out_specs, check_vma=False
    )
```

time: 545 us -> 445 us (0.82)
  the two profiles are of different devices: /device:TPU:13 before, /device:TPU:1 now
where the time goes in v2:
time: 445 us; the launch traced here: 437 us
  waiting for transfers between devices  181 us (41%)
  starting transfers between devices  84 us (19%)
  Pallas kernels  59.3 us (13%)
  other arithmetic  43.2 us (10%)
  local copies, waits for them, and re-layouts  36.7 us (8%)
  matrix products  17.8 us (4%)
  between operations  15.4 us (3%)
    all_to_all x7, waiting for transfers between devices, gather(): return lax.all_to_all(copies, axis, 0, 0, tiled=True)  87.4 us
    ppermute x3, waiting for transfers between devices, reduce_over_hi(): lax.ppermute(sent, 'fsdp', XH_SWAP).astype(f32)  33.4 us
    all_to_all x7, starting transfers between devices, gather(): return lax.all_to_all(copies, axis, 0, 0, tiled=True)  31.7 us
    all_to_all x3, waiting for transfers between devices, reduce(): lax.all_to_all(part, axis, 0, 0, tiled=True).astype(f32)  31.7 us
    pallas_call x2, Pallas kernels, feed_forward(): pl.pallas_call(ffn_kernel, grid_spec=pltpu.PrefetchScalarGridSpec(num_sca...  20.8 us
    dot_general x8, matrix products, contract(): lax.dot_general(left, right, (((left_dim,), (right_dim,)), ((), ())), pre...  17.8 us
    pallas_call x1, Pallas kernels, attention_grad(): local_call(attention_grad_kernel, outs, scratch)  15.1 us
    all_to_all x3, starting transfers between devices, reduce(): lax.all_to_all(part, axis, 0, 0, tiled=True).astype(f32)  10.9 us
  transfers between devices with their start and end apart: 39, of which 17 were waited for; matrix products, arithmetic and copies ran while one was open for 18% of the time, Pallas kernels for 11%

profile of v2, /device:TPU:1, one launch (start us, length us, event | category | flops | bytes accessed | tf_op | source)
XLA Modules:
  0.0 437.1 jit_solution(8673356001708133655)
XLA Ops:
  11.6 3.7 collective-permute-start.3
  23.9 6.0 %all-to-all-start = ((bf16[8,64,1536]{2,1,0:T(8,128)(2,1)}), bf16[8,64,1536]{2,1,0:T(8,128)(2,1)}, u32[]{:S(2)}, u32[]{:S(2)}) async-start(bf16[8,64,1536]{2,1,0:T(8,128)(2,1)} %broadcast_in_dim.100), calls=%async_computation | async-start | bytes 3145728 | tf_op jit(solution)/shard_map/all_to_all | solution.py:49
  45.7 14.9 %all-to-all-done = bf16[8,64,1536]{2,1,0:T(8,128)(2,1)} async-done(((bf16[8,64,1536]{2,1,0:T(8,128)(2,1)}), bf16[8,64,1536]{2,1,0:T(8,128)(2,1)}, u32[]{:S(2)}, u32[]{:S(2)}) %all-to-all-start) | async-done | bytes 1572896 | tf_op jit(solution)/shard_map/all_to_all | solution.py:49
  64.7 4.0 all-to-all-start.1
  73.3 9.9 %shard_map.186 = (bf16[1024,128]{1,0:T(8,128)(2,1)}, bf16[1024,128]{1,0:T(8,128)(2,1)}, bf16[1024,128]{1,0:T(8,128)(2,1)}, bf16[1024,128]{1,0:T(8,128)(2,1)}, f3...) custom-call(bf16[512,1536]{1,0:T(8,128)(2,1)} %bitcast.mine, ...), custom_call_target="tpu_custom_call" | custom-call | flops 1000000 | bytes 100000 | tf_op jit(solution)/shard_map/pallas_call | solution.py:314
  83.2 7.0 %all-to-all-done.1 = bf16[8,64,1536]{2,1,0:T(8,128)(2,1)S(1)} async-done(((bf16[8,64,1536]{2,1,0:T(8,128)(2,1)}), bf16[8,64,1536]{2,1,0:T(8,128)(2,1)S(1)}, u32[]{:S(2)}, u32[]{:S(2)}) %all-to-all-start.1) | async-done | bytes 1572896 | tf_op jit(solution)/shard_map/all_to_all | solution.py:49
  97.2 3.6 all-to-all-start.2
  101.6 20.2 %all-to-all-done.2 = bf16[8,64,1536]{2,1,0:T(8,128)(2,1)S(1)} async-done(((bf16[8,64,1536]{2,1,0:T(8,128)(2,1)}), bf16[8,64,1536]{2,1,0:T(8,128)(2,1)S(1)}, u32[]{:S(2)}, u32[]{:S(2)}) %all-to-all-start.2) | async-done | bytes 1572896 | tf_op jit(solution)/shard_map/all_to_all | solution.py:53
  124.5 4.3 all-to-all-start.3
  130.2 18.9 %all-to-all-done.3 = bf16[8,64,1536]{2,1,0:T(8,128)(2,1)} async-done(((bf16[8,64,1536]{2,1,0:T(8,128)(2,1)}), bf16[8,64,1536]{2,1,0:T(8,128)(2,1)}, u32[]{:S(2)}, u32[]{:S(2)}) %all-to-all-start.3) | async-done | bytes 1572896 | tf_op jit(solution)/shard_map/all_to_all | solution.py:49
  151.2 3.4 collective-permute-done.10.rows
  154.5 10.4 %shard_map.188 = (bf16[512,640]{1,0:T(8,128)(2,1)}, bf16[512,1280]{1,0:T(8,128)(2,1)}, bf16[512,1536]{1,0:T(8,128)(2,1)}) custom-call(s32[1]{0:T(128)} %bitcast.22.hi, bf16[512,1536]{1,0:T(8,128)(2,1)} %collective-permute-done.10.rows, bf16[512,1536]{1,0:T(8,128)(2,1)} %collective-permute-done.11.grad, ...), custom_call_target="tpu_custom_call" | custom-call | flops 1000000 | bytes 100000 | tf_op jit(solution)/shard_map/pallas_call | solution.py:342
  165.4 10.4 %shard_map.187 = (bf16[512,640]{1,0:T(8,128)(2,1)}, bf16[512,1280]{1,0:T(8,128)(2,1)}, bf16[512,1536]{1,0:T(8,128)(2,1)}) custom-call(s32[1]{0:T(128)} %bitcast.22.hi, bf16[512,1536]{1,0:T(8,128)(2,1)} %bitcast.23.rows, bf16[512,1536]{1,0:T(8,128)(2,1)} %bitcast.78, bf16[768,1920]{1,0:T(8,128)(2,1)} %all-gather.3.cloned.1.call-done.weight_own, ...), custom_call_target="tpu_custom_call" | custom-call | flops 1000000 | bytes 100000 | tf_op jit(solution)/shard_map/pallas_call | solution.py:342
  184.8 3.7 all-to-all-start.4
  188.6 3.8 fusion.13
  192.4 3.8 fusion
  198.4 11.4 %all-to-all-done.4 = bf16[8,64,1536]{2,1,0:T(8,128)(2,1)S(1)} async-done(((bf16[8,64,1536]{2,1,0:T(8,128)(2,1)}), bf16[8,64,1536]{2,1,0:T(8,128)(2,1)S(1)}, u32[]{:S(2)}, u32[]{:S(2)}) %all-to-all-start.4) | async-done | bytes 1572896 | tf_op jit(solution)/shard_map/all_to_all | solution.py:53
  213.4 3.6 all-to-all-start.5
  220.0 21.2 %collective-permute-done.13 = bf16[192,640]{1,0:T(8,128)(2,1)S(1)} collective-permute-done((bf16[192,640]{1,0:T(8,128)(2,1)S(1)}, bf16[192,640]{1,0:T(8,128)(2,1)S(1)}, u32[]{:S(2)}, u32[]{:S(2)}) %collective-permute-start.13) | collective-permute-done | bytes 245792 | tf_op jit(solution)/shard_map/ppermute | solution.py:88
  244.1 4.7 %all-to-all-start.6 = ((bf16[8,192,640]{2,1,0:T(8,128)(2,1)}), bf16[8,192,640]{2,1,0:T(8,128)(2,1)}, u32[]{:S(2)}, u32[]{:S(2)}) async-start(bf16[8,192,640]{2,1,0:T(8,128)(2,1)} %broadcast_in_dim.119), calls=%async_computation.7 | async-start | bytes 3932160 | tf_op jit(solution)/shard_map/all_to_all | solution.py:49
  254.1 15.1 %shard_map.189 = (bf16[512,1536]{1,0:T(8,128)(2,1)}, bf16[512,1536]{1,0:T(8,128)(2,1)}, bf16[1664,512]{1,0:T(8,128)(2,1)}) custom-call(bf16[512,1536]{1,0:T(8,128)(2,1)} %bitcast.85, bf16[512,1536]{1,0:T(8,128)(2,1)} %collective-permute-done.14.branch_other, bf16[512,1536]{1,0:T(8,128)(2,1)} %bitcast.mine, bf16[512,1536]{1,0:T(8,128)(2,1)} %collective-permute-done.other, ...), custom_call_target="tpu_custom_call" | custom-call | flops 1000000 | bytes 100000 | tf_op jit(solution)/shard_map/pallas_call | solution.py:329
  280.4 3.6 all-to-all-start.7
  288.3 10.8 %reduce-scatter.7.cloned.1.call-done = bf16[416,512]{1,0:T(8,128)(2,1)} async-done(((bf16[1664,512]{1,0:T(8,128)(2,1)}), bf16[416,512]{1,0:T(8,128)(2,1)}) %reduce-scatter.7.cloned.1.call-update) | async-done | bytes 426000 | tf_op jit(solution)/shard_map/reduce_scatter | solution.py:78
  303.6 3.5 shard_map.190
  307.3 12.2 %collective-permute-done.15 = bf16[208,512]{1,0:T(8,128)(2,1)} collective-permute-done((bf16[208,512]{1,0:T(8,128)(2,1)}, bf16[208,512]{1,0:T(8,128)(2,1)}, u32[]{:S(2)}, u32[]{:S(2)}) %collective-permute-start.15) | collective-permute-done | bytes 213024 | tf_op jit(solution)/shard_map/ppermute | solution.py:88
  324.6 4.9 %all-to-all-start.8 = ((bf16[8,192,1280]{2,1,0:T(8,128)(2,1)}), bf16[8,192,1280]{2,1,0:T(8,128)(2,1)}, u32[]{:S(2)}, u32[]{:S(2)}) async-start(bf16[8,192,1280]{2,1,0:T(8,128)(2,1)} %broadcast_in_dim.120), calls=%async_computation.11 | async-start | bytes 7864320 | tf_op jit(solution)/shard_map/all_to_all | solution.py:49
  340.7 34.1 %all-to-all-done.8.parts = bf16[8,192,1280]{2,1,0:T(8,128)(2,1)} async-done(((bf16[8,192,1280]{2,1,0:T(8,128)(2,1)}), bf16[8,192,1280]{2,1,0:T(8,128)(2,1)}, u32[]{:S(2)}, u32[]{:S(2)}) %all-to-all-start.8) | async-done | bytes 3932192 | tf_op jit(solution)/shard_map/all_to_all | solution.py:49
  376.2 4.1 all-to-all-start.9
  380.4 7.4 %shard_map.192 = f32[192,2,4480]{2,1,0:T(2,128)} custom-call(bf16[8,192,1280]{2,1,0:T(8,128)(2,1)} %all-to-all-done.8.parts), custom_call_target="tpu_custom_call" | custom-call | flops 1000000 | bytes 100000 | tf_op jit(solution)/shard_map/pallas_call | solution.py:513
  387.8 8.6 %multiply_reduce_fusion = f32[192]{0:T(256)S(1)} fusion(f32[192,2,4480]{2,1,0:T(2,128)} %shard_map.192, bf16[192,2,4480]{2,1,0:T(2,128)(2,1)} %param.18), kind=kLoop, calls=%fused_computation.3 | loop fusion | flops 5160768 | bytes 10322688 | tf_op jit(solution)/shard_map/reduce_sum | solution.py:533
  396.4 9.3 %all-to-all-done.9.parts = bf16[8,208,512]{2,1,0:T(8,128)(2,1)S(1)} async-done(((bf16[8,208,512]{2,1,0:T(8,128)(2,1)}), bf16[8,208,512]{2,1,0:T(8,128)(2,1)S(1)}, u32[]{:S(2)}, u32[]{:S(2)}) %all-to-all-start.9) | async-done | bytes 1703968 | tf_op jit(solution)/shard_map/all_to_all | solution.py:49
  410.8 6.9 %collective-permute-start.22 = (f32[2,192]{1,0:T(2,128)S(1)}, f32[2,192]{1,0:T(2,128)S(1)}, u32[]{:S(2)}, u32[]{:S(2)}) collective-permute-start(f32[2,192]{1,0:T(2,128)S(1)} %pad_maximum_fusion.6), channel_id=1, source_target_pairs={{0,1},{1,0},{2,3},{3,2},{4,5},{5,4},{6,7},{7,6},{8,9},{9,8},{10,11... | collective-permute-start | bytes 4616 | tf_op jit(solution)/shard_map/ppermute | solution.py:537
  (233 shorter events, 132.1 us)
Async XLA Ops:
  7.2 144.0 %all-gather.3.cloned.1.call-start = ((), (), s32[]{:S(2)}) async-start(), calls=%async_computation.14 | async-start | bytes 3686400 | tf_op jit(solution)/shard_map/all_gather | solution.py:69
  11.6 33.2 %collective-permute-start.3 = (bf16[208,512]{1,0:T(8,128)(2,1)}, bf16[208,512]{1,0:T(8,128)(2,1)}, u32[]{:S(2)}, u32[]{:S(2)}) collective-permute-start(bf16[208,512]{1,0:T(8,128)(2,1)} %maximum_maximum_fusion), channel_id=1, source_target_pairs={{0,32},{16,48},{32,0},{48,16},{64,96},{80,112},{96,64},{112,80},{1... | collective-permute-start | bytes 638984 | tf_op jit(solution)/shard_map/ppermute | solution.py:63
  15.3 28.4 %collective-permute-start.2 = (bf16[208,512]{1,0:T(8,128)(2,1)}, bf16[208,512]{1,0:T(8,128)(2,1)}, u32[]{:S(2)}, u32[]{:S(2)}) collective-permute-start(bf16[208,512]{1,0:T(8,128)(2,1)} %maximum_maximum_fusion), channel_id=1, source_target_pairs={{0,48},{16,0},{32,16},{48,32},{64,112},{80,64},{96,80},{112,96},{1... | collective-permute-start | bytes 638984 | tf_op jit(solution)/shard_map/ppermute | solution.py:63
  16.1 24.6 %collective-permute-start.1 = (bf16[208,512]{1,0:T(8,128)(2,1)}, bf16[208,512]{1,0:T(8,128)(2,1)}, u32[]{:S(2)}, u32[]{:S(2)}) collective-permute-start(bf16[208,512]{1,0:T(8,128)(2,1)} %maximum_maximum_fusion), channel_id=1, source_target_pairs={{0,16},{16,32},{32,48},{48,0},{64,80},{80,96},{96,112},{112,64},{1... | collective-permute-start | bytes 638984 | tf_op jit(solution)/shard_map/ppermute | solution.py:63
  16.8 23.1 %collective-permute-start.4 = (bf16[208,512]{1,0:T(8,128)(2,1)}, bf16[208,512]{1,0:T(8,128)(2,1)}, u32[]{:S(2)}, u32[]{:S(2)}) collective-permute-start(bf16[208,512]{1,0:T(8,128)(2,1)} %maximum_maximum_fusion), channel_id=1, source_target_pairs={{0,64},{16,80},{32,96},{48,112},{64,0},{80,16},{96,32},{112,48},{1... | collective-permute-start | bytes 638984 | tf_op jit(solution)/shard_map/ppermute | solution.py:425
  22.0 61.1 %collective-permute-start.8 = (bf16[192,1920]{1,0:T(8,128)(2,1)}, bf16[192,1920]{1,0:T(8,128)(2,1)}, u32[]{:S(2)}, u32[]{:S(2)}) collective-permute-start(bf16[192,1920]{1,0:T(8,128)(2,1)} %pad_maximum_fusion.3), channel_id=1, source_target_pairs={{0,64},{16,80},{32,96},{48,112},{64,0},{80,16},{96,32},{112,48},{1... | collective-permute-start | bytes 2211848 | tf_op jit(solution)/shard_map/ppermute | solution.py:435
  23.9 36.6 %all-to-all-start = ((bf16[8,64,1536]{2,1,0:T(8,128)(2,1)}), bf16[8,64,1536]{2,1,0:T(8,128)(2,1)}, u32[]{:S(2)}, u32[]{:S(2)}) async-start(bf16[8,64,1536]{2,1,0:T(8,128)(2,1)} %broadcast_in_dim.100), calls=%async_computation | async-start | bytes 3145728 | tf_op jit(solution)/shard_map/all_to_all | solution.py:49
  39.9 30.9 %collective-permute-start.7 = (bf16[208,512]{1,0:T(8,128)(2,1)}, bf16[208,512]{1,0:T(8,128)(2,1)}, u32[]{:S(2)}, u32[]{:S(2)}) collective-permute-start(bf16[208,512]{1,0:T(8,128)(2,1)} %collective-permute-done.4), channel_id=1, source_target_pairs={{0,32},{16,48},{32,0},{48,16},{64,96},{80,112},{96,64},{112,80},{1... | collective-permute-start | bytes 638984 | tf_op jit(solution)/shard_map/ppermute | solution.py:63
  40.7 29.1 %collective-permute-start.6 = (bf16[208,512]{1,0:T(8,128)(2,1)}, bf16[208,512]{1,0:T(8,128)(2,1)}, u32[]{:S(2)}, u32[]{:S(2)}) collective-permute-start(bf16[208,512]{1,0:T(8,128)(2,1)} %collective-permute-done.4), channel_id=1, source_target_pairs={{0,48},{16,0},{32,16},{48,32},{64,112},{80,64},{96,80},{112,96},{1... | collective-permute-start | bytes 638984 | tf_op jit(solution)/shard_map/ppermute | solution.py:63
  43.7 25.1 %collective-permute-start.5 = (bf16[208,512]{1,0:T(8,128)(2,1)}, bf16[208,512]{1,0:T(8,128)(2,1)}, u32[]{:S(2)}, u32[]{:S(2)}) collective-permute-start(bf16[208,512]{1,0:T(8,128)(2,1)} %collective-permute-done.4), channel_id=1, source_target_pairs={{0,16},{16,32},{32,48},{48,0},{64,80},{80,96},{96,112},{112,64},{1... | collective-permute-start | bytes 638984 | tf_op jit(solution)/shard_map/ppermute | solution.py:63
  60.6 12.7 %collective-permute-start = (bf16[512,1536]{1,0:T(8,128)(2,1)}, bf16[512,1536]{1,0:T(8,128)(2,1)}, u32[]{:S(2)}, u32[]{:S(2)}) collective-permute-start(bf16[512,1536]{1,0:T(8,128)(2,1)} %bitcast.mine), channel_id=1, source_target_pairs={{0,1},{1,0},{2,3},{3,2},{4,5},{5,4},{6,7},{7,6},{8,9},{9,8},{10,11... | collective-permute-start | bytes 4718600 | tf_op jit(solution)/shard_map/ppermute | solution.py:115
  64.7 25.5 %all-to-all-start.1 = ((bf16[8,64,1536]{2,1,0:T(8,128)(2,1)}), bf16[8,64,1536]{2,1,0:T(8,128)(2,1)S(1)}, u32[]{:S(2)}, u32[]{:S(2)}) async-start(bf16[8,64,1536]{2,1,0:T(8,128)(2,1)} %broadcast_in_dim.113), calls=%async_computation.1 | async-start | bytes 3145728 | tf_op jit(solution)/shard_map/all_to_all | solution.py:49
  97.2 24.6 %all-to-all-start.2 = ((bf16[8,64,1536]{2,1,0:T(8,128)(2,1)}), bf16[8,64,1536]{2,1,0:T(8,128)(2,1)S(1)}, u32[]{:S(2)}, u32[]{:S(2)}) async-start(bf16[8,64,1536]{2,1,0:T(8,128)(2,1)} %bitcast.83), calls=%async_computation.2 | async-start | bytes 3145728 | tf_op jit(solution)/shard_map/all_to_all | solution.py:53
  100.8 50.4 %all-gather.5.cloned.1.call-start = ((), (), s32[]{:S(2)}) async-start(), calls=%async_computation.15 | async-start | bytes 3686400 | tf_op jit(solution)/shard_map/all_gather | solution.py:69
  124.5 24.5 %all-to-all-start.3 = ((bf16[8,64,1536]{2,1,0:T(8,128)(2,1)}), bf16[8,64,1536]{2,1,0:T(8,128)(2,1)}, u32[]{:S(2)}, u32[]{:S(2)}) async-start(bf16[8,64,1536]{2,1,0:T(8,128)(2,1)} %broadcast_in_dim.117), calls=%async_computation.3 | async-start | bytes 3145728 | tf_op jit(solution)/shard_map/all_to_all | solution.py:49
  128.8 88.2 %reduce-scatter.5.cloned.1.call-start = ((), (), s32[]{:S(2)}) async-start(), calls=%async_computation.16 | async-start | bytes 2457600 | tf_op jit(solution)/shard_map/reduce_scatter | solution.py:78
  128.9 22.3 %collective-permute-start.11 = (bf16[512,1536]{1,0:T(8,128)(2,1)S(1)}, bf16[512,1536]{1,0:T(8,128)(2,1)}, u32[]{:S(2)}, u32[]{:S(2)}) collective-permute-start(bf16[512,1536]{1,0:T(8,128)(2,1)S(1)} %bitcast.77), channel_id=1, source_target_pairs={{0,1},{1,0},{2,3},{3,2},{4,5},{5,4},{6,7},{7,6},{8,9},{9,8},{10,11... | collective-permute-start | bytes 4718600 | tf_op jit(solution)/shard_map/ppermute | solution.py:115
  164.9 10.9 %collective-permute-start.12 = (bf16[512,1536]{1,0:T(8,128)(2,1)}, bf16[512,1536]{1,0:T(8,128)(2,1)S(1)}, u32[]{:S(2)}, u32[]{:S(2)}) collective-permute-start(bf16[512,1536]{1,0:T(8,128)(2,1)} %get-tuple-element.78), channel_id=1, source_target_pairs={{0,1},{1,0},{2,3},{3,2},{4,5},{5,4},{6,7},{7,6},{8,9},{9,8},{10,11... | collective-permute-start | bytes 4718600 | tf_op jit(solution)/shard_map/ppermute | solution.py:119
  184.8 25.0 %all-to-all-start.4 = ((bf16[8,64,1536]{2,1,0:T(8,128)(2,1)}), bf16[8,64,1536]{2,1,0:T(8,128)(2,1)S(1)}, u32[]{:S(2)}, u32[]{:S(2)}) async-start(bf16[8,64,1536]{2,1,0:T(8,128)(2,1)} %bitcast.25), calls=%async_computation.4 | async-start | bytes 3145728 | tf_op jit(solution)/shard_map/all_to_all | solution.py:53
  188.5 95.4 %reduce-scatter.9.cloned.1.call-start = ((), (), s32[]{:S(2)}) async-start(), calls=%async_computation.18 | async-start | bytes 4915200 | tf_op jit(solution)/shard_map/reduce_scatter | solution.py:78
  213.4 29.1 %all-to-all-start.5 = ((bf16[8,64,1536]{2,1,0:T(8,128)(2,1)}), bf16[8,64,1536]{2,1,0:T(8,128)(2,1)S(1)}, u32[]{:S(2)}, u32[]{:S(2)}) async-start(bf16[8,64,1536]{2,1,0:T(8,128)(2,1)} %broadcast_in_dim.118), calls=%async_computation.5 | async-start | bytes 3145728 | tf_op jit(solution)/shard_map/all_to_all | solution.py:49
  218.1 23.1 %collective-permute-start.13 = (bf16[192,640]{1,0:T(8,128)(2,1)S(1)}, bf16[192,640]{1,0:T(8,128)(2,1)S(1)}, u32[]{:S(2)}, u32[]{:S(2)}) collective-permute-start(bf16[192,640]{1,0:T(8,128)(2,1)S(1)} %broadcast_select_fusion.5), channel_id=1, source_target_pairs={{0,64},{16,80},{32,96},{48,112},{64,0},{80,16},{96,32},{112,48},{1... | collective-permute-start | bytes 737288 | tf_op jit(solution)/shard_map/ppermute | solution.py:88
  244.1 28.3 %all-to-all-start.6 = ((bf16[8,192,640]{2,1,0:T(8,128)(2,1)}), bf16[8,192,640]{2,1,0:T(8,128)(2,1)}, u32[]{:S(2)}, u32[]{:S(2)}) async-start(bf16[8,192,640]{2,1,0:T(8,128)(2,1)} %broadcast_in_dim.119), calls=%async_computation.7 | async-start | bytes 3932160 | tf_op jit(solution)/shard_map/all_to_all | solution.py:49
  248.8 50.3 %reduce-scatter.7.cloned.1.call-start = ((), (), s32[]{:S(2)}) async-start(), calls=%async_computation.17 | async-start | bytes 2129920 | tf_op jit(solution)/shard_map/reduce_scatter | solution.py:78
  280.4 26.7 %all-to-all-start.7 = ((bf16[8,64,1536]{2,1,0:T(8,128)(2,1)}), bf16[8,64,1536]{2,1,0:T(8,128)(2,1)S(1)}, u32[]{:S(2)}, u32[]{:S(2)}) async-start(bf16[8,64,1536]{2,1,0:T(8,128)(2,1)} %bitcast.82), calls=%async_computation.9 | async-start | bytes 3145728 | tf_op jit(solution)/shard_map/all_to_all | solution.py:53
  286.0 35.2 %collective-permute-start.17 = (bf16[192,1280]{1,0:T(8,128)(2,1)}, bf16[192,1280]{1,0:T(8,128)(2,1)}, u32[]{:S(2)}, u32[]{:S(2)}) collective-permute-start(bf16[192,1280]{1,0:T(8,128)(2,1)} %broadcast_select_fusion.4), channel_id=1, source_target_pairs={{0,64},{16,80},{32,96},{48,112},{64,0},{80,16},{96,32},{112,48},{1... | collective-permute-start | bytes 1474568 | tf_op jit(solution)/shard_map/ppermute | solution.py:88
  300.8 18.7 %collective-permute-start.15 = (bf16[208,512]{1,0:T(8,128)(2,1)}, bf16[208,512]{1,0:T(8,128)(2,1)}, u32[]{:S(2)}, u32[]{:S(2)}) collective-permute-start(bf16[208,512]{1,0:T(8,128)(2,1)} %broadcast_select_fusion.6), channel_id=1, source_target_pairs={{0,64},{16,80},{32,96},{48,112},{64,0},{80,16},{96,32},{112,48},{1... | collective-permute-start | bytes 638984 | tf_op jit(solution)/shard_map/ppermute | solution.py:88
  324.6 50.3 %all-to-all-start.8 = ((bf16[8,192,1280]{2,1,0:T(8,128)(2,1)}), bf16[8,192,1280]{2,1,0:T(8,128)(2,1)}, u32[]{:S(2)}, u32[]{:S(2)}) async-start(bf16[8,192,1280]{2,1,0:T(8,128)(2,1)} %broadcast_in_dim.120), calls=%async_computation.11 | async-start | bytes 7864320 | tf_op jit(solution)/shard_map/all_to_all | solution.py:49
  329.5 88.2 %reduce-scatter.11.cloned.1.call-start = ((), (), s32[]{:S(2)}) async-start(), calls=%async_computation.19 | async-start | bytes 1966080 | tf_op jit(solution)/shard_map/reduce_scatter | solution.py:96
  376.2 29.4 %all-to-all-start.9 = ((bf16[8,208,512]{2,1,0:T(8,128)(2,1)}), bf16[8,208,512]{2,1,0:T(8,128)(2,1)S(1)}, u32[]{:S(2)}, u32[]{:S(2)}) async-start(bf16[8,208,512]{2,1,0:T(8,128)(2,1)} %broadcast_in_dim.121), calls=%async_computation.13 | async-start | bytes 3407872 | tf_op jit(solution)/shard_map/all_to_all | solution.py:49
  410.8 16.7 %collective-permute-start.22 = (f32[2,192]{1,0:T(2,128)S(1)}, f32[2,192]{1,0:T(2,128)S(1)}, u32[]{:S(2)}, u32[]{:S(2)}) collective-permute-start(f32[2,192]{1,0:T(2,128)S(1)} %pad_maximum_fusion.6), channel_id=1, source_target_pairs={{0,1},{1,0},{2,3},{3,2},{4,5},{5,4},{6,7},{7,6},{8,9},{9,8},{10,11... | collective-permute-start | bytes 4616 | tf_op jit(solution)/shard_map/ppermute | solution.py:537
  418.8 6.6 %collective-permute-start.20 = (bf16[64,1536]{1,0:T(8,128)(2,1)S(1)}, bf16[64,1536]{1,0:T(8,128)(2,1)S(1)}, u32[]{:S(2)}, u32[]{:S(2)}) collective-permute-start(bf16[64,1536]{1,0:T(8,128)(2,1)S(1)} %broadcast_select_fusion.7), channel_id=1, source_target_pairs={{0,2},{2,0},{4,6},{6,4},{8,10},{10,8},{12,14},{14,12},{1,3},{3,1},... | collective-permute-start | bytes 589832 | tf_op jit(solution)/shard_map/ppermute | solution.py:106
  (39 other events, 254.5 us)
Sparse Core Ops, SparseCore 0:
  22.2 47.7 all-gather.2
  103.3 37.4 all-gather.4
  184.9 25.5 reduce-scatter.4
  213.4 44.3 reduce-scatter.8
  272.6 26.4 reduce-scatter.6
  375.0 41.3 reduce-scatter.10

commit v3 on v2

--- a/solution.py
+++ b/solution.py
@@ -49,8 +49,12 @@
     return lax.all_to_all(copies, axis, 0, 0, tiled=True)
 
 
-def reduce(part, axis):
-    return jnp.sum(lax.all_to_all(part, axis, 0, 0, tiled=True).astype(f32), axis=0)
+def spread(part, axis):
+    return lax.all_to_all(part, axis, 0, 0, tiled=True)
+
+
+def summed(parts):
+    return jnp.sum(parts.astype(f32), axis=0)
 
 
 def gather_small(own, far):
@@ -81,33 +85,18 @@
     return pair.reshape(2, -1, part.shape[1])
 
 
-def reduce_over_hi(pair):
+def swap_over_hi(pair):
     hi = lax.axis_index("fsdp") // 4
-    kept = jnp.where(hi == 0, pair[0], pair[1])
     sent = jnp.where(hi == 0, pair[1], pair[0])
-    return (kept.astype(f32) + lax.ppermute(sent, "fsdp", XH_SWAP).astype(f32)).astype(bf16)
+    return jnp.where(hi == 0, pair[0], pair[1]), lax.ppermute(sent, "fsdp", XH_SWAP)
+
+
+def added(kept, got):
+    return (kept.astype(f32) + got.astype(f32)).astype(bf16)
 
 
 def gather_along_z(own):
     return lax.all_gather(own, "ctx", axis=0, axis_index_groups=Z_GROUPS)
-
-
-def reduce_along_z(part):
-    pair = lax.psum_scatter(
-        part, "ctx", scatter_dimension=0, axis_index_groups=Z_GROUPS, tiled=True
-    )
-    return pair.reshape(2, -1, part.shape[1])
-
-
-def reduce_over_lo(pair):
-    lo = lax.axis_index("ctx") % 2
-    kept = jnp.where(lo == 0, pair[0], pair[1])
-    sent = jnp.where(lo == 0, pair[1], pair[0])
-    return kept.astype(f32) + lax.ppermute(sent, "ctx", XL_SWAP).astype(f32)
-
-
-def gather_over_lo(own):
-    return ordered(own, lax.ppermute(own, "ctx", XL_SWAP), lax.axis_index("ctx") % 2)
 
 
 def both_cores(mine):
@@ -227,8 +216,7 @@
         out_part += contract(branch_other[:, cols], low, 0, 0)
         both = jnp.concatenate([qkv_part, out_part], axis=1).astype(bf16)
         for j in range(2):
-            place = (2 * i + j) % 4 * 2 + (2 * i + j) // 4
-            base = place * (shard + 16)
+            base = (2 * i + j) * (shard + 16)
             grads[base : base + shard, :] = both[j * shard : (j + 1) * shard, :]
             grads[base + shard : base + shard + 16, :] = pad
 
@@ -258,6 +246,15 @@
         grad_rows[:, at] = contract(grad_gu[...], weight[:, : 2 * units], 1, 1).astype(bf16)
 
 
+def output_kernel(hi, mine, other, weight_own, weight_far, out_mine, out_other):
+    width = weight_own.shape[0]
+    units = mine.shape[1]
+    for weight, place in ((weight_own, hi[0]), (weight_far, 1 - hi[0])):
+        at = pl.ds(pl.multiple_of(place * width, HEAD), width)
+        for rows, out in ((other, out_other), (mine, out_mine)):
+            out[:, at] = contract(rows[...], weight[:, 2 * units :], 1, 1).astype(bf16)
+
+
 def down_grad_kernel(parts, out):
     start = 0
     for i in range(8):
@@ -277,7 +274,7 @@
             start += BLOCK
 
 
-def attention_weight_grad_kernel(parts, grad_qkv, grad_out, sums):
+def attention_weight_grad_kernel(parts, grad_qkv, grad_out, sums, rest):
     shard = grad_qkv.shape[0]
     qcols = GROUP_Q * HEAD
     pairs = 0.0
@@ -292,6 +289,7 @@
         tails += tail[:, HEAD : 3 * HEAD]
     grad_qkv[:, qcols:] = pairs
     sums[:, qcols:] = tails
+    rest[...] = sum(parts[i, shard:, :].astype(f32) for i in range(8))
 
 
 def local_call(kernel, outs, scratch=()):
@@ -329,6 +327,19 @@
     return local_call(attention_grad_kernel, outs, scratch)(
         branch_mine, branch_other, mine, other, gain, att, *rest
     )
+
+
+def output_rows(hi, rows, weight_own, weight_far):
+    shape = (rows[0].shape[0], 2 * weight_own.shape[0])
+    whole = [pl.BlockSpec(memory_space=pltpu.VMEM)] * 4
+    return pl.pallas_call(
+        output_kernel,
+        in_specs=[pl.BlockSpec(memory_space=pltpu.SMEM)] + whole,
+        out_specs=[pl.BlockSpec(memory_space=pltpu.VMEM)] * 2,
+        out_shape=[jax.ShapeDtypeStruct(shape, bf16)] * 2,
+        compiler_params=pltpu.CompilerParams(vmem_limit_bytes=VMEM_BYTES),
+        cost_estimate=COST,
+    )(hi, *rows, weight_own, weight_far)
 
 
 def feed_forward(hi, rows, grad, weight_own, weight_far):
@@ -432,7 +443,6 @@
     down_own = lax.dynamic_slice_in_dim(down_weight, start, units).T
     ffn_own = jnp.concatenate([gu_own[:, 0], gu_own[:, 1], down_own], axis=1)
     ffn_line = gather_along_y(ffn_own)
-    ffn_far = lax.ppermute(ffn_own, "fsdp", XH_SWAP)
 
     att_all = gather_small(att_own, att_far)
     extra = att_all[:, shard].astype(f32)
@@ -449,19 +459,23 @@
     cosine, sine = rotary(places - first)
     order = (cosine, sine, first[:, None], places[:, None], places[None, :])
 
-    unit_mine, grad_own = tie(gather(unit_own, "ctx"), grad_own)
+    ffn_far = lax.ppermute(ffn_own, "fsdp", XH_SWAP)
+    unit_mine, att_all, grad_own, ffn_line, ffn_far, *order = tie(
+        gather(unit_own, "ctx"), att_all, grad_own, ffn_line, ffn_far, *order
+    )
+    ffn_far = gather_along_y(ffn_far)
     grad_mine = gather(grad_own, "ctx")
     units_all = both_cores(unit_mine)
     held = attention(*units_all, gain_a, att_all, bias, *order)
-    *held, grad_mine, ffn_far = tie(*held, grad_mine, ffn_far)
+    *held, grad_mine = tie(*held, grad_mine)
     query, key, value, attended, log_total, branch_mine, branch_other = held
-    ffn_far = gather_along_y(ffn_far)
     grads = both_cores(grad_mine)
     branch_parts = pair_sums(branch_mine, branch_other)
-    branch = reduce(branch_parts, "ctx")
+    branch = summed(spread(branch_parts, "ctx"))
     middle = tok + branch
     scale_m = rms_scale(middle)
     normed2_mine = gather((middle * scale_m * gain_m).astype(bf16), "ctx")
+    normed2_mine, ffn_far, *grads = tie(normed2_mine, ffn_far, *grads)
     normed2 = both_cores(normed2_mine)
 
     hi = (f // 4)[None]
@@ -471,45 +485,63 @@
     parts = pair_sums(*parts)
     parts, *held = tie(parts, *normed2, *grad_gu, *hidden, *grads)
     normed2, grad_gu, hidden, grads = held[0:2], held[2:4], held[4:6], held[6:8]
-    grad_normed2 = reduce(parts, "ctx")
-
-    down_sums = reduce_along_y(by_y(over_rows(grads, hidden)))
-    grad_normed2, gu_blocks = tie(grad_normed2, by_y(over_rows(normed2, grad_gu)))
+    normed2_parts = spread(parts, "ctx")
+
+    gu_blocks, *held = tie(by_y(over_rows(normed2, grad_gu)), *grads, *hidden)
+    grads, hidden = held[:2], held[2:]
     gu_sums = reduce_along_y(gu_blocks)
-
-    def output_rows(rows):
-        own_side = contract(rows, ffn_line[:, 2 * units :], 1, 1).astype(bf16)
-        far_side = contract(rows, ffn_far[:, 2 * units :], 1, 1).astype(bf16)
-        return jnp.concatenate(
-            [jnp.where(f < 4, own_side, far_side), jnp.where(f < 4, far_side, own_side)], axis=1
-        )
-
-    grad_middle = cot + norm_back(middle, scale_m, gain_m, grad_normed2)
-    branch_mine = gather(grad_middle.astype(bf16), "ctx")
-    branch_mine, down_share = tie(branch_mine, reduce_over_hi(down_sums))
+    output_parts = pair_sums(*output_rows(hi, hidden, ffn_line, ffn_far))
+    normed2_parts, down_blocks, output_parts = tie(
+        normed2_parts, by_y(over_rows(grads, hidden)), output_parts
+    )
+    down_sums = reduce_along_y(down_blocks)
+
+    grad_middle = cot + norm_back(middle, scale_m, gain_m, summed(normed2_parts))
+    gu_kept, gu_got = swap_over_hi(gu_sums)
+    branch_mine, gu_kept, gu_got, output_parts = tie(
+        gather(grad_middle.astype(bf16), "ctx"), gu_kept, gu_got, output_parts
+    )
+    output_pair = lax.psum_scatter(
+        output_parts.reshape(-1, width),
+        "ctx",
+        scatter_dimension=0,
+        axis_index_groups=Z_GROUPS,
+        tiled=True,
+    ).reshape(2, own, width)
+    gu_share = added(gu_kept, gu_got)
+    gu_far = lax.ppermute(gu_share, "ctx", XL_SWAP)
     grad_branch = both_cores(branch_mine)
-    down_part = gather(down_share, "ctx")
     normed_mine, normed_other, att_grads = attention_grad(
         *grad_branch, *units_all, gain_a, att_all, query, key, value, attended, log_total, *order
     )
-    att_grads, down_part = tie(att_grads, down_part)
-    att_sums = reduce_along_y(att_grads)
+    att_grads, gu_far, down_sums = tie(att_grads, gu_far, down_sums)
+    att_parts = spread(att_grads.reshape(8, -1, 4 * HEAD), "fsdp")
+    gu_part = gather_along_z(ordered(gu_share, gu_far, c % 2)).reshape(8, shard, -1)
     normed_parts = pair_sums(normed_mine, normed_other)
-    grad_normed, gu_share, *hidden = tie(
-        reduce(normed_parts, "ctx"), reduce_over_hi(gu_sums), *hidden
-    )
-    gu_part = gather(gu_share, "ctx")
-    grad_tokens = both_halves(grad_middle + norm_back(tok, scale_a, gain_a, grad_normed))
-    output_parts = pair_sums(*[output_rows(h) for h in hidden])
+    down_kept, down_got = swap_over_hi(down_sums)
+    gain_part = jnp.sum(gu_share.astype(f32) * ffn_own[:, : 2 * units].astype(f32), axis=1)
+    gain_row = jnp.pad(gain_part.astype(bf16)[None], ((shard + 1, 14), (0, 4 * HEAD - shard)))
+    att_parts, down_kept, down_got, gain_row, normed_parts, output_pair = tie(
+        att_parts, down_kept, down_got, gain_row, normed_parts, output_pair
+    )
+    att_part = gather((summed(att_parts) + gain_row).astype(bf16), "ctx")
+    output_kept = jnp.where(c % 2 == 0, output_pair[0], output_pair[1])
+    output_sent = jnp.where(c % 2 == 0, output_pair[1], output_pair[0])
+    output_got = lax.ppermute(output_sent, "ctx", XL_SWAP)
+    down_share = added(down_kept, down_got)
+    down_far = lax.ppermute(down_share, "ctx", XL_SWAP)
+    att_part, down_share, down_far, output_kept, output_got, normed_parts = tie(
+        att_part, down_share, down_far, output_kept, output_got, normed_parts
+    )
+    output = both_halves(middle + output_kept.astype(f32) + output_got.astype(f32))
+    down_part = gather_along_z(ordered(down_share, down_far, c % 2)).reshape(8, shard, units)
+    normed_parts = spread(normed_parts, "ctx")
+    grad_tokens = both_halves(
+        grad_middle + norm_back(tok, scale_a, gain_a, summed(normed_parts))
+    )
     grad_down_weight = assemble(
         down_grad_kernel, down_part, [((shard, down_weight.shape[0]), f32)]
     )[0]
-    att_share, gu_part, output_parts, grad_down_weight, grad_tokens = tie(
-        reduce_over_hi(att_sums), gu_part, output_parts, grad_down_weight, grad_tokens
-    )
-    att_part = gather(att_share, "ctx")
-    output_pair = reduce_along_z(output_parts.reshape(-1, width))
-    output = both_halves(middle + reduce_over_lo(output_pair))
     grad_gu_weight = pl.pallas_call(
         gate_up_grad_kernel,
         grid=(shard // GRAD_ROWS,),
@@ -519,10 +551,15 @@
         compiler_params=pltpu.CompilerParams(vmem_limit_bytes=VMEM_BYTES),
         cost_estimate=COST,
     )(gu_part)
-    grad_qkv_weight, grad_out_weight, sums = assemble(
+    grad_qkv_weight, grad_out_weight, sums, rest = assemble(
         attention_weight_grad_kernel,
         att_part,
-        [(qkv_weight.shape, f32), ((shard, qcols), f32), ((16, qkv_weight.shape[1]), f32)],
+        [
+            (qkv_weight.shape, f32),
+            ((shard, qcols), f32),
+            ((16, qkv_weight.shape[1]), f32),
+            ((16, 4 * HEAD), f32),
+        ],
     )
     split_at = qcols + HEAD
     own_bias = lax.dynamic_slice(sums, (0, f * (split_at // 8)), (1, split_at // 8))
@@ -530,8 +567,7 @@
     gain_sums = jnp.stack(
         [
             jnp.sum(grad_qkv_weight * qkv_weight.astype(f32), axis=1) / norm_attn.astype(f32),
-            jnp.sum(grad_gu_weight * gate_up_weight.astype(f32), axis=(1, 2))
-            / norm_mlp.astype(f32),
+            rest[1, :shard] / norm_mlp.astype(f32),
         ]
     )
     gain_sums = gain_sums + lax.ppermute(gain_sums, "tp", TP_SWAP)

time: 445 us -> 418 us (0.939)
  starting transfers between devices: 84 us -> 70.1 us
  matrix products: 17.8 us -> 10.2 us
  other arithmetic: 43.2 us -> 36 us
  Pallas kernels: 59.3 us -> 66.4 us
    all_to_all x7 -> x5, waiting for transfers between devices: 87.4 us -> 45.3 us  [gather(): return lax.all_to_all(copies, axis, 0, 0, tiled=True)]
    ppermute x4 -> x5, waiting for transfers between devices: 36.2 us -> 58 us  [the longest x2 31.1 us: swap_over_hi(): lax.ppermute(sent, 'fsdp', XH_SWAP)]
    all_to_all x3 -> x4, waiting for transfers between devices: 31.7 us -> 46.4 us  [spread(): return lax.all_to_all(part, axis, 0, 0, tiled=True)]
    ppermute x6, waiting for transfers between devices: 0.02 us -> 14.6 us  [gather_small(): piece = lax.ppermute(base, 'fsdp', y_shift(k))]
    all_to_all x7 -> x5, starting transfers between devices: 31.7 us -> 21.8 us  [gather(): return lax.all_to_all(copies, axis, 0, 0, tiled=True)]
    reduce_scatter x3 -> x2, waiting for transfers between devices: 10.9 us -> 3.22 us  [reduce_along_y(): lax.psum_scatter(part, 'fsdp', scatter_dimension=0, axis_index_groups=Y_G...]
    dot_general x8 -> x4, matrix products: 17.8 us -> 10.2 us  [contract(): lax.dot_general(left, right, (((left_dim,), (right_dim,)), ((), ())), pre...]
    pallas_call x0 -> x1, Pallas kernels: none -> 7.14 us  [output_rows(): pl.pallas_call(output_kernel, in_specs=[pl.BlockSpec(memory_space=pltpu.S...]
  transfers between devices with their start and end apart: 39 -> 40, of which waited for: 17 -> 19; matrix products, arithmetic and copies ran while one was open for 18% -> 15% of each run, Pallas kernels for 11% -> 13%
where the time goes in v3:
time: 418 us; the launch traced here: 410 us
  waiting for transfers between devices  180 us (43%)
  starting transfers between devices  70.1 us (17%)
  Pallas kernels  66.4 us (16%)
  other arithmetic  36 us (9%)
  local copies, waits for them, and re-layouts  33 us (8%)
  between operations  15.2 us (4%)
  matrix products  10.2 us (2%)
    all_to_all x4, waiting for transfers between devices, spread(): return lax.all_to_all(part, axis, 0, 0, tiled=True)  46.4 us
    all_to_all x5, waiting for transfers between devices, gather(): return lax.all_to_all(copies, axis, 0, 0, tiled=True)  45.3 us
    ppermute x2, waiting for transfers between devices, swap_over_hi(): lax.ppermute(sent, 'fsdp', XH_SWAP)  31.1 us
    ppermute x1, waiting for transfers between devices, on_device(): output_got = lax.ppermute(output_sent, 'ctx', XL_SWAP)  26.9 us
    all_to_all x5, starting transfers between devices, gather(): return lax.all_to_all(copies, axis, 0, 0, tiled=True)  21.8 us
    pallas_call x2, Pallas kernels, feed_forward(): pl.pallas_call(ffn_kernel, grid_spec=pltpu.PrefetchScalarGridSpec(num_sca...  20.8 us
    all_to_all x4, starting transfers between devices, spread(): return lax.all_to_all(part, axis, 0, 0, tiled=True)  15.3 us
    pallas_call x1, Pallas kernels, attention_grad(): local_call(attention_grad_kernel, outs, scratch)  14.9 us
  transfers between devices with their start and end apart: 40, of which 19 were waited for; matrix products, arithmetic and copies ran while one was open for 15% of the time, Pallas kernels for 13%

profile of v3, /device:TPU:1, one launch (start us, length us, event | category | flops | bytes accessed | tf_op | source)
XLA Modules:
  0.0 410.5 jit_solution(11311432676757347476)
XLA Ops:
  25.4 6.1 %all-to-all-start = ((bf16[8,64,1536]{2,1,0:T(8,128)(2,1)}), bf16[8,64,1536]{2,1,0:T(8,128)(2,1)}, u32[]{:S(2)}, u32[]{:S(2)}) async-start(bf16[8,64,1536]{2,1,0:T(8,128)(2,1)} %broadcast_in_dim.89), calls=%async_computation | async-start | bytes 3145728 | tf_op jit(solution)/shard_map/all_to_all | solution.py:49
  44.9 6.5 %collective-permute-done.4 = bf16[208,512]{1,0:T(8,128)(2,1)S(1)} collective-permute-done((bf16[208,512]{1,0:T(8,128)(2,1)S(1)}, bf16[208,512]{1,0:T(8,128)(2,1)S(1)}, u32[]{:S(2)}, u32[]{:S(2)}) %collective-permute-start.4) | collective-permute-done | bytes 213024 | tf_op jit(solution)/shard_map/ppermute | solution.py:67
  51.5 8.0 %collective-permute-done.6 = bf16[208,512]{1,0:T(8,128)(2,1)S(1)} collective-permute-done((bf16[208,512]{1,0:T(8,128)(2,1)S(1)}, bf16[208,512]{1,0:T(8,128)(2,1)S(1)}, u32[]{:S(2)}, u32[]{:S(2)}) %collective-permute-start.6) | collective-permute-done | bytes 213024 | tf_op jit(solution)/shard_map/ppermute | solution.py:67
  59.6 3.5 all-to-all-done
  66.8 4.0 all-to-all-start.1
  74.5 9.9 %shard_map.186 = (bf16[1024,128]{1,0:T(8,128)(2,1)}, bf16[1024,128]{1,0:T(8,128)(2,1)}, bf16[1024,128]{1,0:T(8,128)(2,1)}, bf16[1024,128]{1,0:T(8,128)(2,1)}, f3...) custom-call(bf16[512,1536]{1,0:T(8,128)(2,1)} %bitcast.19.mine, ...), custom_call_target="tpu_custom_call" | custom-call | flops 1000000 | bytes 100000 | tf_op jit(solution)/shard_map/pallas_call | solution.py:312
  84.4 7.5 %all-to-all-done.1 = bf16[8,64,1536]{2,1,0:T(8,128)(2,1)S(1)} async-done(((bf16[8,64,1536]{2,1,0:T(8,128)(2,1)}), bf16[8,64,1536]{2,1,0:T(8,128)(2,1)S(1)}, u32[]{:S(2)}, u32[]{:S(2)}) %all-to-all-start.1) | async-done | bytes 1572896 | tf_op jit(solution)/shard_map/all_to_all | solution.py:49
  93.1 3.2 collective-permute-done.9
  99.2 3.6 all-to-all-start.2
  103.3 20.6 %all-to-all-done.2 = bf16[8,64,1536]{2,1,0:T(8,128)(2,1)S(1)} async-done(((bf16[8,64,1536]{2,1,0:T(8,128)(2,1)}), bf16[8,64,1536]{2,1,0:T(8,128)(2,1)S(1)}, u32[]{:S(2)}, u32[]{:S(2)}) %all-to-all-start.2) | async-done | bytes 1572896 | tf_op jit(solution)/shard_map/all_to_all | solution.py:53
  127.1 3.6 all-to-all-start.3
  130.8 20.0 %all-to-all-done.3 = bf16[8,64,1536]{2,1,0:T(8,128)(2,1)S(1)} async-done(((bf16[8,64,1536]{2,1,0:T(8,128)(2,1)}), bf16[8,64,1536]{2,1,0:T(8,128)(2,1)S(1)}, u32[]{:S(2)}, u32[]{:S(2)}) %all-to-all-start.3) | async-done | bytes 1572896 | tf_op jit(solution)/shard_map/all_to_all | solution.py:49
  157.1 10.4 %shard_map.188 = (bf16[512,640]{1,0:T(8,128)(2,1)}, bf16[512,1280]{1,0:T(8,128)(2,1)}, bf16[512,1536]{1,0:T(8,128)(2,1)}) custom-call(s32[1]{0:T(128)} %bitcast.22.hi, bf16[512,1536]{1,0:T(8,128)(2,1)} %copy-done.16, bf16[512,1536]{1,0:T(8,128)(2,1)} %collective-permute-done.10.grad, bf16[768,1920]{1,0:T(8,128)(2,1)} %all-gather.7.cloned.1.call-done.weight_own, ...), custom_call_target="tpu_custom_call" | custom-call | flops 1000000 | bytes 100000 | tf_op jit(solution)/shard_map/pallas_call | solution.py:353
  168.4 10.4 %shard_map.187 = (bf16[512,640]{1,0:T(8,128)(2,1)}, bf16[512,1280]{1,0:T(8,128)(2,1)}, bf16[512,1536]{1,0:T(8,128)(2,1)}) custom-call(s32[1]{0:T(128)} %bitcast.22.hi, bf16[512,1536]{1,0:T(8,128)(2,1)} %bitcast.99, bf16[512,1536]{1,0:T(8,128)(2,1)} %bitcast.93, bf16[768,1920]{1,0:T(8,128)(2,1)} %all-gather.7.cloned.1.call-done.weight_own, ...), custom_call_target="tpu_custom_call" | custom-call | flops 1000000 | bytes 100000 | tf_op jit(solution)/shard_map/pallas_call | solution.py:353
  178.8 3.1 add_convert_fusion.3
  188.9 7.1 %shard_map.189 = (bf16[512,1536]{1,0:T(8,128)(2,1)}, bf16[512,1536]{1,0:T(8,128)(2,1)}) custom-call(s32[1]{0:T(128)} %bitcast.22.hi, bf16[512,640]{1,0:T(8,128)(2,1)} %get-tuple-element.130.mine, bf16[512,640]{1,0:T(8,128)(2,1)} %get-tuple-element.132.other, bf16[768,1920]{1,0:T(8,128)(2,1)} %all-gather.7.cloned.1.call-done.weight_own, ...), custom_call_target="tpu_custom_call" | custom-call | flops 1000000 | bytes 100000 | tf_op jit(solution)/shard_map/pallas_call | solution.py:335
  196.1 3.7 all-to-all-start.4
  210.5 10.3 %all-to-all-done.4 = bf16[8,64,1536]{2,1,0:T(8,128)(2,1)S(1)} async-done(((bf16[8,64,1536]{2,1,0:T(8,128)(2,1)}), bf16[8,64,1536]{2,1,0:T(8,128)(2,1)S(1)}, u32[]{:S(2)}, u32[]{:S(2)}) %all-to-all-start.4) | async-done | bytes 1572896 | tf_op jit(solution)/shard_map/all_to_all | solution.py:53
  224.2 3.6 all-to-all-start.5
  227.9 3.2 reduce-scatter.4.cloned.1.call-done
  235.8 12.0 %all-to-all-done.5 = bf16[8,64,1536]{2,1,0:T(8,128)(2,1)S(1)} async-done(((bf16[8,64,1536]{2,1,0:T(8,128)(2,1)}), bf16[8,64,1536]{2,1,0:T(8,128)(2,1)S(1)}, u32[]{:S(2)}, u32[]{:S(2)}) %all-to-all-start.5) | async-done | bytes 1572896 | tf_op jit(solution)/shard_map/all_to_all | solution.py:49
  247.8 10.0 %collective-permute-done.14 = bf16[192,1280]{1,0:T(8,128)(2,1)S(1)} collective-permute-done((bf16[192,1280]{1,0:T(8,128)(2,1)}, bf16[192,1280]{1,0:T(8,128)(2,1)S(1)}, u32[]{:S(2)}, u32[]{:S(2)}) %collective-permute-start.14) | collective-permute-done | bytes 491552 | tf_op jit(solution)/shard_map/ppermute | solution.py:91
  263.6 14.9 %shard_map.190 = (bf16[512,1536]{1,0:T(8,128)(2,1)}, bf16[512,1536]{1,0:T(8,128)(2,1)}, bf16[1664,512]{1,0:T(8,128)(2,1)}) custom-call(bf16[512,1536]{1,0:T(8,128)(2,1)} %bitcast.103, bf16[512,1536]{1,0:T(8,128)(2,1)} %collective-permute-done.15.branch_other, bf16[512,1536]{1,0:T(8,128)(2,1)} %bitcast.19.mine, ...), custom_call_target="tpu_custom_call" | custom-call | flops 1000000 | bytes 100000 | tf_op jit(solution)/shard_map/pallas_call | solution.py:327
  280.1 4.5 %all-to-all-start.6 = ((bf16[8,208,512]{2,1,0:T(8,128)(2,1)}), bf16[8,208,512]{2,1,0:T(8,128)(2,1)}, u32[]{:S(2)}, u32[]{:S(2)}) async-start(bf16[8,208,512]{2,1,0:T(8,128)(2,1)} %bitcast.106), calls=%async_computation.8 | async-start | bytes 3407872 | tf_op jit(solution)/shard_map/all_to_all | solution.py:53
  290.6 21.1 %collective-permute-done.17 = bf16[192,640]{1,0:T(8,128)(2,1)S(1)} collective-permute-done((bf16[192,640]{1,0:T(8,128)(2,1)S(1)}, bf16[192,640]{1,0:T(8,128)(2,1)S(1)}, u32[]{:S(2)}, u32[]{:S(2)}) %collective-permute-start.17) | collective-permute-done | bytes 245792 | tf_op jit(solution)/shard_map/ppermute | solution.py:91
  314.9 4.6 %all-to-all-start.7 = ((bf16[8,208,512]{2,1,0:T(8,128)(2,1)}), bf16[8,208,512]{2,1,0:T(8,128)(2,1)}, u32[]{:S(2)}, u32[]{:S(2)}) async-start(bf16[8,208,512]{2,1,0:T(8,128)(2,1)} %broadcast_in_dim.108), calls=%async_computation.10 | async-start | bytes 3407872 | tf_op jit(solution)/shard_map/all_to_all | solution.py:49
  321.6 26.9 %collective-permute-done.20 = bf16[64,1536]{1,0:T(8,128)(2,1)S(1)} collective-permute-done((bf16[64,1536]{1,0:T(8,128)(2,1)S(1)}, bf16[64,1536]{1,0:T(8,128)(2,1)S(1)}, u32[]{:S(2)}, u32[]{:S(2)}) %collective-permute-start.20) | collective-permute-done | bytes 196640 | tf_op jit(solution)/shard_map/ppermute | solution.py:530
  358.3 3.6 all-to-all-start.8
  367.8 15.6 %all-to-all-done.8 = bf16[8,64,1536]{2,1,0:T(8,128)(2,1)S(1)} async-done(((bf16[8,64,1536]{2,1,0:T(8,128)(2,1)}), bf16[8,64,1536]{2,1,0:T(8,128)(2,1)S(1)}, u32[]{:S(2)}, u32[]{:S(2)}) %all-to-all-start.8) | async-done | bytes 1572896 | tf_op jit(solution)/shard_map/all_to_all | solution.py:53
  387.8 7.5 %shard_map.192 = f32[192,2,4480]{2,1,0:T(2,128)} custom-call(bf16[8,192,1280]{2,1,0:T(8,128)(2,1)} %all-gather.11.cloned.1.call-done.parts), custom_call_target="tpu_custom_call" | custom-call | flops 1000000 | bytes 100000 | tf_op jit(solution)/shard_map/pallas_call | solution.py:545
  395.3 4.5 %all-gather.13.cloned.1.call-done.parts = bf16[8,192,640]{2,1,0:T(8,128)(2,1)} async-done(((bf16[2,192,640]{2,1,0:T(8,128)(2,1)}), bf16[8,192,640]{2,1,0:T(8,128)(2,1)}) %all-gather.13.cloned.1.call-update) | async-done | bytes 1966096 | tf_op jit(solution)/shard_map/all_gather | solution.py:99
  399.9 3.5 shard_map.193
  (253 shorter events, 118.2 us)
Async XLA Ops:
  7.2 55.8 %all-gather.7.cloned.1.call-start = ((), (), s32[]{:S(2)}) async-start(), calls=%async_computation.12 | async-start | bytes 3686400 | tf_op jit(solution)/shard_map/all_gather | solution.py:73
  14.7 24.7 %collective-permute-start = (bf16[208,512]{1,0:T(8,128)(2,1)S(1)}, bf16[208,512]{1,0:T(8,128)(2,1)}, u32[]{:S(2)}, u32[]{:S(2)}) collective-permute-start(bf16[208,512]{1,0:T(8,128)(2,1)S(1)} %maximum_maximum_fusion), channel_id=1, source_target_pairs={{0,16},{16,32},{32,48},{48,0},{64,80},{80,96},{96,112},{112,64},{1... | collective-permute-start | bytes 638984 | tf_op jit(solution)/shard_map/ppermute | solution.py:67
  16.9 25.8 %collective-permute-start.1 = (bf16[208,512]{1,0:T(8,128)(2,1)S(1)}, bf16[208,512]{1,0:T(8,128)(2,1)}, u32[]{:S(2)}, u32[]{:S(2)}) collective-permute-start(bf16[208,512]{1,0:T(8,128)(2,1)S(1)} %maximum_maximum_fusion), channel_id=1, source_target_pairs={{0,48},{16,0},{32,16},{48,32},{64,112},{80,64},{96,80},{112,96},{1... | collective-permute-start | bytes 638984 | tf_op jit(solution)/shard_map/ppermute | solution.py:67
  18.4 25.5 %collective-permute-start.2 = (bf16[208,512]{1,0:T(8,128)(2,1)S(1)}, bf16[208,512]{1,0:T(8,128)(2,1)}, u32[]{:S(2)}, u32[]{:S(2)}) collective-permute-start(bf16[208,512]{1,0:T(8,128)(2,1)S(1)} %maximum_maximum_fusion), channel_id=1, source_target_pairs={{0,32},{16,48},{32,0},{48,16},{64,96},{80,112},{96,64},{112,80},{1... | collective-permute-start | bytes 638984 | tf_op jit(solution)/shard_map/ppermute | solution.py:67
  20.0 19.0 %collective-permute-start.3 = (bf16[208,512]{1,0:T(8,128)(2,1)S(1)}, bf16[208,512]{1,0:T(8,128)(2,1)S(1)}, u32[]{:S(2)}, u32[]{:S(2)}) collective-permute-start(bf16[208,512]{1,0:T(8,128)(2,1)S(1)} %maximum_maximum_fusion), channel_id=1, source_target_pairs={{0,64},{16,80},{32,96},{48,112},{64,0},{80,16},{96,32},{112,48},{1... | collective-permute-start | bytes 638984 | tf_op jit(solution)/shard_map/ppermute | solution.py:436
  22.7 36.8 %collective-permute-start.7 = (bf16[192,1920]{1,0:T(8,128)(2,1)}, bf16[192,1920]{1,0:T(8,128)(2,1)}, u32[]{:S(2)}, u32[]{:S(2)}) collective-permute-start(bf16[192,1920]{1,0:T(8,128)(2,1)} %pad_maximum_fusion.3), channel_id=1, source_target_pairs={{0,64},{16,80},{32,96},{48,112},{64,0},{80,16},{96,32},{112,48},{1... | collective-permute-start | bytes 2211848 | tf_op jit(solution)/shard_map/ppermute | solution.py:462
  25.4 37.6 %all-to-all-start = ((bf16[8,64,1536]{2,1,0:T(8,128)(2,1)}), bf16[8,64,1536]{2,1,0:T(8,128)(2,1)}, u32[]{:S(2)}, u32[]{:S(2)}) async-start(bf16[8,64,1536]{2,1,0:T(8,128)(2,1)} %broadcast_in_dim.89), calls=%async_computation | async-start | bytes 3145728 | tf_op jit(solution)/shard_map/all_to_all | solution.py:49
  38.9 12.5 %collective-permute-start.4 = (bf16[208,512]{1,0:T(8,128)(2,1)S(1)}, bf16[208,512]{1,0:T(8,128)(2,1)S(1)}, u32[]{:S(2)}, u32[]{:S(2)}) collective-permute-start(bf16[208,512]{1,0:T(8,128)(2,1)S(1)} %collective-permute-done.3), channel_id=1, source_target_pairs={{0,16},{16,32},{32,48},{48,0},{64,80},{80,96},{96,112},{112,64},{1... | collective-permute-start | bytes 638984 | tf_op jit(solution)/shard_map/ppermute | solution.py:67
  39.4 12.0 %collective-permute-start.5 = (bf16[208,512]{1,0:T(8,128)(2,1)S(1)}, bf16[208,512]{1,0:T(8,128)(2,1)S(1)}, u32[]{:S(2)}, u32[]{:S(2)}) collective-permute-start(bf16[208,512]{1,0:T(8,128)(2,1)S(1)} %collective-permute-done.3), channel_id=1, source_target_pairs={{0,48},{16,0},{32,16},{48,32},{64,112},{80,64},{96,80},{112,96},{1... | collective-permute-start | bytes 638984 | tf_op jit(solution)/shard_map/ppermute | solution.py:67
  42.7 16.9 %collective-permute-start.6 = (bf16[208,512]{1,0:T(8,128)(2,1)S(1)}, bf16[208,512]{1,0:T(8,128)(2,1)S(1)}, u32[]{:S(2)}, u32[]{:S(2)}) collective-permute-start(bf16[208,512]{1,0:T(8,128)(2,1)S(1)} %collective-permute-done.3), channel_id=1, source_target_pairs={{0,32},{16,48},{32,0},{48,16},{64,96},{80,112},{96,64},{112,80},{1... | collective-permute-start | bytes 638984 | tf_op jit(solution)/shard_map/ppermute | solution.py:67
  63.0 11.5 %collective-permute-start.8 = (bf16[512,1536]{1,0:T(8,128)(2,1)}, bf16[512,1536]{1,0:T(8,128)(2,1)}, u32[]{:S(2)}, u32[]{:S(2)}) collective-permute-start(bf16[512,1536]{1,0:T(8,128)(2,1)} %bitcast.19.mine), channel_id=1, source_target_pairs={{0,1},{1,0},{2,3},{3,2},{4,5},{5,4},{6,7},{7,6},{8,9},{9,8},{10,11... | collective-permute-start | bytes 4718600 | tf_op jit(solution)/shard_map/ppermute | solution.py:104
  66.8 25.1 %all-to-all-start.1 = ((bf16[8,64,1536]{2,1,0:T(8,128)(2,1)}), bf16[8,64,1536]{2,1,0:T(8,128)(2,1)S(1)}, u32[]{:S(2)}, u32[]{:S(2)}) async-start(bf16[8,64,1536]{2,1,0:T(8,128)(2,1)} %broadcast_in_dim.104), calls=%async_computation.1 | async-start | bytes 3145728 | tf_op jit(solution)/shard_map/all_to_all | solution.py:49
  70.7 60.0 %all-gather.9.cloned.1.call-start = ((), (), s32[]{:S(2)}) async-start(), calls=%async_computation.13 | async-start | bytes 3686400 | tf_op jit(solution)/shard_map/all_gather | solution.py:73
  99.2 24.7 %all-to-all-start.2 = ((bf16[8,64,1536]{2,1,0:T(8,128)(2,1)}), bf16[8,64,1536]{2,1,0:T(8,128)(2,1)S(1)}, u32[]{:S(2)}, u32[]{:S(2)}) async-start(bf16[8,64,1536]{2,1,0:T(8,128)(2,1)} %bitcast.101), calls=%async_computation.2 | async-start | bytes 3145728 | tf_op jit(solution)/shard_map/all_to_all | solution.py:53
  102.9 27.8 %collective-permute-start.10 = (bf16[512,1536]{1,0:T(8,128)(2,1)S(1)}, bf16[512,1536]{1,0:T(8,128)(2,1)}, u32[]{:S(2)}, u32[]{:S(2)}) collective-permute-start(bf16[512,1536]{1,0:T(8,128)(2,1)S(1)} %bitcast.92), channel_id=1, source_target_pairs={{0,1},{1,0},{2,3},{3,2},{4,5},{5,4},{6,7},{7,6},{8,9},{9,8},{10,11... | collective-permute-start | bytes 4718600 | tf_op jit(solution)/shard_map/ppermute | solution.py:104
  127.1 23.7 %all-to-all-start.3 = ((bf16[8,64,1536]{2,1,0:T(8,128)(2,1)}), bf16[8,64,1536]{2,1,0:T(8,128)(2,1)S(1)}, u32[]{:S(2)}, u32[]{:S(2)}) async-start(bf16[8,64,1536]{2,1,0:T(8,128)(2,1)} %broadcast_in_dim.106), calls=%async_computation.3 | async-start | bytes 3145728 | tf_op jit(solution)/shard_map/all_to_all | solution.py:49
  130.7 100.4 %reduce-scatter.4.cloned.1.call-start = ((), (), s32[]{:S(2)}) async-start(), calls=%async_computation.14 | async-start | bytes 4915200 | tf_op jit(solution)/shard_map/reduce_scatter | solution.py:82
  196.1 24.7 %all-to-all-start.4 = ((bf16[8,64,1536]{2,1,0:T(8,128)(2,1)}), bf16[8,64,1536]{2,1,0:T(8,128)(2,1)S(1)}, u32[]{:S(2)}, u32[]{:S(2)}) async-start(bf16[8,64,1536]{2,1,0:T(8,128)(2,1)} %bitcast.25), calls=%async_computation.4 | async-start | bytes 3145728 | tf_op jit(solution)/shard_map/all_to_all | solution.py:53
  199.9 79.1 %reduce-scatter.6.cloned.1.call-start = ((), (), s32[]{:S(2)}) async-start(), calls=%async_computation.15 | async-start | bytes 2457600 | tf_op jit(solution)/shard_map/reduce_scatter | solution.py:82
  224.2 23.6 %all-to-all-start.5 = ((bf16[8,64,1536]{2,1,0:T(8,128)(2,1)}), bf16[8,64,1536]{2,1,0:T(8,128)(2,1)S(1)}, u32[]{:S(2)}, u32[]{:S(2)}) async-start(bf16[8,64,1536]{2,1,0:T(8,128)(2,1)} %broadcast_in_dim.107), calls=%async_computation.5 | async-start | bytes 3145728 | tf_op jit(solution)/shard_map/all_to_all | solution.py:49
  227.8 84.0 %reduce-scatter.8.cloned.1.call-start = ((), (), s32[]{:S(2)}) async-start(), calls=%async_computation.16 | async-start | bytes 1966080 | tf_op jit(solution)/shard_map/reduce_scatter | solution.py:504
  233.1 24.7 %collective-permute-start.14 = (bf16[192,1280]{1,0:T(8,128)(2,1)}, bf16[192,1280]{1,0:T(8,128)(2,1)S(1)}, u32[]{:S(2)}, u32[]{:S(2)}) collective-permute-start(bf16[192,1280]{1,0:T(8,128)(2,1)} %get-tuple-element.178), channel_id=1, source_target_pairs={{0,64},{16,80},{32,96},{48,112},{64,0},{80,16},{96,32},{112,48},{1... | collective-permute-start | bytes 1474568 | tf_op jit(solution)/shard_map/ppermute | solution.py:91
  257.9 130.0 %all-gather.11.cloned.1.call-start = ((), (), s32[]{:S(2)}) async-start(), calls=%async_computation.17 | async-start | bytes 4915200 | tf_op jit(solution)/shard_map/all_gather | solution.py:99
  261.8 17.1 %collective-permute-start.16 = (bf16[192,1280]{1,0:T(8,128)(2,1)S(1)}, bf16[192,1280]{1,0:T(8,128)(2,1)S(1)}, u32[]{:S(2)}, u32[]{:S(2)}) collective-permute-start(bf16[192,1280]{1,0:T(8,128)(2,1)S(1)} %get-tuple-element.171), channel_id=1, source_target_pairs={{0,2},{2,0},{4,6},{6,4},{8,10},{10,8},{12,14},{14,12},{1,3},{3,1},... | collective-permute-start | bytes 1474568 | tf_op jit(solution)/shard_map/ppermute | solution.py:512
  280.1 31.7 %all-to-all-start.6 = ((bf16[8,208,512]{2,1,0:T(8,128)(2,1)}), bf16[8,208,512]{2,1,0:T(8,128)(2,1)}, u32[]{:S(2)}, u32[]{:S(2)}) async-start(bf16[8,208,512]{2,1,0:T(8,128)(2,1)} %bitcast.106), calls=%async_computation.8 | async-start | bytes 3407872 | tf_op jit(solution)/shard_map/all_to_all | solution.py:53
  284.7 27.1 %collective-permute-start.17 = (bf16[192,640]{1,0:T(8,128)(2,1)S(1)}, bf16[192,640]{1,0:T(8,128)(2,1)S(1)}, u32[]{:S(2)}, u32[]{:S(2)}) collective-permute-start(bf16[192,640]{1,0:T(8,128)(2,1)S(1)} %get-tuple-element.186), channel_id=1, source_target_pairs={{0,64},{16,80},{32,96},{48,112},{64,0},{80,16},{96,32},{112,48},{1... | collective-permute-start | bytes 737288 | tf_op jit(solution)/shard_map/ppermute | solution.py:91
  314.9 35.9 %all-to-all-start.7 = ((bf16[8,208,512]{2,1,0:T(8,128)(2,1)}), bf16[8,208,512]{2,1,0:T(8,128)(2,1)}, u32[]{:S(2)}, u32[]{:S(2)}) async-start(bf16[8,208,512]{2,1,0:T(8,128)(2,1)} %broadcast_in_dim.108), calls=%async_computation.10 | async-start | bytes 3407872 | tf_op jit(solution)/shard_map/all_to_all | solution.py:49
  319.6 28.8 %collective-permute-start.19 = (bf16[192,640]{1,0:T(8,128)(2,1)S(1)}, bf16[192,640]{1,0:T(8,128)(2,1)S(1)}, u32[]{:S(2)}, u32[]{:S(2)}) collective-permute-start(bf16[192,640]{1,0:T(8,128)(2,1)S(1)} %add_convert_fusion.6), channel_id=1, source_target_pairs={{0,2},{2,0},{4,6},{6,4},{8,10},{10,8},{12,14},{14,12},{1,3},{3,1},... | collective-permute-start | bytes 737288 | tf_op jit(solution)/shard_map/ppermute | solution.py:532
  321.2 27.2 %collective-permute-start.20 = (bf16[64,1536]{1,0:T(8,128)(2,1)S(1)}, bf16[64,1536]{1,0:T(8,128)(2,1)S(1)}, u32[]{:S(2)}, u32[]{:S(2)}) collective-permute-start(bf16[64,1536]{1,0:T(8,128)(2,1)S(1)} %get-tuple-element.190), channel_id=1, source_target_pairs={{0,2},{2,0},{4,6},{6,4},{8,10},{10,8},{12,14},{14,12},{1,3},{3,1},... | collective-permute-start | bytes 589832 | tf_op jit(solution)/shard_map/ppermute | solution.py:530
  358.3 25.1 %all-to-all-start.8 = ((bf16[8,64,1536]{2,1,0:T(8,128)(2,1)}), bf16[8,64,1536]{2,1,0:T(8,128)(2,1)S(1)}, u32[]{:S(2)}, u32[]{:S(2)}) async-start(bf16[8,64,1536]{2,1,0:T(8,128)(2,1)} %bitcast.38), calls=%async_computation.11 | async-start | bytes 3145728 | tf_op jit(solution)/shard_map/all_to_all | solution.py:53
  361.9 38.0 %all-gather.13.cloned.1.call-start = ((), (), s32[]{:S(2)}) async-start(), calls=%async_computation.18 | async-start | bytes 2457600 | tf_op jit(solution)/shard_map/all_gather | solution.py:99
  362.0 23.5 %collective-permute-start.21 = (f32[64,1536]{1,0:T(8,128)S(1)}, f32[64,1536]{1,0:T(8,128)S(1)}, u32[]{:S(2)}, u32[]{:S(2)}) collective-permute-start(f32[64,1536]{1,0:T(8,128)S(1)} %convert_add_fusion), channel_id=1, source_target_pairs={{0,1},{1,0},{2,3},{3,2},{4,5},{5,4},{6,7},{7,6},{8,9},{9,8},{10,11... | collective-permute-start | bytes 1179656 | tf_op jit(solution)/shard_map/ppermute | solution.py:119
  (48 other events, 436.9 us)
Sparse Core Ops, SparseCore 0:
  12.0 50.9 all-gather.6
  93.2 35.5 all-gather.8
  189.0 41.9 reduce-scatter.3
  233.9 28.3 reduce-scatter.5
  264.6 24.7 reduce-scatter.7
  290.9 64.8 all-gather.10
  366.7 33.1 all-gather.12

commit v4 on v3

--- a/solution.py
+++ b/solution.py
@@ -51,6 +51,10 @@
 
 def spread(part, axis):
     return lax.all_to_all(part, axis, 0, 0, tiled=True)
+
+
+def spread_along_z(part):
+    return lax.all_to_all(part, "ctx", 0, 0, tiled=True, axis_index_groups=Z_GROUPS)
 
 
 def summed(parts):
@@ -130,13 +134,14 @@
     return grads * cosine - pltpu.roll(grads, HEAD // 2, 1) * sine
 
 
-def masked_scores(query, key, first, last, places):
+def masked_scores(query, key, ends, places):
     scores = contract(query, key, 1, 1) * HEAD ** (-0.5)
+    first, last = ends[:, :1], ends[:, HEAD // 2 : HEAD // 2 + 1]
     return jnp.where((places >= first) & (places <= last), scores, -1e30)
 
 
 def attention_kernel(
-    mine, other, gain, att, bias, cosine, sine, first, last, places,
+    mine, other, gain, att, bias, cosine, sine, ends, places,
     query, key, value, attended, log_total, branch_mine, branch_other, weight,
 ):
     shard = weight.shape[0] // 8
@@ -154,7 +159,7 @@
     for i in range(4):
         at = slice(i * ROWS, (i + 1) * ROWS)
         half = slice(i % 2 * ROWS, (i % 2 + 1) * ROWS)
-        scores = masked_scores(query[at, :], key[...], first[at, :], last[at, :], places[...])
+        scores = masked_scores(query[at, :], key[...], ends[at, :], places[...])
         top = jnp.max(scores, axis=1, keepdims=True)
         raised = jnp.exp(scores - top)
         total = jnp.sum(raised, axis=1, keepdims=True)
@@ -168,7 +173,7 @@
 
 def attention_grad_kernel(
     branch_mine, branch_other, mine, other, gain, att, query, key, value, attended, log_total,
-    cosine, sine, first, last, places,
+    cosine, sine, ends, places,
     normed_mine, normed_other, grads, weight, normed, grad_qkv, grad_key, grad_value,
 ):
     shard = weight.shape[0] // 8
@@ -181,7 +186,7 @@
         normed[at, :] = (rows.astype(f32) * gain[...]).astype(bf16)
         branch = (branch_mine if i < 2 else branch_other)[half, :]
         grad_att = contract(branch, weight[:, 3 * HEAD :], 1, 0).astype(bf16)
-        scores = masked_scores(query[at, :], key[...], first[at, :], last[at, :], places[...])
+        scores = masked_scores(query[at, :], key[...], ends[at, :], places[...])
         probs = jnp.exp(scores - log_total[at, :])
         grad_probs = contract(grad_att, value[...], 1, 1)
         inner = jnp.sum(probs * grad_probs, axis=1, keepdims=True)
@@ -246,6 +251,17 @@
         grad_rows[:, at] = contract(grad_gu[...], weight[:, : 2 * units], 1, 1).astype(bf16)
 
 
+def weight_grad_kernel(left_mine, left_other, right_mine, right_other, out):
+    shard = left_mine.shape[1] // 8
+    for i in range(4):
+        cols = slice(2 * i * shard, 2 * (i + 1) * shard)
+        part = contract(left_mine[:, cols], right_mine[...], 0, 0)
+        part += contract(left_other[:, cols], right_other[...], 0, 0)
+        for j in range(2):
+            base = ((2 * i + j) % 4 * 2 + (2 * i + j) // 4) * shard
+            out[base : base + shard, :] = part[j * shard : (j + 1) * shard, :].astype(bf16)
+
+
 def output_kernel(hi, mine, other, weight_own, weight_far, out_mine, out_other):
     width = weight_own.shape[0]
     units = mine.shape[1]
@@ -306,11 +322,11 @@
     return local_call(kernel, outs)(parts)
 
 
-def attention(mine, other, gain, att, bias, cosine, sine, first, last, places):
+def attention(mine, other, gain, att, bias, cosine, sine, ends, places):
     half, width = mine.shape
     outs = [((2 * half, HEAD), bf16)] * 4 + [((2 * half, 1), f32)] + [((half, width), bf16)] * 2
     return local_call(attention_kernel, outs, [((width, 4 * HEAD), bf16)])(
-        mine, other, gain, att, bias, cosine, sine, first, last, places
+        mine, other, gain, att, bias, cosine, sine, ends, places
     )
 
 
@@ -327,6 +343,11 @@
     return local_call(attention_grad_kernel, outs, scratch)(
         branch_mine, branch_other, mine, other, gain, att, *rest
     )
+
+
+def weight_grad(lefts, rights):
+    outs = [((lefts[0].shape[1], rights[0].shape[1]), bf16)]
+    return local_call(weight_grad_kernel, outs)(*lefts, *rights)[0]
 
 
 def output_rows(hi, rows, weight_own, weight_far):
@@ -442,7 +463,6 @@
     gu_own = jnp.where(inside, gu_own, jnp.zeros_like(gu_own))
     down_own = lax.dynamic_slice_in_dim(down_weight, start, units).T
     ffn_own = jnp.concatenate([gu_own[:, 0], gu_own[:, 1], down_own], axis=1)
-    ffn_line = gather_along_y(ffn_own)
 
     att_all = gather_small(att_own, att_far)
     extra = att_all[:, shard].astype(f32)
@@ -457,25 +477,29 @@
     places = jnp.transpose(deal_all, (1, 0, 2)).reshape(-1)
     first = sequence_of(places, lengths[0])
     cosine, sine = rotary(places - first)
-    order = (cosine, sine, first[:, None], places[:, None], places[None, :])
-
+    ends = jnp.where(jnp.arange(HEAD) < HEAD // 2, first[:, None], places[:, None])
+    order = (cosine, sine, ends, places[None, :])
+
+    grad_far = lax.ppermute(grad_own, "ctx", XL_SWAP)
+    unit_mine, att_all, grad_own, grad_far, ffn_own, *order = tie(
+        gather(unit_own, "ctx"), att_all, grad_own, grad_far, ffn_own, *order
+    )
     ffn_far = lax.ppermute(ffn_own, "fsdp", XH_SWAP)
-    unit_mine, att_all, grad_own, ffn_line, ffn_far, *order = tie(
-        gather(unit_own, "ctx"), att_all, grad_own, ffn_line, ffn_far, *order
-    )
-    ffn_far = gather_along_y(ffn_far)
-    grad_mine = gather(grad_own, "ctx")
+    ffn_line = gather_along_y(ffn_own)
+    grad_pair = ordered(grad_own, grad_far, c % 2)
+    grad_mine = spread_along_z(jnp.broadcast_to(grad_pair[None], (4,) + grad_pair.shape))
     units_all = both_cores(unit_mine)
     held = attention(*units_all, gain_a, att_all, bias, *order)
-    *held, grad_mine = tie(*held, grad_mine)
+    *held, grad_mine, ffn_far = tie(*held, grad_mine, ffn_far)
     query, key, value, attended, log_total, branch_mine, branch_other = held
+    ffn_far = gather_along_y(ffn_far)
+    branch_parts = pair_sums(branch_mine, branch_other)
     grads = both_cores(grad_mine)
-    branch_parts = pair_sums(branch_mine, branch_other)
     branch = summed(spread(branch_parts, "ctx"))
     middle = tok + branch
     scale_m = rms_scale(middle)
     normed2_mine = gather((middle * scale_m * gain_m).astype(bf16), "ctx")
-    normed2_mine, ffn_far, *grads = tie(normed2_mine, ffn_far, *grads)
+    normed2_mine, ffn_line, ffn_far, *grads = tie(normed2_mine, ffn_line, ffn_far, *grads)
     normed2 = both_cores(normed2_mine)
 
     hi = (f // 4)[None]
@@ -490,58 +514,48 @@
     gu_blocks, *held = tie(by_y(over_rows(normed2, grad_gu)), *grads, *hidden)
     grads, hidden = held[:2], held[2:]
     gu_sums = reduce_along_y(gu_blocks)
-    output_parts = pair_sums(*output_rows(hi, hidden, ffn_line, ffn_far))
-    normed2_parts, down_blocks, output_parts = tie(
-        normed2_parts, by_y(over_rows(grads, hidden)), output_parts
+    normed2_parts, down_blocks, *output_raw = tie(
+        normed2_parts,
+        weight_grad(grads, hidden),
+        *output_rows(hi, hidden, ffn_line, ffn_far),
     )
     down_sums = reduce_along_y(down_blocks)
 
     grad_middle = cot + norm_back(middle, scale_m, gain_m, summed(normed2_parts))
+    output_parts = pair_sums(*output_raw)
     gu_kept, gu_got = swap_over_hi(gu_sums)
     branch_mine, gu_kept, gu_got, output_parts = tie(
         gather(grad_middle.astype(bf16), "ctx"), gu_kept, gu_got, output_parts
     )
-    output_pair = lax.psum_scatter(
-        output_parts.reshape(-1, width),
-        "ctx",
-        scatter_dimension=0,
-        axis_index_groups=Z_GROUPS,
-        tiled=True,
-    ).reshape(2, own, width)
+    output_parts = spread_along_z(output_parts.reshape(4, 2 * own, width))
     gu_share = added(gu_kept, gu_got)
     gu_far = lax.ppermute(gu_share, "ctx", XL_SWAP)
     grad_branch = both_cores(branch_mine)
     normed_mine, normed_other, att_grads = attention_grad(
         *grad_branch, *units_all, gain_a, att_all, query, key, value, attended, log_total, *order
     )
-    att_grads, gu_far, down_sums = tie(att_grads, gu_far, down_sums)
+    att_grads, gu_far, output_parts = tie(att_grads, gu_far, output_parts)
+    output_pair = summed(output_parts).reshape(2, own, width)
+    output_kept = jnp.where(c % 2 == 0, output_pair[0], output_pair[1])
+    output_sent = jnp.where(c % 2 == 0, output_pair[1], output_pair[0]).astype(bf16)
+    output_got = lax.ppermute(output_sent, "ctx", XL_SWAP)
     att_parts = spread(att_grads.reshape(8, -1, 4 * HEAD), "fsdp")
     gu_part = gather_along_z(ordered(gu_share, gu_far, c % 2)).reshape(8, shard, -1)
     normed_parts = pair_sums(normed_mine, normed_other)
-    down_kept, down_got = swap_over_hi(down_sums)
     gain_part = jnp.sum(gu_share.astype(f32) * ffn_own[:, : 2 * units].astype(f32), axis=1)
     gain_row = jnp.pad(gain_part.astype(bf16)[None], ((shard + 1, 14), (0, 4 * HEAD - shard)))
-    att_parts, down_kept, down_got, gain_row, normed_parts, output_pair = tie(
-        att_parts, down_kept, down_got, gain_row, normed_parts, output_pair
+    att_parts, down_sums, gain_row, normed_parts, output_kept, output_got = tie(
+        att_parts, down_sums, gain_row, normed_parts, output_kept, output_got
     )
     att_part = gather((summed(att_parts) + gain_row).astype(bf16), "ctx")
-    output_kept = jnp.where(c % 2 == 0, output_pair[0], output_pair[1])
-    output_sent = jnp.where(c % 2 == 0, output_pair[1], output_pair[0])
-    output_got = lax.ppermute(output_sent, "ctx", XL_SWAP)
+    down_kept, down_got = swap_over_hi(down_sums)
+    att_part, down_kept, down_got, normed_parts = tie(
+        att_part, down_kept, down_got, normed_parts
+    )
     down_share = added(down_kept, down_got)
-    down_far = lax.ppermute(down_share, "ctx", XL_SWAP)
-    att_part, down_share, down_far, output_kept, output_got, normed_parts = tie(
-        att_part, down_share, down_far, output_kept, output_got, normed_parts
-    )
-    output = both_halves(middle + output_kept.astype(f32) + output_got.astype(f32))
-    down_part = gather_along_z(ordered(down_share, down_far, c % 2)).reshape(8, shard, units)
-    normed_parts = spread(normed_parts, "ctx")
-    grad_tokens = both_halves(
-        grad_middle + norm_back(tok, scale_a, gain_a, summed(normed_parts))
-    )
-    grad_down_weight = assemble(
-        down_grad_kernel, down_part, [((shard, down_weight.shape[0]), f32)]
-    )[0]
+    down_pair = ordered(down_share, lax.ppermute(down_share, "ctx", XL_SWAP), c % 2)
+    down_part = gather_along_z(down_pair).reshape(8, shard, units)
+    output = both_halves(middle + output_kept + output_got.astype(f32))
     grad_gu_weight = pl.pallas_call(
         gate_up_grad_kernel,
         grid=(shard // GRAD_ROWS,),
@@ -551,6 +565,13 @@
         compiler_params=pltpu.CompilerParams(vmem_limit_bytes=VMEM_BYTES),
         cost_estimate=COST,
     )(gu_part)
+    normed_parts, grad_gu_weight = tie(spread(normed_parts, "ctx"), grad_gu_weight)
+    grad_tokens = both_halves(
+        grad_middle + norm_back(tok, scale_a, gain_a, summed(normed_parts))
+    )
+    grad_down_weight = assemble(
+        down_grad_kernel, down_part, [((shard, down_weight.shape[0]), f32)]
+    )[0]
     grad_qkv_weight, grad_out_weight, sums, rest = assemble(
         attention_weight_grad_kernel,
         att_part,

time: 418 us -> 407 us (0.974)
  waiting for transfers between devices: 180 us -> 149 us
  other arithmetic: 36 us -> 46.7 us
  starting transfers between devices: 70.1 us -> 80.8 us
  Pallas kernels: 66.4 us -> 73.2 us
  local copies, waits for them, and re-layouts: 33 us -> 28.6 us
    all_to_all x5 -> x4, waiting for transfers between devices: 45.3 us -> 25 us  [gather(): return lax.all_to_all(copies, axis, 0, 0, tiled=True)]
    all_to_all x4, waiting for transfers between devices: 46.4 us -> 32.1 us  [spread(): return lax.all_to_all(part, axis, 0, 0, tiled=True)]
    ppermute x6, waiting for transfers between devices: 14.6 us -> 4.04 us  [gather_small(): piece = lax.ppermute(base, 'fsdp', y_shift(k))]
    ppermute x1, waiting for transfers between devices: 26.9 us -> 18.5 us  [on_device(): output_got = lax.ppermute(output_sent, 'ctx', XL_SWAP)]
    all_to_all x0 -> x2, starting transfers between devices: none -> 8 us  [spread_along_z(): lax.all_to_all(part, 'ctx', 0, 0, tiled=True, axis_index_groups=Z_GROUPS)]
    all_gather x2, waiting for transfers between devices: 4.51 us -> 11.5 us  [gather_along_z(): return lax.all_gather(own, 'ctx', axis=0, axis_index_groups=Z_GROUPS)]
    pallas_call x0 -> x1, Pallas kernels: none -> 6.23 us  [weight_grad(): return local_call(weight_grad_kernel, outs)(*lefts, *rights)[0]]
    ppermute x1, waiting for transfers between devices: 0.01 us -> 6.06 us  [on_device(): ffn_far = lax.ppermute(ffn_own, 'fsdp', XH_SWAP)]
  transfers between devices with their start and end apart: 40 -> 41, of which waited for: 19 -> 17; matrix products, arithmetic and copies ran while one was open for 15% -> 15% of each run, Pallas kernels for 13% -> 16%
where the time goes in v4:
time: 407 us; the launch traced here: 399 us
  waiting for transfers between devices  149 us (37%)
  starting transfers between devices  80.8 us (20%)
  Pallas kernels  73.2 us (18%)
  other arithmetic  46.7 us (11%)
  local copies, waits for them, and re-layouts  28.6 us (7%)
  between operations  15.3 us (4%)
  matrix products  6.08 us (1%)
    ppermute x2, waiting for transfers between devices, swap_over_hi(): lax.ppermute(sent, 'fsdp', XH_SWAP)  33.1 us
    all_to_all x4, waiting for transfers between devices, spread(): return lax.all_to_all(part, axis, 0, 0, tiled=True)  32.1 us
    all_to_all x4, waiting for transfers between devices, gather(): return lax.all_to_all(copies, axis, 0, 0, tiled=True)  25 us
    pallas_call x2, Pallas kernels, feed_forward(): pl.pallas_call(ffn_kernel, grid_spec=pltpu.PrefetchScalarGridSpec(num_sca...  20.8 us
    ppermute x1, waiting for transfers between devices, on_device(): output_got = lax.ppermute(output_sent, 'ctx', XL_SWAP)  18.5 us
    all_to_all x4, starting transfers between devices, gather(): return lax.all_to_all(copies, axis, 0, 0, tiled=True)  16.8 us
    all_to_all x4, starting transfers between devices, spread(): return lax.all_to_all(part, axis, 0, 0, tiled=True)  15.9 us
    pallas_call x1, Pallas kernels, attention_grad(): local_call(attention_grad_kernel, outs, scratch)  14.8 us
  transfers between devices with their start and end apart: 41, of which 17 were waited for; matrix products, arithmetic and copies ran while one was open for 15% of the time, Pallas kernels for 16%

profile of v4, /device:TPU:1, one launch (start us, length us, event | category | flops | bytes accessed | tf_op | source)
XLA Modules:
  0.0 399.5 jit_solution(16222335515625463852)
XLA Ops:
  24.1 5.2 %all-to-all-start = ((bf16[8,64,1536]{2,1,0:T(8,128)(2,1)}), bf16[8,64,1536]{2,1,0:T(8,128)(2,1)}, u32[]{:S(2)}, u32[]{:S(2)}) async-start(bf16[8,64,1536]{2,1,0:T(8,128)(2,1)} %broadcast_in_dim.109), calls=%async_computation | async-start | bytes 3145728 | tf_op jit(solution)/shard_map/all_to_all | solution.py:49
  55.3 3.7 collective-permute-start.8
  61.4 4.0 all-to-all-start.1
  68.9 9.9 %shard_map.186 = (bf16[1024,128]{1,0:T(8,128)(2,1)}, bf16[1024,128]{1,0:T(8,128)(2,1)}, bf16[1024,128]{1,0:T(8,128)(2,1)}, bf16[1024,128]{1,0:T(8,128)(2,1)}, f3...) custom-call(bf16[512,1536]{1,0:T(8,128)(2,1)} %bitcast.18.mine, ...), custom_call_target="tpu_custom_call" | custom-call | flops 1000000 | bytes 100000 | tf_op jit(solution)/shard_map/pallas_call | solution.py:328
  78.9 6.1 %collective-permute-done.9 = bf16[192,1920]{1,0:T(8,128)(2,1)} collective-permute-done((bf16[192,1920]{1,0:T(8,128)(2,1)}, bf16[192,1920]{1,0:T(8,128)(2,1)}, u32[]{:S(2)}, u32[]{:S(2)}) %collective-permute-start.9) | collective-permute-done | bytes 737312 | tf_op jit(solution)/shard_map/ppermute | solution.py:487
  93.2 3.7 all-to-all-start.2
  97.8 20.0 %all-to-all-done.2 = bf16[8,64,1536]{2,1,0:T(8,128)(2,1)S(1)} async-done(((bf16[8,64,1536]{2,1,0:T(8,128)(2,1)}), bf16[8,64,1536]{2,1,0:T(8,128)(2,1)S(1)}, u32[]{:S(2)}, u32[]{:S(2)}) %all-to-all-start.2) | async-done | bytes 1572896 | tf_op jit(solution)/shard_map/all_to_all | solution.py:53
  120.5 4.3 %all-to-all-start.3 = ((bf16[8,64,1536]{2,1,0:T(8,128)(2,1)}), bf16[8,64,1536]{2,1,0:T(8,128)(2,1)}, u32[]{:S(2)}, u32[]{:S(2)}) async-start(bf16[8,64,1536]{2,1,0:T(8,128)(2,1)} %broadcast_in_dim.129), calls=%async_computation.3 | async-start | bytes 3145728 | tf_op jit(solution)/shard_map/all_to_all | solution.py:49
  124.9 19.8 %all-to-all-done.3 = bf16[8,64,1536]{2,1,0:T(8,128)(2,1)} async-done(((bf16[8,64,1536]{2,1,0:T(8,128)(2,1)}), bf16[8,64,1536]{2,1,0:T(8,128)(2,1)}, u32[]{:S(2)}, u32[]{:S(2)}) %all-to-all-start.3) | async-done | bytes 1572896 | tf_op jit(solution)/shard_map/all_to_all | solution.py:49
  151.5 10.4 %shard_map.188 = (bf16[512,640]{1,0:T(8,128)(2,1)}, bf16[512,1280]{1,0:T(8,128)(2,1)}, bf16[512,1536]{1,0:T(8,128)(2,1)}) custom-call(s32[1]{0:T(128)} %bitcast.23.hi, bf16[512,1536]{1,0:T(8,128)(2,1)} %copy-done.10, bf16[512,1536]{1,0:T(8,128)(2,1)} %collective-permute-done.11.grad.left_other, bf16[768,1920]{1,0:T(8,128)(2,1)} %all-gather.7.cloned.1.call-done.weight_own, ...), custom_call_target="tpu_custom_call" | custom-call | flops 1000000 | bytes 100000 | tf_op jit(solution)/shard_map/pallas_call | solution.py:374
  162.5 10.4 %shard_map.187 = (bf16[512,640]{1,0:T(8,128)(2,1)}, bf16[512,1280]{1,0:T(8,128)(2,1)}, bf16[512,1536]{1,0:T(8,128)(2,1)}) custom-call(s32[1]{0:T(128)} %bitcast.23.hi, bf16[512,1536]{1,0:T(8,128)(2,1)} %bitcast.25.rows, bf16[512,1536]{1,0:T(8,128)(2,1)} %bitcast.84, bf16[768,1920]{1,0:T(8,128)(2,1)} %all-gather.7.cloned.1.call-done.weight_own, ...), custom_call_target="tpu_custom_call" | custom-call | flops 1000000 | bytes 100000 | tf_op jit(solution)/shard_map/pallas_call | solution.py:374
  178.3 3.8 fusion
  184.3 3.6 all-to-all-start.4
  188.0 7.8 %shard_map.190 = (bf16[512,1536]{1,0:T(8,128)(2,1)}, bf16[512,1536]{1,0:T(8,128)(2,1)}) custom-call(s32[1]{0:T(128)} %bitcast.23.hi, bf16[512,640]{1,0:T(8,128)(2,1)} %get-tuple-element.134.right_mine.mine, bf16[512,640]{1,0:T(8,128)(2,1)} %get-tuple-element.135.right_other.other, bf16[768,1920]{1,0:T(8,128)(2,1)} %all-gather.7.cloned.1.call-done.weight_own, ...), custom_call_target="tpu_custom_call" | custom-call | flops 1000000 | bytes 100000 | tf_op jit(solution)/shard_map/pallas_call | solution.py:356
  195.7 6.2 %shard_map.189 = bf16[1536,640]{1,0:T(8,128)(2,1)} custom-call(bf16[512,1536]{1,0:T(8,128)(2,1)} %bitcast.85, bf16[512,1536]{1,0:T(8,128)(2,1)} %collective-permute-done.11.grad.left_other, bf16[512,640]{1,0:T(8,128)(2,1)} %get-tuple-element.134.right_mine.mine, bf16[512,640]{1,0:T(8,128)(2,1)} %get-tuple-element.135.right_other.other), custom_call_target="tpu_custom_call" | custom-call | flops 1000000 | bytes 100000 | tf_op jit(solution)/shard_map/pallas_call | solution.py:350
  202.0 7.2 %all-to-all-done.4 = bf16[8,64,1536]{2,1,0:T(8,128)(2,1)S(1)} async-done(((bf16[8,64,1536]{2,1,0:T(8,128)(2,1)}), bf16[8,64,1536]{2,1,0:T(8,128)(2,1)S(1)}, u32[]{:S(2)}, u32[]{:S(2)}) %all-to-all-start.4) | async-done | bytes 1572896 | tf_op jit(solution)/shard_map/all_to_all | solution.py:53
  213.9 3.6 all-to-all-start.5
  217.5 8.5 %reduce-scatter.3.cloned.1.call-done = bf16[384,1280]{1,0:T(8,128)(2,1)} async-done(((bf16[1536,1280]{1,0:T(8,128)(2,1)}), bf16[384,1280]{1,0:T(8,128)(2,1)}) %reduce-scatter.3.cloned.1.call-update) | async-done | bytes 983056 | tf_op jit(solution)/shard_map/reduce_scatter | solution.py:86
  233.8 5.2 %all-to-all-done.5 = bf16[8,64,1536]{2,1,0:T(8,128)(2,1)S(1)} async-done(((bf16[8,64,1536]{2,1,0:T(8,128)(2,1)}), bf16[8,64,1536]{2,1,0:T(8,128)(2,1)S(1)}, u32[]{:S(2)}, u32[]{:S(2)}) %all-to-all-start.5) | async-done | bytes 1572896 | tf_op jit(solution)/shard_map/all_to_all | solution.py:49
  239.0 9.3 %collective-permute-done.14 = bf16[192,1280]{1,0:T(8,128)(2,1)} collective-permute-done((bf16[192,1280]{1,0:T(8,128)(2,1)}, bf16[192,1280]{1,0:T(8,128)(2,1)}, u32[]{:S(2)}, u32[]{:S(2)}) %collective-permute-start.14) | collective-permute-done | bytes 491552 | tf_op jit(solution)/shard_map/ppermute | solution.py:95
  248.9 4.0 %all-to-all-start.6 = ((bf16[4,128,1536]{2,1,0:T(8,128)(2,1)}), bf16[4,128,1536]{2,1,0:T(8,128)(2,1)S(1)}, u32[]{:S(2)}, u32[]{:S(2)}) async-start(bf16[4,128,1536]{2,1,0:T(8,128)(2,1)} %bitcast.32), calls=%async_computation.7 | async-start | bytes 3145728 | tf_op jit(solution)/shard_map/all_to_all | solution.py:57
  255.9 14.8 %shard_map.191 = (bf16[512,1536]{1,0:T(8,128)(2,1)}, bf16[512,1536]{1,0:T(8,128)(2,1)}, bf16[1664,512]{1,0:T(8,128)(2,1)}) custom-call(bf16[512,1536]{1,0:T(8,128)(2,1)} %bitcast.89, bf16[512,1536]{1,0:T(8,128)(2,1)} %collective-permute-done.16.branch_other, bf16[512,1536]{1,0:T(8,128)(2,1)} %bitcast.18.mine, ...), custom_call_target="tpu_custom_call" | custom-call | flops 1000000 | bytes 100000 | tf_op jit(solution)/shard_map/pallas_call | solution.py:343
  277.6 4.3 %all-to-all-start.7 = ((bf16[8,208,512]{2,1,0:T(8,128)(2,1)}), bf16[8,208,512]{2,1,0:T(8,128)(2,1)S(1)}, u32[]{:S(2)}, u32[]{:S(2)}) async-start(bf16[8,208,512]{2,1,0:T(8,128)(2,1)} %bitcast.92), calls=%async_computation.8 | async-start | bytes 3407872 | tf_op jit(solution)/shard_map/all_to_all | solution.py:53
  288.8 18.5 %collective-permute-done.19 = bf16[64,1536]{1,0:T(8,128)(2,1)S(1)} collective-permute-done((bf16[64,1536]{1,0:T(8,128)(2,1)S(1)}, bf16[64,1536]{1,0:T(8,128)(2,1)S(1)}, u32[]{:S(2)}, u32[]{:S(2)}) %collective-permute-start.19) | collective-permute-done | bytes 196640 | tf_op jit(solution)/shard_map/ppermute | solution.py:541
  309.3 3.7 all-to-all-start.8
  313.1 3.3 collective-permute-start.21
  316.4 23.8 %collective-permute-done.21 = bf16[192,640]{1,0:T(8,128)(2,1)S(1)} collective-permute-done((bf16[192,640]{1,0:T(8,128)(2,1)S(1)}, bf16[192,640]{1,0:T(8,128)(2,1)S(1)}, u32[]{:S(2)}, u32[]{:S(2)}) %collective-permute-start.21) | collective-permute-done | bytes 245792 | tf_op jit(solution)/shard_map/ppermute | solution.py:95
  344.8 4.3 %all-to-all-start.9 = ((bf16[8,64,1536]{2,1,0:T(8,128)(2,1)}), bf16[8,64,1536]{2,1,0:T(8,128)(2,1)}, u32[]{:S(2)}, u32[]{:S(2)}) async-start(bf16[8,64,1536]{2,1,0:T(8,128)(2,1)} %bitcast.86), calls=%async_computation.11 | async-start | bytes 3145728 | tf_op jit(solution)/shard_map/all_to_all | solution.py:53
  358.4 7.4 %shard_map.192 = f32[192,2,4480]{2,1,0:T(2,128)} custom-call(bf16[8,192,1280]{2,1,0:T(8,128)(2,1)} %all-gather.11.cloned.1.call-done.parts), custom_call_target="tpu_custom_call" | custom-call | flops 1000000 | bytes 100000 | tf_op jit(solution)/shard_map/pallas_call | solution.py:559
  365.8 4.8 %all-to-all-done.9 = bf16[8,64,1536]{2,1,0:T(8,128)(2,1)} async-done(((bf16[8,64,1536]{2,1,0:T(8,128)(2,1)}), bf16[8,64,1536]{2,1,0:T(8,128)(2,1)}, u32[]{:S(2)}, u32[]{:S(2)}) %all-to-all-start.9) | async-done | bytes 1572896 | tf_op jit(solution)/shard_map/all_to_all | solution.py:53
  374.9 11.5 %all-gather.13.cloned.1.call-done.parts = bf16[8,192,640]{2,1,0:T(8,128)(2,1)} async-done(((bf16[2,192,640]{2,1,0:T(8,128)(2,1)}), bf16[8,192,640]{2,1,0:T(8,128)(2,1)}) %all-gather.13.cloned.1.call-update) | async-done | bytes 1966096 | tf_op jit(solution)/shard_map/all_gather | solution.py:103
  386.4 3.7 shard_map.194
  (251 shorter events, 127.3 us)
Async XLA Ops:
  11.6 33.2 %collective-permute-start = (bf16[208,512]{1,0:T(8,128)(2,1)}, bf16[208,512]{1,0:T(8,128)(2,1)}, u32[]{:S(2)}, u32[]{:S(2)}) collective-permute-start(bf16[208,512]{1,0:T(8,128)(2,1)} %maximum_maximum_fusion), channel_id=1, source_target_pairs={{0,16},{16,32},{32,48},{48,0},{64,80},{80,96},{96,112},{112,64},{1... | collective-permute-start | bytes 638984 | tf_op jit(solution)/shard_map/ppermute | solution.py:71
  13.7 34.3 %collective-permute-start.1 = (bf16[208,512]{1,0:T(8,128)(2,1)}, bf16[208,512]{1,0:T(8,128)(2,1)}, u32[]{:S(2)}, u32[]{:S(2)}) collective-permute-start(bf16[208,512]{1,0:T(8,128)(2,1)} %maximum_maximum_fusion), channel_id=1, source_target_pairs={{0,48},{16,0},{32,16},{48,32},{64,112},{80,64},{96,80},{112,96},{1... | collective-permute-start | bytes 638984 | tf_op jit(solution)/shard_map/ppermute | solution.py:71
  15.2 34.0 %collective-permute-start.2 = (bf16[208,512]{1,0:T(8,128)(2,1)}, bf16[208,512]{1,0:T(8,128)(2,1)}, u32[]{:S(2)}, u32[]{:S(2)}) collective-permute-start(bf16[208,512]{1,0:T(8,128)(2,1)} %maximum_maximum_fusion), channel_id=1, source_target_pairs={{0,32},{16,48},{32,0},{48,16},{64,96},{80,112},{96,64},{112,80},{1... | collective-permute-start | bytes 638984 | tf_op jit(solution)/shard_map/ppermute | solution.py:71
  16.8 27.5 %collective-permute-start.3 = (bf16[208,512]{1,0:T(8,128)(2,1)}, bf16[208,512]{1,0:T(8,128)(2,1)}, u32[]{:S(2)}, u32[]{:S(2)}) collective-permute-start(bf16[208,512]{1,0:T(8,128)(2,1)} %maximum_maximum_fusion), channel_id=1, source_target_pairs={{0,64},{16,80},{32,96},{48,112},{64,0},{80,16},{96,32},{112,48},{1... | collective-permute-start | bytes 638984 | tf_op jit(solution)/shard_map/ppermute | solution.py:457
  24.1 31.1 %all-to-all-start = ((bf16[8,64,1536]{2,1,0:T(8,128)(2,1)}), bf16[8,64,1536]{2,1,0:T(8,128)(2,1)}, u32[]{:S(2)}, u32[]{:S(2)}) async-start(bf16[8,64,1536]{2,1,0:T(8,128)(2,1)} %broadcast_in_dim.109), calls=%async_computation | async-start | bytes 3145728 | tf_op jit(solution)/shard_map/all_to_all | solution.py:49
  29.3 95.5 %all-gather.7.cloned.1.call-start = ((), (), s32[]{:S(2)}) async-start(), calls=%async_computation.12 | async-start | bytes 3686400 | tf_op jit(solution)/shard_map/all_gather | solution.py:77
  31.1 24.2 %collective-permute-start.7 = (bf16[64,1536]{1,0:T(8,128)(2,1)}, bf16[64,1536]{1,0:T(8,128)(2,1)}, u32[]{:S(2)}, u32[]{:S(2)}) collective-permute-start(bf16[64,1536]{1,0:T(8,128)(2,1)} %dynamic-slice_convert_fusion), channel_id=1, source_target_pairs={{0,2},{2,0},{4,6},{6,4},{8,10},{10,8},{12,14},{14,12},{1,3},{3,1},... | collective-permute-start | bytes 589832 | tf_op jit(solution)/shard_map/ppermute | solution.py:483
  55.3 13.6 %collective-permute-start.8 = (bf16[512,1536]{1,0:T(8,128)(2,1)}, bf16[512,1536]{1,0:T(8,128)(2,1)}, u32[]{:S(2)}, u32[]{:S(2)}) collective-permute-start(bf16[512,1536]{1,0:T(8,128)(2,1)} %bitcast.18.mine), channel_id=1, source_target_pairs={{0,1},{1,0},{2,3},{3,2},{4,5},{5,4},{6,7},{7,6},{8,9},{9,8},{10,11... | collective-permute-start | bytes 4718600 | tf_op jit(solution)/shard_map/ppermute | solution.py:108
  61.4 24.1 %all-to-all-start.1 = ((bf16[4,2,64,1536]{3,2,1,0:T(8,128)(2,1)}), bf16[4,2,64,1536]{3,2,1,0:T(8,128)(2,1)S(1)}, u32[]{:S(2)}, u32[]{:S(2)}) async-start(bf16[4,2,64,1536]{3,2,1,0:T(8,128)(2,1)} %broadcast_in_dim.127), calls=%async_computation.1 | async-start | bytes 3145728 | tf_op jit(solution)/shard_map/all_to_all | solution.py:57
  65.4 79.3 %all-gather.9.cloned.1.call-start = ((), (), s32[]{:S(2)}) async-start(), calls=%async_computation.13 | async-start | bytes 3686400 | tf_op jit(solution)/shard_map/all_gather | solution.py:77
  65.4 19.5 %collective-permute-start.9 = (bf16[192,1920]{1,0:T(8,128)(2,1)}, bf16[192,1920]{1,0:T(8,128)(2,1)}, u32[]{:S(2)}, u32[]{:S(2)}) collective-permute-start(bf16[192,1920]{1,0:T(8,128)(2,1)} %pad_maximum_fusion.3), channel_id=1, source_target_pairs={{0,64},{16,80},{32,96},{48,112},{64,0},{80,16},{96,32},{112,48},{1... | collective-permute-start | bytes 2211848 | tf_op jit(solution)/shard_map/ppermute | solution.py:487
  93.2 24.5 %all-to-all-start.2 = ((bf16[8,64,1536]{2,1,0:T(8,128)(2,1)}), bf16[8,64,1536]{2,1,0:T(8,128)(2,1)S(1)}, u32[]{:S(2)}, u32[]{:S(2)}) async-start(bf16[8,64,1536]{2,1,0:T(8,128)(2,1)} %bitcast.87), calls=%async_computation.2 | async-start | bytes 3145728 | tf_op jit(solution)/shard_map/all_to_all | solution.py:53
  97.1 27.8 %collective-permute-start.11 = (bf16[512,1536]{1,0:T(8,128)(2,1)S(1)}, bf16[512,1536]{1,0:T(8,128)(2,1)}, u32[]{:S(2)}, u32[]{:S(2)}) collective-permute-start(bf16[512,1536]{1,0:T(8,128)(2,1)S(1)} %bitcast.83), channel_id=1, source_target_pairs={{0,1},{1,0},{2,3},{3,2},{4,5},{5,4},{6,7},{7,6},{8,9},{9,8},{10,11... | collective-permute-start | bytes 4718600 | tf_op jit(solution)/shard_map/ppermute | solution.py:108
  120.5 24.2 %all-to-all-start.3 = ((bf16[8,64,1536]{2,1,0:T(8,128)(2,1)}), bf16[8,64,1536]{2,1,0:T(8,128)(2,1)}, u32[]{:S(2)}, u32[]{:S(2)}) async-start(bf16[8,64,1536]{2,1,0:T(8,128)(2,1)} %broadcast_in_dim.129), calls=%async_computation.3 | async-start | bytes 3145728 | tf_op jit(solution)/shard_map/all_to_all | solution.py:49
  124.8 101.2 %reduce-scatter.3.cloned.1.call-start = ((), (), s32[]{:S(2)}) async-start(), calls=%async_computation.14 | async-start | bytes 4915200 | tf_op jit(solution)/shard_map/reduce_scatter | solution.py:86
  161.9 10.9 %collective-permute-start.13 = (bf16[512,1536]{1,0:T(8,128)(2,1)}, bf16[512,1536]{1,0:T(8,128)(2,1)S(1)}, u32[]{:S(2)}, u32[]{:S(2)}) collective-permute-start(bf16[512,1536]{1,0:T(8,128)(2,1)} %get-tuple-element.118), channel_id=1, source_target_pairs={{0,1},{1,0},{2,3},{3,2},{4,5},{5,4},{6,7},{7,6},{8,9},{9,8},{10,11... | collective-permute-start | bytes 4718600 | tf_op jit(solution)/shard_map/ppermute | solution.py:112
  184.3 24.9 %all-to-all-start.4 = ((bf16[8,64,1536]{2,1,0:T(8,128)(2,1)}), bf16[8,64,1536]{2,1,0:T(8,128)(2,1)S(1)}, u32[]{:S(2)}, u32[]{:S(2)}) async-start(bf16[8,64,1536]{2,1,0:T(8,128)(2,1)} %bitcast.26), calls=%async_computation.4 | async-start | bytes 3145728 | tf_op jit(solution)/shard_map/all_to_all | solution.py:53
  187.9 100.9 %reduce-scatter.5.cloned.1.call-start = ((), (), s32[]{:S(2)}) async-start(), calls=%async_computation.15 | async-start | bytes 2457600 | tf_op jit(solution)/shard_map/reduce_scatter | solution.py:86
  209.2 21.7 %collective-permute-start.15 = (bf16[512,1536]{1,0:T(8,128)(2,1)}, bf16[512,1536]{1,0:T(8,128)(2,1)}, u32[]{:S(2)}, u32[]{:S(2)}) collective-permute-start(bf16[512,1536]{1,0:T(8,128)(2,1)} %get-tuple-element.141), channel_id=1, source_target_pairs={{0,1},{1,0},{2,3},{3,2},{4,5},{5,4},{6,7},{7,6},{8,9},{9,8},{10,11... | collective-permute-start | bytes 4718600 | tf_op jit(solution)/shard_map/ppermute | solution.py:112
  213.9 25.1 %all-to-all-start.5 = ((bf16[8,64,1536]{2,1,0:T(8,128)(2,1)}), bf16[8,64,1536]{2,1,0:T(8,128)(2,1)S(1)}, u32[]{:S(2)}, u32[]{:S(2)}) async-start(bf16[8,64,1536]{2,1,0:T(8,128)(2,1)} %broadcast_in_dim.130), calls=%async_computation.5 | async-start | bytes 3145728 | tf_op jit(solution)/shard_map/all_to_all | solution.py:49
  228.2 20.2 %collective-permute-start.14 = (bf16[192,1280]{1,0:T(8,128)(2,1)}, bf16[192,1280]{1,0:T(8,128)(2,1)}, u32[]{:S(2)}, u32[]{:S(2)}) collective-permute-start(bf16[192,1280]{1,0:T(8,128)(2,1)} %get-tuple-element.182), channel_id=1, source_target_pairs={{0,64},{16,80},{32,96},{48,112},{64,0},{80,16},{96,32},{112,48},{1... | collective-permute-start | bytes 1474568 | tf_op jit(solution)/shard_map/ppermute | solution.py:95
  248.9 24.6 %all-to-all-start.6 = ((bf16[4,128,1536]{2,1,0:T(8,128)(2,1)}), bf16[4,128,1536]{2,1,0:T(8,128)(2,1)S(1)}, u32[]{:S(2)}, u32[]{:S(2)}) async-start(bf16[4,128,1536]{2,1,0:T(8,128)(2,1)} %bitcast.32), calls=%async_computation.7 | async-start | bytes 3145728 | tf_op jit(solution)/shard_map/all_to_all | solution.py:57
  253.0 105.5 %all-gather.11.cloned.1.call-start = ((), (), s32[]{:S(2)}) async-start(), calls=%async_computation.16 | async-start | bytes 4915200 | tf_op jit(solution)/shard_map/all_gather | solution.py:103
  254.6 16.1 %collective-permute-start.17 = (bf16[192,1280]{1,0:T(8,128)(2,1)S(1)}, bf16[192,1280]{1,0:T(8,128)(2,1)}, u32[]{:S(2)}, u32[]{:S(2)}) collective-permute-start(bf16[192,1280]{1,0:T(8,128)(2,1)S(1)} %get-tuple-element.175), channel_id=1, source_target_pairs={{0,2},{2,0},{4,6},{6,4},{8,10},{10,8},{12,14},{14,12},{1,3},{3,1},... | collective-permute-start | bytes 1474568 | tf_op jit(solution)/shard_map/ppermute | solution.py:532
  277.6 29.7 %all-to-all-start.7 = ((bf16[8,208,512]{2,1,0:T(8,128)(2,1)}), bf16[8,208,512]{2,1,0:T(8,128)(2,1)S(1)}, u32[]{:S(2)}, u32[]{:S(2)}) async-start(bf16[8,208,512]{2,1,0:T(8,128)(2,1)} %bitcast.92), calls=%async_computation.8 | async-start | bytes 3407872 | tf_op jit(solution)/shard_map/all_to_all | solution.py:53
  283.8 23.5 %collective-permute-start.19 = (bf16[64,1536]{1,0:T(8,128)(2,1)S(1)}, bf16[64,1536]{1,0:T(8,128)(2,1)S(1)}, u32[]{:S(2)}, u32[]{:S(2)}) collective-permute-start(bf16[64,1536]{1,0:T(8,128)(2,1)S(1)} %select_convert_fusion), channel_id=1, source_target_pairs={{0,2},{2,0},{4,6},{6,4},{8,10},{10,8},{12,14},{14,12},{1,3},{3,1},... | collective-permute-start | bytes 589832 | tf_op jit(solution)/shard_map/ppermute | solution.py:541
  309.3 30.9 %all-to-all-start.8 = ((bf16[8,208,512]{2,1,0:T(8,128)(2,1)}), bf16[8,208,512]{2,1,0:T(8,128)(2,1)S(1)}, u32[]{:S(2)}, u32[]{:S(2)}) async-start(bf16[8,208,512]{2,1,0:T(8,128)(2,1)} %broadcast_in_dim.131), calls=%async_computation.10 | async-start | bytes 3407872 | tf_op jit(solution)/shard_map/all_to_all | solution.py:49
  313.1 27.1 %collective-permute-start.21 = (bf16[192,640]{1,0:T(8,128)(2,1)S(1)}, bf16[192,640]{1,0:T(8,128)(2,1)S(1)}, u32[]{:S(2)}, u32[]{:S(2)}) collective-permute-start(bf16[192,640]{1,0:T(8,128)(2,1)S(1)} %get-tuple-element.190), channel_id=1, source_target_pairs={{0,64},{16,80},{32,96},{48,112},{64,0},{80,16},{96,32},{112,48},{1... | collective-permute-start | bytes 737288 | tf_op jit(solution)/shard_map/ppermute | solution.py:95
  344.8 25.8 %all-to-all-start.9 = ((bf16[8,64,1536]{2,1,0:T(8,128)(2,1)}), bf16[8,64,1536]{2,1,0:T(8,128)(2,1)}, u32[]{:S(2)}, u32[]{:S(2)}) async-start(bf16[8,64,1536]{2,1,0:T(8,128)(2,1)} %bitcast.86), calls=%async_computation.11 | async-start | bytes 3145728 | tf_op jit(solution)/shard_map/all_to_all | solution.py:53
  349.1 37.3 %all-gather.13.cloned.1.call-start = ((), (), s32[]{:S(2)}) async-start(), calls=%async_computation.17 | async-start | bytes 2457600 | tf_op jit(solution)/shard_map/all_gather | solution.py:103
  355.8 18.5 %collective-permute-start.23 = (f32[2,192]{1,0:T(2,128)S(1)}, f32[2,192]{1,0:T(2,128)S(1)}, u32[]{:S(2)}, u32[]{:S(2)}) collective-permute-start(f32[2,192]{1,0:T(2,128)S(1)} %pad_maximum_fusion.8), channel_id=1, source_target_pairs={{0,1},{1,0},{2,3},{3,2},{4,5},{5,4},{6,7},{7,6},{8,9},{9,8},{10,11... | collective-permute-start | bytes 4616 | tf_op jit(solution)/shard_map/ppermute | solution.py:594
  373.4 16.7 %collective-permute-start.22 = (f32[64,1536]{1,0:T(8,128)}, f32[64,1536]{1,0:T(8,128)}, u32[]{:S(2)}, u32[]{:S(2)}) collective-permute-start(f32[64,1536]{1,0:T(8,128)} %subtract_add_fusion), channel_id=1, source_target_pairs={{0,1},{1,0},{2,3},{3,2},{4,5},{5,4},{6,7},{7,6},{8,9},{9,8},{10,11... | collective-permute-start | bytes 1179656 | tf_op jit(solution)/shard_map/ppermute | solution.py:123
  (47 other events, 272.9 us)
Sparse Core Ops, SparseCore 0:
  55.4 40.1 all-gather.6
  97.2 38.0 all-gather.8
  184.4 41.5 reduce-scatter.2
  228.8 28.3 reduce-scatter.4
  276.5 57.0 all-gather.10
  351.9 34.4 all-gather.12

commit v5 on v4

--- a/solution.py
+++ b/solution.py
@@ -17,6 +17,7 @@
 ROWS = 256
 GRAD_ROWS = 64
 VMEM_BYTES = 60 * 2**20
+VMEM_PART = 32 * 2**20
 COST = pl.CostEstimate(flops=10**6, bytes_accessed=10**5, transcendentals=0)
 
 TP_SWAP = [(0, 1), (1, 0)]
@@ -77,11 +78,6 @@
     return lax.all_gather(own, "fsdp", axis=0, axis_index_groups=Y_GROUPS, tiled=True)
 
 
-def by_y(part):
-    rows, width = part.shape
-    return jnp.swapaxes(part.astype(bf16).reshape(2, 4, -1, width), 0, 1).reshape(rows, width)
-
-
 def reduce_along_y(part):
     pair = lax.psum_scatter(
         part, "fsdp", scatter_dimension=0, axis_index_groups=Y_GROUPS, tiled=True
@@ -112,10 +108,6 @@
     got = lax.ppermute(other, "tp", TP_SWAP)
     total = (mine.astype(f32) + got.astype(f32)).astype(bf16)
     return total.reshape(8, -1, total.shape[1])
-
-
-def over_rows(lefts, rights):
-    return contract(lefts[0], rights[0], 0, 0) + contract(lefts[1], rights[1], 0, 0)
 
 
 def both_halves(own):
@@ -292,28 +284,31 @@
 
 def attention_weight_grad_kernel(parts, grad_qkv, grad_out, sums, rest):
     shard = grad_qkv.shape[0]
+    base = parts.shape[1] - shard - 16
+    at = slice(base, base + shard)
+    tail = slice(base + shard, base + shard + 16)
     qcols = GROUP_Q * HEAD
     pairs = 0.0
     tails = 0.0
     for i in range(GROUP_Q):
         cols = slice(i * HEAD, (i + 1) * HEAD)
-        grad_qkv[:, cols] = parts[i, :shard, :HEAD].astype(f32)
-        grad_out[:, cols] = parts[i, :shard, 3 * HEAD :].astype(f32)
-        tail = parts[i, shard:, :].astype(f32)
-        sums[:, cols] = tail[:, :HEAD]
-        pairs += parts[i, :shard, HEAD : 3 * HEAD].astype(f32)
-        tails += tail[:, HEAD : 3 * HEAD]
+        grad_qkv[:, cols] = parts[i, at, :HEAD].astype(f32)
+        grad_out[:, cols] = parts[i, at, 3 * HEAD :].astype(f32)
+        last = parts[i, tail, :].astype(f32)
+        sums[:, cols] = last[:, :HEAD]
+        pairs += parts[i, at, HEAD : 3 * HEAD].astype(f32)
+        tails += last[:, HEAD : 3 * HEAD]
     grad_qkv[:, qcols:] = pairs
     sums[:, qcols:] = tails
-    rest[...] = sum(parts[i, shard:, :].astype(f32) for i in range(8))
-
-
-def local_call(kernel, outs, scratch=()):
+    rest[...] = sum(parts[i, tail, :].astype(f32) for i in range(8))
+
+
+def local_call(kernel, outs, scratch=(), limit=VMEM_PART):
     return pl.pallas_call(
         kernel,
         out_shape=[jax.ShapeDtypeStruct(shape, dtype) for shape, dtype in outs],
         scratch_shapes=[pltpu.VMEM(shape, dtype) for shape, dtype in scratch],
-        compiler_params=pltpu.CompilerParams(vmem_limit_bytes=VMEM_BYTES),
+        compiler_params=pltpu.CompilerParams(vmem_limit_bytes=limit),
         cost_estimate=COST,
     )
 
@@ -325,7 +320,7 @@
 def attention(mine, other, gain, att, bias, cosine, sine, ends, places):
     half, width = mine.shape
     outs = [((2 * half, HEAD), bf16)] * 4 + [((2 * half, 1), f32)] + [((half, width), bf16)] * 2
-    return local_call(attention_kernel, outs, [((width, 4 * HEAD), bf16)])(
+    return local_call(attention_kernel, outs, [((width, 4 * HEAD), bf16)], VMEM_BYTES)(
         mine, other, gain, att, bias, cosine, sine, ends, places
     )
 
@@ -340,7 +335,7 @@
         ((2 * half, HEAD), f32),
         ((2 * half, HEAD), f32),
     ]
-    return local_call(attention_grad_kernel, outs, scratch)(
+    return local_call(attention_grad_kernel, outs, scratch, VMEM_BYTES)(
         branch_mine, branch_other, mine, other, gain, att, *rest
     )
 
@@ -358,7 +353,7 @@
         in_specs=[pl.BlockSpec(memory_space=pltpu.SMEM)] + whole,
         out_specs=[pl.BlockSpec(memory_space=pltpu.VMEM)] * 2,
         out_shape=[jax.ShapeDtypeStruct(shape, bf16)] * 2,
-        compiler_params=pltpu.CompilerParams(vmem_limit_bytes=VMEM_BYTES),
+        compiler_params=pltpu.CompilerParams(vmem_limit_bytes=VMEM_PART),
         cost_estimate=COST,
     )(hi, *rows, weight_own, weight_far)
 
@@ -382,7 +377,7 @@
         out_shape=[
             jax.ShapeDtypeStruct((count, cols), bf16) for cols in (units, 2 * units, width)
         ],
-        compiler_params=pltpu.CompilerParams(vmem_limit_bytes=VMEM_BYTES),
+        compiler_params=pltpu.CompilerParams(vmem_limit_bytes=VMEM_PART),
         cost_estimate=COST,
     )(hi, rows, grad, weight_own, weight_far)
 
@@ -480,14 +475,14 @@
     ends = jnp.where(jnp.arange(HEAD) < HEAD // 2, first[:, None], places[:, None])
     order = (cosine, sine, ends, places[None, :])
 
-    grad_far = lax.ppermute(grad_own, "ctx", XL_SWAP)
-    unit_mine, att_all, grad_own, grad_far, ffn_own, *order = tie(
-        gather(unit_own, "ctx"), att_all, grad_own, grad_far, ffn_own, *order
+    grad_pair = ordered(grad_own, lax.ppermute(grad_own, "ctx", XL_SWAP), c % 2)
+    grad_copies = jnp.broadcast_to(grad_pair[None], (4,) + grad_pair.shape)
+    unit_mine, att_all, grad_copies, ffn_own, *order = tie(
+        gather(unit_own, "ctx"), att_all, grad_copies, ffn_own, *order
     )
     ffn_far = lax.ppermute(ffn_own, "fsdp", XH_SWAP)
     ffn_line = gather_along_y(ffn_own)
-    grad_pair = ordered(grad_own, grad_far, c % 2)
-    grad_mine = spread_along_z(jnp.broadcast_to(grad_pair[None], (4,) + grad_pair.shape))
+    grad_mine = spread_along_z(grad_copies)
     units_all = both_cores(unit_mine)
     held = attention(*units_all, gain_a, att_all, bias, *order)
     *held, grad_mine, ffn_far = tie(*held, grad_mine, ffn_far)
@@ -499,7 +494,6 @@
     middle = tok + branch
     scale_m = rms_scale(middle)
     normed2_mine = gather((middle * scale_m * gain_m).astype(bf16), "ctx")
-    normed2_mine, ffn_line, ffn_far, *grads = tie(normed2_mine, ffn_line, ffn_far, *grads)
     normed2 = both_cores(normed2_mine)
 
     hi = (f // 4)[None]
@@ -511,7 +505,7 @@
     normed2, grad_gu, hidden, grads = held[0:2], held[2:4], held[4:6], held[6:8]
     normed2_parts = spread(parts, "ctx")
 
-    gu_blocks, *held = tie(by_y(over_rows(normed2, grad_gu)), *grads, *hidden)
+    gu_blocks, *held = tie(weight_grad(normed2, grad_gu), *grads, *hidden)
     grads, hidden = held[:2], held[2:]
     gu_sums = reduce_along_y(gu_blocks)
     normed2_parts, down_blocks, *output_raw = tie(
@@ -534,27 +528,32 @@
     normed_mine, normed_other, att_grads = attention_grad(
         *grad_branch, *units_all, gain_a, att_all, query, key, value, attended, log_total, *order
     )
-    att_grads, gu_far, output_parts = tie(att_grads, gu_far, output_parts)
-    output_pair = summed(output_parts).reshape(2, own, width)
-    output_kept = jnp.where(c % 2 == 0, output_pair[0], output_pair[1])
-    output_sent = jnp.where(c % 2 == 0, output_pair[1], output_pair[0]).astype(bf16)
-    output_got = lax.ppermute(output_sent, "ctx", XL_SWAP)
+    att_grads, gu_share, gu_far, output_parts = tie(att_grads, gu_share, gu_far, output_parts)
     att_parts = spread(att_grads.reshape(8, -1, 4 * HEAD), "fsdp")
     gu_part = gather_along_z(ordered(gu_share, gu_far, c % 2)).reshape(8, shard, -1)
     normed_parts = pair_sums(normed_mine, normed_other)
+    normed_parts, down_sums, output_parts, gu_share = tie(
+        normed_parts, down_sums, output_parts, gu_share
+    )
+    down_kept, down_got = swap_over_hi(down_sums)
+    output_pair = summed(output_parts).reshape(2, own, width)
     gain_part = jnp.sum(gu_share.astype(f32) * ffn_own[:, : 2 * units].astype(f32), axis=1)
     gain_row = jnp.pad(gain_part.astype(bf16)[None], ((shard + 1, 14), (0, 4 * HEAD - shard)))
-    att_parts, down_sums, gain_row, normed_parts, output_kept, output_got = tie(
-        att_parts, down_sums, gain_row, normed_parts, output_kept, output_got
-    )
-    att_part = gather((summed(att_parts) + gain_row).astype(bf16), "ctx")
-    down_kept, down_got = swap_over_hi(down_sums)
-    att_part, down_kept, down_got, normed_parts = tie(
-        att_part, down_kept, down_got, normed_parts
+    output_kept = jnp.where(c % 2 == 0, output_pair[0], output_pair[1])
+    output_sent = jnp.where(c % 2 == 0, output_pair[1], output_pair[0]).astype(bf16)
+    att_parts, down_kept, down_got, gain_row, normed_parts, output_kept, output_sent = tie(
+        att_parts, down_kept, down_got, gain_row, normed_parts, output_kept, output_sent
+    )
+    att_share = (summed(att_parts) + gain_row).astype(bf16)
+    thirds = [normed_parts[:, :, i * 4 * HEAD : (i + 1) * 4 * HEAD] for i in range(3)]
+    packed = jnp.concatenate(
+        thirds + [jnp.broadcast_to(att_share[None], (8,) + att_share.shape)], axis=1
     )
     down_share = added(down_kept, down_got)
-    down_pair = ordered(down_share, lax.ppermute(down_share, "ctx", XL_SWAP), c % 2)
-    down_part = gather_along_z(down_pair).reshape(8, shard, units)
+    down_far = lax.ppermute(down_share, "ctx", XL_SWAP)
+    output_got = lax.ppermute(output_sent, "ctx", XL_SWAP)
+    packed, down_share, down_far, output_got = tie(packed, down_share, down_far, output_got)
+    down_part = gather_along_z(ordered(down_share, down_far, c % 2)).reshape(8, shard, units)
     output = both_halves(middle + output_kept + output_got.astype(f32))
     grad_gu_weight = pl.pallas_call(
         gate_up_grad_kernel,
@@ -562,16 +561,14 @@
         in_specs=[pl.BlockSpec((8, GRAD_ROWS, 2 * units), lambda i: (0, i, 0))],
         out_specs=pl.BlockSpec((GRAD_ROWS,) + gate_up_weight.shape[1:], lambda i: (i, 0, 0)),
         out_shape=jax.ShapeDtypeStruct(gate_up_weight.shape, f32),
-        compiler_params=pltpu.CompilerParams(vmem_limit_bytes=VMEM_BYTES),
+        compiler_params=pltpu.CompilerParams(vmem_limit_bytes=VMEM_PART),
         cost_estimate=COST,
     )(gu_part)
-    normed_parts, grad_gu_weight = tie(spread(normed_parts, "ctx"), grad_gu_weight)
-    grad_tokens = both_halves(
-        grad_middle + norm_back(tok, scale_a, gain_a, summed(normed_parts))
-    )
-    grad_down_weight = assemble(
-        down_grad_kernel, down_part, [((shard, down_weight.shape[0]), f32)]
-    )[0]
+    att_part, grad_gu_weight, output = tie(spread(packed, "ctx"), grad_gu_weight, output)
+    grad_normed = jnp.concatenate(
+        [summed(att_part[:, i * own : (i + 1) * own]) for i in range(3)], axis=1
+    )
+    grad_tokens = both_halves(grad_middle + norm_back(tok, scale_a, gain_a, grad_normed))
     grad_qkv_weight, grad_out_weight, sums, rest = assemble(
         attention_weight_grad_kernel,
         att_part,
@@ -582,6 +579,10 @@
             ((16, 4 * HEAD), f32),
         ],
     )
+    sums, rest, down_part = tie(sums, rest, down_part)
+    grad_down_weight = assemble(
+        down_grad_kernel, down_part, [((shard, down_weight.shape[0]), f32)]
+    )[0]
     split_at = qcols + HEAD
     own_bias = lax.dynamic_slice(sums, (0, f * (split_at // 8)), (1, split_at // 8))
     own_value = lax.dynamic_slice(sums, (0, split_at + f * (HEAD // 8)), (1, HEAD // 8))

time: 407 us -> 400 us (0.983)
  local copies, waits for them, and re-layouts: 28.6 us -> 41.8 us
  Pallas kernels: 73.2 us -> 61.4 us
  other arithmetic: 46.7 us -> 53.6 us
  matrix products: 6.08 us -> 0 us
  starting transfers between devices: 80.8 us -> 75.7 us
  waiting for transfers between devices: 149 us -> 144 us
    all_to_all x4, waiting for transfers between devices: 32.1 us -> 57.7 us  [spread(): return lax.all_to_all(part, axis, 0, 0, tiled=True)]
    ppermute x2, waiting for transfers between devices: 33.1 us -> 13.5 us  [swap_over_hi(): lax.ppermute(sent, 'fsdp', XH_SWAP)]
    unnamed x78 -> x114, local copies, waits for them, and re-layouts: 4.64 us -> 22.4 us
    ppermute x1, waiting for transfers between devices: 18.5 us -> 5.93 us  [on_device(): output_got = lax.ppermute(output_sent, 'ctx', XL_SWAP)]
    pallas_call x2, Pallas kernels: 20.8 us -> 14.1 us  [feed_forward(): pl.pallas_call(ffn_kernel, grid_spec=pltpu.PrefetchScalarGridSpec(num_sca...]
    dot_general x2 -> x0, matrix products: 6.08 us -> none  [contract(): lax.dot_general(left, right, (((left_dim,), (right_dim,)), ((), ())), pre...]
    pallas_call x1, Pallas kernels: 7.78 us -> 2.64 us  [output_rows(): pl.pallas_call(output_kernel, in_specs=[pl.BlockSpec(memory_space=pltpu.S...]
    pallas_call x1 -> x2, Pallas kernels: 6.23 us -> 11 us  [weight_grad(): return local_call(weight_grad_kernel, outs)(*lefts, *rights)[0]]
  transfers between devices with their start and end apart: 41 -> 40, of which waited for: 17 -> 19; matrix products, arithmetic and copies ran while one was open for 15% -> 16% of each run, Pallas kernels for 16% -> 12%
where the time goes in v5:
time: 400 us; the launch traced here: 392 us
  waiting for transfers between devices  144 us (36%)
  starting transfers between devices  75.7 us (19%)
  Pallas kernels  61.4 us (15%)
  other arithmetic  53.6 us (13%)
  local copies, waits for them, and re-layouts  41.8 us (10%)
  between operations  15.4 us (4%)
    all_to_all x4, waiting for transfers between devices, spread(): return lax.all_to_all(part, axis, 0, 0, tiled=True)  57.7 us
    all_to_all x3, waiting for transfers between devices, gather(): return lax.all_to_all(copies, axis, 0, 0, tiled=True)  28.3 us
    unnamed x114, local copies, waits for them, and re-layouts  22.4 us
    all_to_all x4, starting transfers between devices, spread(): return lax.all_to_all(part, axis, 0, 0, tiled=True)  17.4 us
    pallas_call x1, Pallas kernels, attention_grad(): local_call(attention_grad_kernel, outs, scratch, VMEM_BYTES)  14.8 us
    pallas_call x2, Pallas kernels, feed_forward(): pl.pallas_call(ffn_kernel, grid_spec=pltpu.PrefetchScalarGridSpec(num_sca...  14.1 us
    all_to_all x3, starting transfers between devices, gather(): return lax.all_to_all(copies, axis, 0, 0, tiled=True)  13.9 us
    ppermute x2, waiting for transfers between devices, swap_over_hi(): lax.ppermute(sent, 'fsdp', XH_SWAP)  13.5 us
  transfers between devices with their start and end apart: 40, of which 19 were waited for; matrix products, arithmetic and copies ran while one was open for 16% of the time, Pallas kernels for 12%

profile of v5, /device:TPU:1, one launch (start us, length us, event | category | flops | bytes accessed | tf_op | source)
XLA Modules:
  0.0 391.9 jit_solution(11506730953678978621)
XLA Ops:
  26.1 6.0 %all-to-all-start = ((bf16[8,64,1536]{2,1,0:T(8,128)(2,1)}), bf16[8,64,1536]{2,1,0:T(8,128)(2,1)}, u32[]{:S(2)}, u32[]{:S(2)}) async-start(bf16[8,64,1536]{2,1,0:T(8,128)(2,1)} %broadcast_in_dim.109), calls=%async_computation | async-start | bytes 3145728 | tf_op jit(solution)/shard_map/all_to_all | solution.py:50
  57.8 3.2 collective-permute-start.8
  61.1 4.3 %all-to-all-start.1 = ((bf16[4,2,64,1536]{3,2,1,0:T(8,128)(2,1)}), bf16[4,2,64,1536]{3,2,1,0:T(8,128)(2,1)S(1)}, u32[]{:S(2)}, u32[]{:S(2)}) async-start(bf16[4,2,64,1536]{3,2,1,0:T(8,128)(2,1)} %broadcast_in_dim.122), calls=%async_computation.1 | async-start | bytes 3145728 | tf_op jit(solution)/shard_map/all_to_all | solution.py:58
  68.1 10.2 %shard_map.186 = (bf16[1024,128]{1,0:T(8,128)(2,1)}, bf16[1024,128]{1,0:T(8,128)(2,1)}, bf16[1024,128]{1,0:T(8,128)(2,1)}, bf16[1024,128]{1,0:T(8,128)(2,1)}, f3...) custom-call(bf16[512,1536]{1,0:T(8,128)(2,1)} %bitcast.20.mine, ...), custom_call_target="tpu_custom_call" | custom-call | flops 1000000 | bytes 100000 | tf_op jit(solution)/shard_map/pallas_call | solution.py:323
  78.3 7.1 %collective-permute-done.9 = bf16[192,1920]{1,0:T(8,128)(2,1)} collective-permute-done((bf16[192,1920]{1,0:T(8,128)(2,1)}, bf16[192,1920]{1,0:T(8,128)(2,1)}, u32[]{:S(2)}, u32[]{:S(2)}) %collective-permute-start.9) | collective-permute-done | bytes 737312 | tf_op jit(solution)/shard_map/ppermute | solution.py:483
  87.0 3.2 collective-permute-done.10
  93.3 4.6 %all-to-all-start.2 = ((bf16[8,64,1536]{2,1,0:T(8,128)(2,1)}), bf16[8,64,1536]{2,1,0:T(8,128)(2,1)S(1)}, u32[]{:S(2)}, u32[]{:S(2)}) async-start(bf16[8,64,1536]{2,1,0:T(8,128)(2,1)} %bitcast.83), calls=%async_computation.2 | async-start | bytes 3145728 | tf_op jit(solution)/shard_map/all_to_all | solution.py:54
  98.7 20.0 %all-to-all-done.2 = bf16[8,64,1536]{2,1,0:T(8,128)(2,1)S(1)} async-done(((bf16[8,64,1536]{2,1,0:T(8,128)(2,1)}), bf16[8,64,1536]{2,1,0:T(8,128)(2,1)S(1)}, u32[]{:S(2)}, u32[]{:S(2)}) %all-to-all-start.2) | async-done | bytes 1572896 | tf_op jit(solution)/shard_map/all_to_all | solution.py:54
  121.4 3.6 all-to-all-start.3
  126.6 18.2 %all-to-all-done.3 = bf16[8,64,1536]{2,1,0:T(8,128)(2,1)S(1)} async-done(((bf16[8,64,1536]{2,1,0:T(8,128)(2,1)}), bf16[8,64,1536]{2,1,0:T(8,128)(2,1)S(1)}, u32[]{:S(2)}, u32[]{:S(2)}) %all-to-all-start.3) | async-done | bytes 1572896 | tf_op jit(solution)/shard_map/all_to_all | solution.py:50
  154.1 7.8 %shard_map.188 = (bf16[512,640]{1,0:T(8,128)(2,1)S(1)}, bf16[512,1280]{1,0:T(8,128)(2,1)S(1)}, bf16[512,1536]{1,0:T(8,128)(2,1)S(1)}) custom-call(s32[1]{0:T(128)} %bitcast.23.hi, bf16[512,1536]{1,0:T(8,128)(2,1)} %collective-permute-done.11.rows.left_other, bf16[512,1536]{1,0:T(8,128)(2,1)} %collective-permute-done.12.grad.left_other, ...), custom_call_target="tpu_custom_call" | custom-call | flops 1000000 | bytes 100000 | tf_op jit(solution)/shard_map/pallas_call | solution.py:369
  162.6 6.3 %shard_map.187 = (bf16[512,640]{1,0:T(8,128)(2,1)S(1)}, bf16[512,1280]{1,0:T(8,128)(2,1)S(1)}, bf16[512,1536]{1,0:T(8,128)(2,1)S(1)}) custom-call(s32[1]{0:T(128)} %bitcast.23.hi, bf16[512,1536]{1,0:T(8,128)(2,1)S(1)} %bitcast.75, bf16[512,1536]{1,0:T(8,128)(2,1)S(1)} %bitcast.78, bf16[768,1920]{1,0:T(8,128)(2,1)S(1)} %copy-done.3, ...), custom_call_target="tpu_custom_call" | custom-call | flops 1000000 | bytes 100000 | tf_op jit(solution)/shard_map/pallas_call | solution.py:369
  170.4 5.7 %shard_map.189 = bf16[1536,1280]{1,0:T(8,128)(2,1)S(1)} custom-call(bf16[512,1536]{1,0:T(8,128)(2,1)S(1)} %bitcast.76, bf16[512,1536]{1,0:T(8,128)(2,1)} %collective-permute-done.11.rows.left_other, bf16[512,1280]{1,0:T(8,128)(2,1)S(1)} %get-tuple-element.124.right_mine, bf16[512,1280]{1,0:T(8,128)(2,1)S(1)} %get-tuple-element.125.right_other), custom_call_target="tpu_custom_call" | custom-call | flops 1000000 | bytes 100000 | tf_op jit(solution)/shard_map/pallas_call | solution.py:345
  178.0 4.3 %all-to-all-start.4 = ((bf16[8,64,1536]{2,1,0:T(8,128)(2,1)}), bf16[8,64,1536]{2,1,0:T(8,128)(2,1)}, u32[]{:S(2)}, u32[]{:S(2)}) async-start(bf16[8,64,1536]{2,1,0:T(8,128)(2,1)} %bitcast.82), calls=%async_computation.4 | async-start | bytes 3145728 | tf_op jit(solution)/shard_map/all_to_all | solution.py:54
  186.4 5.3 %shard_map.190 = bf16[1536,640]{1,0:T(8,128)(2,1)} custom-call(bf16[512,1536]{1,0:T(8,128)(2,1)S(1)} %bitcast.79, bf16[512,1536]{1,0:T(8,128)(2,1)} %collective-permute-done.12.grad.left_other, bf16[512,640]{1,0:T(8,128)(2,1)S(1)} %copy-done.18, bf16[512,640]{1,0:T(8,128)(2,1)S(1)} %copy-done.15), custom_call_target="tpu_custom_call" | custom-call | flops 1000000 | bytes 100000 | tf_op jit(solution)/shard_map/pallas_call | solution.py:345
  209.7 4.3 %all-to-all-start.5 = ((bf16[8,64,1536]{2,1,0:T(8,128)(2,1)}), bf16[8,64,1536]{2,1,0:T(8,128)(2,1)}, u32[]{:S(2)}, u32[]{:S(2)}) async-start(bf16[8,64,1536]{2,1,0:T(8,128)(2,1)} %broadcast_in_dim.130), calls=%async_computation.5 | async-start | bytes 3145728 | tf_op jit(solution)/shard_map/all_to_all | solution.py:50
  214.0 4.8 %reduce-scatter.3.cloned.1.call-done = bf16[384,1280]{1,0:T(8,128)(2,1)} async-done(((bf16[1536,1280]{1,0:T(8,128)(2,1)}), bf16[384,1280]{1,0:T(8,128)(2,1)}) %reduce-scatter.3.cloned.1.call-update) | async-done | bytes 983056 | tf_op jit(solution)/shard_map/reduce_scatter | solution.py:82
  225.5 10.1 %all-to-all-done.5 = bf16[8,64,1536]{2,1,0:T(8,128)(2,1)} async-done(((bf16[8,64,1536]{2,1,0:T(8,128)(2,1)}), bf16[8,64,1536]{2,1,0:T(8,128)(2,1)}, u32[]{:S(2)}, u32[]{:S(2)}) %all-to-all-start.5) | async-done | bytes 1572896 | tf_op jit(solution)/shard_map/all_to_all | solution.py:50
  235.5 8.3 %collective-permute-done.14 = bf16[192,1280]{1,0:T(8,128)(2,1)} collective-permute-done((bf16[192,1280]{1,0:T(8,128)(2,1)}, bf16[192,1280]{1,0:T(8,128)(2,1)}, u32[]{:S(2)}, u32[]{:S(2)}) %collective-permute-start.14) | collective-permute-done | bytes 491552 | tf_op jit(solution)/shard_map/ppermute | solution.py:91
  244.5 4.1 %all-to-all-start.6 = ((bf16[4,128,1536]{2,1,0:T(8,128)(2,1)}), bf16[4,128,1536]{2,1,0:T(8,128)(2,1)S(1)}, u32[]{:S(2)}, u32[]{:S(2)}) async-start(bf16[4,128,1536]{2,1,0:T(8,128)(2,1)} %bitcast.81), calls=%async_computation.7 | async-start | bytes 3145728 | tf_op jit(solution)/shard_map/all_to_all | solution.py:58
  251.0 14.8 %shard_map.192 = (bf16[512,1536]{1,0:T(8,128)(2,1)}, bf16[512,1536]{1,0:T(8,128)(2,1)}, bf16[1664,512]{1,0:T(8,128)(2,1)}) custom-call(bf16[512,1536]{1,0:T(8,128)(2,1)} %bitcast.28.branch_mine, bf16[512,1536]{1,0:T(8,128)(2,1)} %collective-permute-done.16.branch_other, bf16[512,1536]{1,0:T(8,128)(2,1)} %bitcast.20.mine, ...), custom_call_target="tpu_custom_call" | custom-call | flops 1000000 | bytes 100000 | tf_op jit(solution)/shard_map/pallas_call | solution.py:338
  265.8 3.3 all-to-all-done.6
  272.5 4.8 %all-to-all-start.7 = ((bf16[8,208,512]{2,1,0:T(8,128)(2,1)}), bf16[8,208,512]{2,1,0:T(8,128)(2,1)S(1)}, u32[]{:S(2)}, u32[]{:S(2)}) async-start(bf16[8,208,512]{2,1,0:T(8,128)(2,1)} %bitcast.85), calls=%async_computation.8 | async-start | bytes 3407872 | tf_op jit(solution)/shard_map/all_to_all | solution.py:54
  277.3 3.4 add_convert_fusion
  284.9 3.2 collective-permute-start.19
  289.8 9.6 %all-to-all-done.7 = bf16[8,208,512]{2,1,0:T(8,128)(2,1)S(1)} async-done(((bf16[8,208,512]{2,1,0:T(8,128)(2,1)}), bf16[8,208,512]{2,1,0:T(8,128)(2,1)S(1)}, u32[]{:S(2)}, u32[]{:S(2)}) %all-to-all-start.7) | async-done | bytes 1703968 | tf_op jit(solution)/shard_map/all_to_all | solution.py:54
  299.5 5.2 %collective-permute-done.19 = bf16[192,640]{1,0:T(8,128)(2,1)} collective-permute-done((bf16[192,640]{1,0:T(8,128)(2,1)}, bf16[192,640]{1,0:T(8,128)(2,1)}, u32[]{:S(2)}, u32[]{:S(2)}) %collective-permute-start.19) | collective-permute-done | bytes 245792 | tf_op jit(solution)/shard_map/ppermute | solution.py:91
  311.3 5.9 %collective-permute-done.21 = bf16[64,1536]{1,0:T(8,128)(2,1)} collective-permute-done((bf16[64,1536]{1,0:T(8,128)(2,1)}, bf16[64,1536]{1,0:T(8,128)(2,1)}, u32[]{:S(2)}, u32[]{:S(2)}) %collective-permute-start.21) | collective-permute-done | bytes 196640 | tf_op jit(solution)/shard_map/ppermute | solution.py:554
  317.2 3.7 all-to-all-start.8
  332.6 5.4 %shard_map.193 = f32[192,2,4480]{2,1,0:T(2,128)} custom-call(bf16[8,192,1280]{2,1,0:T(8,128)(2,1)S(1)} %copy-done.13), custom_call_target="tpu_custom_call" | custom-call | flops 1000000 | bytes 100000 | tf_op jit(solution)/shard_map/pallas_call | solution.py:558
  338.1 25.1 %all-to-all-done.8.parts = bf16[8,400,512]{2,1,0:T(8,128)(2,1)S(1)} async-done(((bf16[8,400,512]{2,1,0:T(8,128)(2,1)}), bf16[8,400,512]{2,1,0:T(8,128)(2,1)S(1)}, u32[]{:S(2)}, u32[]{:S(2)}) %all-to-all-start.8) | async-done | bytes 3276832 | tf_op jit(solution)/shard_map/all_to_all | solution.py:54
  365.4 10.8 %all-gather.13.cloned.1.call-done.parts = bf16[8,192,640]{2,1,0:T(8,128)(2,1)} async-done(((bf16[2,192,640]{2,1,0:T(8,128)(2,1)}), bf16[8,192,640]{2,1,0:T(8,128)(2,1)}) %all-gather.13.cloned.1.call-update) | async-done | bytes 1966096 | tf_op jit(solution)/shard_map/all_gather | solution.py:99
  (286 shorter events, 139.5 us)
Async XLA Ops:
  11.6 36.5 %collective-permute-start = (bf16[208,512]{1,0:T(8,128)(2,1)}, bf16[208,512]{1,0:T(8,128)(2,1)}, u32[]{:S(2)}, u32[]{:S(2)}) collective-permute-start(bf16[208,512]{1,0:T(8,128)(2,1)} %maximum_maximum_fusion), channel_id=1, source_target_pairs={{0,16},{16,32},{32,48},{48,0},{64,80},{80,96},{96,112},{112,64},{1... | collective-permute-start | bytes 638984 | tf_op jit(solution)/shard_map/ppermute | solution.py:72
  13.7 35.5 %collective-permute-start.1 = (bf16[208,512]{1,0:T(8,128)(2,1)}, bf16[208,512]{1,0:T(8,128)(2,1)}, u32[]{:S(2)}, u32[]{:S(2)}) collective-permute-start(bf16[208,512]{1,0:T(8,128)(2,1)} %maximum_maximum_fusion), channel_id=1, source_target_pairs={{0,48},{16,0},{32,16},{48,32},{64,112},{80,64},{96,80},{112,96},{1... | collective-permute-start | bytes 638984 | tf_op jit(solution)/shard_map/ppermute | solution.py:72
  15.2 34.9 %collective-permute-start.2 = (bf16[208,512]{1,0:T(8,128)(2,1)}, bf16[208,512]{1,0:T(8,128)(2,1)}, u32[]{:S(2)}, u32[]{:S(2)}) collective-permute-start(bf16[208,512]{1,0:T(8,128)(2,1)} %maximum_maximum_fusion), channel_id=1, source_target_pairs={{0,32},{16,48},{32,0},{48,16},{64,96},{80,112},{96,64},{112,80},{1... | collective-permute-start | bytes 638984 | tf_op jit(solution)/shard_map/ppermute | solution.py:72
  16.8 28.5 %collective-permute-start.3 = (bf16[208,512]{1,0:T(8,128)(2,1)}, bf16[208,512]{1,0:T(8,128)(2,1)}, u32[]{:S(2)}, u32[]{:S(2)}) collective-permute-start(bf16[208,512]{1,0:T(8,128)(2,1)} %maximum_maximum_fusion), channel_id=1, source_target_pairs={{0,64},{16,80},{32,96},{48,112},{64,0},{80,16},{96,32},{112,48},{1... | collective-permute-start | bytes 638984 | tf_op jit(solution)/shard_map/ppermute | solution.py:452
  21.2 22.8 %collective-permute-start.7 = (bf16[64,1536]{1,0:T(8,128)(2,1)}, bf16[64,1536]{1,0:T(8,128)(2,1)}, u32[]{:S(2)}, u32[]{:S(2)}) collective-permute-start(bf16[64,1536]{1,0:T(8,128)(2,1)} %dynamic-slice_convert_fusion), channel_id=1, source_target_pairs={{0,2},{2,0},{4,6},{6,4},{8,10},{10,8},{12,14},{14,12},{1,3},{3,1},... | collective-permute-start | bytes 589832 | tf_op jit(solution)/shard_map/ppermute | solution.py:478
  26.1 30.3 %all-to-all-start = ((bf16[8,64,1536]{2,1,0:T(8,128)(2,1)}), bf16[8,64,1536]{2,1,0:T(8,128)(2,1)}, u32[]{:S(2)}, u32[]{:S(2)}) async-start(bf16[8,64,1536]{2,1,0:T(8,128)(2,1)} %broadcast_in_dim.109), calls=%async_computation | async-start | bytes 3145728 | tf_op jit(solution)/shard_map/all_to_all | solution.py:50
  32.1 116.3 %all-gather.7.cloned.1.call-start = ((), (), s32[]{:S(2)}) async-start(), calls=%async_computation.11 | async-start | bytes 3686400 | tf_op jit(solution)/shard_map/all_gather | solution.py:78
  45.8 7.9 %collective-permute-start.5 = (bf16[208,512]{1,0:T(8,128)(2,1)}, bf16[208,512]{1,0:T(8,128)(2,1)S(1)}, u32[]{:S(2)}, u32[]{:S(2)}) collective-permute-start(bf16[208,512]{1,0:T(8,128)(2,1)} %collective-permute-done.3), channel_id=1, source_target_pairs={{0,48},{16,0},{32,16},{48,32},{64,112},{80,64},{96,80},{112,96},{1... | collective-permute-start | bytes 638984 | tf_op jit(solution)/shard_map/ppermute | solution.py:72
  48.0 8.4 %collective-permute-start.6 = (bf16[208,512]{1,0:T(8,128)(2,1)}, bf16[208,512]{1,0:T(8,128)(2,1)S(1)}, u32[]{:S(2)}, u32[]{:S(2)}) collective-permute-start(bf16[208,512]{1,0:T(8,128)(2,1)} %collective-permute-done.3), channel_id=1, source_target_pairs={{0,32},{16,48},{32,0},{48,16},{64,96},{80,112},{96,64},{112,80},{1... | collective-permute-start | bytes 638984 | tf_op jit(solution)/shard_map/ppermute | solution.py:72
  57.8 10.2 %collective-permute-start.8 = (bf16[512,1536]{1,0:T(8,128)(2,1)}, bf16[512,1536]{1,0:T(8,128)(2,1)}, u32[]{:S(2)}, u32[]{:S(2)}) collective-permute-start(bf16[512,1536]{1,0:T(8,128)(2,1)} %bitcast.20.mine), channel_id=1, source_target_pairs={{0,1},{1,0},{2,3},{3,2},{4,5},{5,4},{6,7},{7,6},{8,9},{9,8},{10,11... | collective-permute-start | bytes 4718600 | tf_op jit(solution)/shard_map/ppermute | solution.py:104
  61.1 25.0 %all-to-all-start.1 = ((bf16[4,2,64,1536]{3,2,1,0:T(8,128)(2,1)}), bf16[4,2,64,1536]{3,2,1,0:T(8,128)(2,1)S(1)}, u32[]{:S(2)}, u32[]{:S(2)}) async-start(bf16[4,2,64,1536]{3,2,1,0:T(8,128)(2,1)} %broadcast_in_dim.122), calls=%async_computation.1 | async-start | bytes 3145728 | tf_op jit(solution)/shard_map/all_to_all | solution.py:58
  65.4 20.1 %collective-permute-start.9 = (bf16[192,1920]{1,0:T(8,128)(2,1)}, bf16[192,1920]{1,0:T(8,128)(2,1)}, u32[]{:S(2)}, u32[]{:S(2)}) collective-permute-start(bf16[192,1920]{1,0:T(8,128)(2,1)} %pad_maximum_fusion.4), channel_id=1, source_target_pairs={{0,64},{16,80},{32,96},{48,112},{64,0},{80,16},{96,32},{112,48},{1... | collective-permute-start | bytes 2211848 | tf_op jit(solution)/shard_map/ppermute | solution.py:483
  93.3 25.5 %all-to-all-start.2 = ((bf16[8,64,1536]{2,1,0:T(8,128)(2,1)}), bf16[8,64,1536]{2,1,0:T(8,128)(2,1)S(1)}, u32[]{:S(2)}, u32[]{:S(2)}) async-start(bf16[8,64,1536]{2,1,0:T(8,128)(2,1)} %bitcast.83), calls=%async_computation.2 | async-start | bytes 3145728 | tf_op jit(solution)/shard_map/all_to_all | solution.py:54
  97.9 50.5 %all-gather.9.cloned.1.call-start = ((), (), s32[]{:S(2)}) async-start(), calls=%async_computation.12 | async-start | bytes 3686400 | tf_op jit(solution)/shard_map/all_gather | solution.py:78
  121.4 23.4 %all-to-all-start.3 = ((bf16[8,64,1536]{2,1,0:T(8,128)(2,1)}), bf16[8,64,1536]{2,1,0:T(8,128)(2,1)S(1)}, u32[]{:S(2)}, u32[]{:S(2)}) async-start(bf16[8,64,1536]{2,1,0:T(8,128)(2,1)} %broadcast_in_dim.129), calls=%async_computation.3 | async-start | bytes 3145728 | tf_op jit(solution)/shard_map/all_to_all | solution.py:50
  125.0 93.8 %reduce-scatter.3.cloned.1.call-start = ((), (), s32[]{:S(2)}) async-start(), calls=%async_computation.13 | async-start | bytes 4915200 | tf_op jit(solution)/shard_map/reduce_scatter | solution.py:82
  125.1 23.3 %collective-permute-start.12 = (bf16[512,1536]{1,0:T(8,128)(2,1)S(1)}, bf16[512,1536]{1,0:T(8,128)(2,1)}, u32[]{:S(2)}, u32[]{:S(2)}) collective-permute-start(bf16[512,1536]{1,0:T(8,128)(2,1)S(1)} %bitcast.77), channel_id=1, source_target_pairs={{0,1},{1,0},{2,3},{3,2},{4,5},{5,4},{6,7},{7,6},{8,9},{9,8},{10,11... | collective-permute-start | bytes 4718600 | tf_op jit(solution)/shard_map/ppermute | solution.py:104
  178.0 25.7 %all-to-all-start.4 = ((bf16[8,64,1536]{2,1,0:T(8,128)(2,1)}), bf16[8,64,1536]{2,1,0:T(8,128)(2,1)}, u32[]{:S(2)}, u32[]{:S(2)}) async-start(bf16[8,64,1536]{2,1,0:T(8,128)(2,1)} %bitcast.82), calls=%async_computation.4 | async-start | bytes 3145728 | tf_op jit(solution)/shard_map/all_to_all | solution.py:54
  182.3 98.5 %reduce-scatter.5.cloned.1.call-start = ((), (), s32[]{:S(2)}) async-start(), calls=%async_computation.14 | async-start | bytes 2457600 | tf_op jit(solution)/shard_map/reduce_scatter | solution.py:82
  203.7 20.3 %collective-permute-start.15 = (bf16[512,1536]{1,0:T(8,128)(2,1)}, bf16[512,1536]{1,0:T(8,128)(2,1)S(1)}, u32[]{:S(2)}, u32[]{:S(2)}) collective-permute-start(bf16[512,1536]{1,0:T(8,128)(2,1)} %copy-done.23), channel_id=1, source_target_pairs={{0,1},{1,0},{2,3},{3,2},{4,5},{5,4},{6,7},{7,6},{8,9},{9,8},{10,11... | collective-permute-start | bytes 4718600 | tf_op jit(solution)/shard_map/ppermute | solution.py:108
  209.7 25.8 %all-to-all-start.5 = ((bf16[8,64,1536]{2,1,0:T(8,128)(2,1)}), bf16[8,64,1536]{2,1,0:T(8,128)(2,1)}, u32[]{:S(2)}, u32[]{:S(2)}) async-start(bf16[8,64,1536]{2,1,0:T(8,128)(2,1)} %broadcast_in_dim.130), calls=%async_computation.5 | async-start | bytes 3145728 | tf_op jit(solution)/shard_map/all_to_all | solution.py:50
  221.0 22.8 %collective-permute-start.14 = (bf16[192,1280]{1,0:T(8,128)(2,1)}, bf16[192,1280]{1,0:T(8,128)(2,1)}, u32[]{:S(2)}, u32[]{:S(2)}) collective-permute-start(bf16[192,1280]{1,0:T(8,128)(2,1)} %get-tuple-element.194), channel_id=1, source_target_pairs={{0,64},{16,80},{32,96},{48,112},{64,0},{80,16},{96,32},{112,48},{1... | collective-permute-start | bytes 1474568 | tf_op jit(solution)/shard_map/ppermute | solution.py:91
  243.9 7.1 %collective-permute-start.16 = (bf16[512,1536]{1,0:T(8,128)(2,1)}, bf16[512,1536]{1,0:T(8,128)(2,1)}, u32[]{:S(2)}, u32[]{:S(2)}) collective-permute-start(bf16[512,1536]{1,0:T(8,128)(2,1)} %bitcast.28.branch_mine), channel_id=1, source_target_pairs={{0,1},{1,0},{2,3},{3,2},{4,5},{5,4},{6,7},{7,6},{8,9},{9,8},{10,11... | collective-permute-start | bytes 4718600 | tf_op jit(solution)/shard_map/ppermute | solution.py:104
  244.5 24.6 %all-to-all-start.6 = ((bf16[4,128,1536]{2,1,0:T(8,128)(2,1)}), bf16[4,128,1536]{2,1,0:T(8,128)(2,1)S(1)}, u32[]{:S(2)}, u32[]{:S(2)}) async-start(bf16[4,128,1536]{2,1,0:T(8,128)(2,1)} %bitcast.81), calls=%async_computation.7 | async-start | bytes 3145728 | tf_op jit(solution)/shard_map/all_to_all | solution.py:58
  248.6 82.0 %all-gather.11.cloned.1.call-start = ((), (), s32[]{:S(2)}) async-start(), calls=%async_computation.15 | async-start | bytes 4915200 | tf_op jit(solution)/shard_map/all_gather | solution.py:99
  249.7 16.1 %collective-permute-start.17 = (bf16[192,1280]{1,0:T(8,128)(2,1)S(1)}, bf16[192,1280]{1,0:T(8,128)(2,1)S(1)}, u32[]{:S(2)}, u32[]{:S(2)}) collective-permute-start(bf16[192,1280]{1,0:T(8,128)(2,1)S(1)} %add_convert_fusion.4), channel_id=1, source_target_pairs={{0,2},{2,0},{4,6},{6,4},{8,10},{10,8},{12,14},{14,12},{1,3},{3,1},... | collective-permute-start | bytes 1474568 | tf_op jit(solution)/shard_map/ppermute | solution.py:526
  272.5 27.0 %all-to-all-start.7 = ((bf16[8,208,512]{2,1,0:T(8,128)(2,1)}), bf16[8,208,512]{2,1,0:T(8,128)(2,1)S(1)}, u32[]{:S(2)}, u32[]{:S(2)}) async-start(bf16[8,208,512]{2,1,0:T(8,128)(2,1)} %bitcast.85), calls=%async_computation.8 | async-start | bytes 3407872 | tf_op jit(solution)/shard_map/all_to_all | solution.py:54
  284.9 19.8 %collective-permute-start.19 = (bf16[192,640]{1,0:T(8,128)(2,1)}, bf16[192,640]{1,0:T(8,128)(2,1)}, u32[]{:S(2)}, u32[]{:S(2)}) collective-permute-start(bf16[192,640]{1,0:T(8,128)(2,1)} %get-tuple-element.202), channel_id=1, source_target_pairs={{0,64},{16,80},{32,96},{48,112},{64,0},{80,16},{96,32},{112,48},{1... | collective-permute-start | bytes 737288 | tf_op jit(solution)/shard_map/ppermute | solution.py:91
  306.0 11.3 %collective-permute-start.20 = (bf16[192,640]{1,0:T(8,128)(2,1)S(1)}, bf16[192,640]{1,0:T(8,128)(2,1)}, u32[]{:S(2)}, u32[]{:S(2)}) collective-permute-start(bf16[192,640]{1,0:T(8,128)(2,1)S(1)} %add_convert_fusion.5), channel_id=1, source_target_pairs={{0,2},{2,0},{4,6},{6,4},{8,10},{10,8},{12,14},{14,12},{1,3},{3,1},... | collective-permute-start | bytes 737288 | tf_op jit(solution)/shard_map/ppermute | solution.py:553
  307.8 9.4 %collective-permute-start.21 = (bf16[64,1536]{1,0:T(8,128)(2,1)}, bf16[64,1536]{1,0:T(8,128)(2,1)}, u32[]{:S(2)}, u32[]{:S(2)}) collective-permute-start(bf16[64,1536]{1,0:T(8,128)(2,1)} %select_convert_fusion), channel_id=1, source_target_pairs={{0,2},{2,0},{4,6},{6,4},{8,10},{10,8},{12,14},{14,12},{1,3},{3,1},... | collective-permute-start | bytes 589832 | tf_op jit(solution)/shard_map/ppermute | solution.py:554
  317.2 46.0 %all-to-all-start.8 = ((bf16[8,400,512]{2,1,0:T(8,128)(2,1)}), bf16[8,400,512]{2,1,0:T(8,128)(2,1)S(1)}, u32[]{:S(2)}, u32[]{:S(2)}) async-start(bf16[8,400,512]{2,1,0:T(8,128)(2,1)} %pad_maximum_fusion), calls=%async_computation.10 | async-start | bytes 6553600 | tf_op jit(solution)/shard_map/all_to_all | solution.py:54
  320.9 55.3 %all-gather.13.cloned.1.call-start = ((), (), s32[]{:S(2)}) async-start(), calls=%async_computation.16 | async-start | bytes 2457600 | tf_op jit(solution)/shard_map/all_gather | solution.py:99
  (64 other events, 422.3 us)
Sparse Core Ops, SparseCore 0:
  61.2 36.4 all-gather.6
  100.4 37.1 all-gather.8
  178.1 40.6 reduce-scatter.2
  221.7 28.3 reduce-scatter.4
  271.4 45.6 all-gather.10
  323.6 52.4 all-gather.12

commit v6 on v5

--- a/solution.py
+++ b/solution.py
@@ -516,10 +516,13 @@
     down_sums = reduce_along_y(down_blocks)
 
     grad_middle = cot + norm_back(middle, scale_m, gain_m, summed(normed2_parts))
+    branch_low = grad_middle.astype(bf16)
+    branch_pair = ordered(branch_low, lax.ppermute(branch_low, "ctx", XL_SWAP), c % 2)
+    branch_spread = spread_along_z(jnp.broadcast_to(branch_pair[None], (4,) + branch_pair.shape))
     output_parts = pair_sums(*output_raw)
     gu_kept, gu_got = swap_over_hi(gu_sums)
     branch_mine, gu_kept, gu_got, output_parts = tie(
-        gather(grad_middle.astype(bf16), "ctx"), gu_kept, gu_got, output_parts
+        branch_spread, gu_kept, gu_got, output_parts
     )
     output_parts = spread_along_z(output_parts.reshape(4, 2 * own, width))
     gu_share = added(gu_kept, gu_got)

time: 400 us -> 396 us (0.990)
    all_to_all x2 -> x3, waiting for transfers between devices: 3.91 us -> 20.1 us  [spread_along_z(): lax.all_to_all(part, 'ctx', 0, 0, tiled=True, axis_index_groups=Z_GROUPS)]
    all_to_all x3 -> x2, waiting for transfers between devices: 28.3 us -> 18.2 us  [gather(): return lax.all_to_all(copies, axis, 0, 0, tiled=True)]
    ppermute x2, waiting for transfers between devices: 13.5 us -> 5.22 us  [swap_over_hi(): lax.ppermute(sent, 'fsdp', XH_SWAP)]
    ppermute x0 -> x1, waiting for transfers between devices: none -> 6.01 us  [on_device(): lax.ppermute(branch_low, 'ctx', XL_SWAP)]
    reduce_scatter x2, waiting for transfers between devices: 4.82 us -> 0.02 us  [reduce_along_y(): lax.psum_scatter(part, 'fsdp', scatter_dimension=0, axis_index_groups=Y_G...]
    all_to_all x3 -> x2, starting transfers between devices: 13.9 us -> 9.62 us  [gather(): return lax.all_to_all(copies, axis, 0, 0, tiled=True)]
    all_to_all x2 -> x3, starting transfers between devices: 8.34 us -> 12.2 us  [spread_along_z(): lax.all_to_all(part, 'ctx', 0, 0, tiled=True, axis_index_groups=Z_GROUPS)]
    unnamed x114 -> x116, local copies, waits for them, and re-layouts: 22.4 us -> 21.6 us
  transfers between devices with their start and end apart: 40 -> 41, of which waited for: 19 -> 18; matrix products, arithmetic and copies ran while one was open for 16% -> 17% of each run, Pallas kernels for 12% -> 12%
where the time goes in v6:
time: 396 us; the launch traced here: 388 us
  waiting for transfers between devices  142 us (36%)
  starting transfers between devices  72.7 us (18%)
  Pallas kernels  61.4 us (16%)
  other arithmetic  54.9 us (14%)
  local copies, waits for them, and re-layouts  41.1 us (10%)
  between operations  15.5 us (4%)
    all_to_all x4, waiting for transfers between devices, spread(): return lax.all_to_all(part, axis, 0, 0, tiled=True)  56.6 us
    unnamed x116, local copies, waits for them, and re-layouts  21.6 us
    all_to_all x3, waiting for transfers between devices, spread_along_z(): lax.all_to_all(part, 'ctx', 0, 0, tiled=True, axis_index_groups=Z_GROUPS)  20.1 us
    all_to_all x2, waiting for transfers between devices, gather(): return lax.all_to_all(copies, axis, 0, 0, tiled=True)  18.2 us
    all_to_all x4, starting transfers between devices, spread(): return lax.all_to_all(part, axis, 0, 0, tiled=True)  16.4 us
    pallas_call x1, Pallas kernels, attention_grad(): local_call(attention_grad_kernel, outs, scratch, VMEM_BYTES)  14.9 us
    pallas_call x2, Pallas kernels, feed_forward(): pl.pallas_call(ffn_kernel, grid_spec=pltpu.PrefetchScalarGridSpec(num_sca...  14.1 us
    all_to_all x3, starting transfers between devices, spread_along_z(): lax.all_to_all(part, 'ctx', 0, 0, tiled=True, axis_index_groups=Z_GROUPS)  12.2 us
  transfers between devices with their start and end apart: 41, of which 18 were waited for; matrix products, arithmetic and copies ran while one was open for 17% of the time, Pallas kernels for 12%

profile of v6, /device:TPU:1, one launch (start us, length us, event | category | flops | bytes accessed | tf_op | source)
XLA Modules:
  0.0 387.9 jit_solution(2589690919946509121)
XLA Ops:
  26.1 6.0 %all-to-all-start = ((bf16[8,64,1536]{2,1,0:T(8,128)(2,1)}), bf16[8,64,1536]{2,1,0:T(8,128)(2,1)}, u32[]{:S(2)}, u32[]{:S(2)}) async-start(bf16[8,64,1536]{2,1,0:T(8,128)(2,1)} %broadcast_in_dim.109), calls=%async_computation | async-start | bytes 3145728 | tf_op jit(solution)/shard_map/all_to_all | solution.py:50
  57.9 3.2 collective-permute-start.8
  61.1 4.3 %all-to-all-start.1 = ((bf16[4,2,64,1536]{3,2,1,0:T(8,128)(2,1)}), bf16[4,2,64,1536]{3,2,1,0:T(8,128)(2,1)S(1)}, u32[]{:S(2)}, u32[]{:S(2)}) async-start(bf16[4,2,64,1536]{3,2,1,0:T(8,128)(2,1)} %broadcast_in_dim.122), calls=%async_computation.1 | async-start | bytes 3145728 | tf_op jit(solution)/shard_map/all_to_all | solution.py:58
  68.1 10.2 %shard_map.186 = (bf16[1024,128]{1,0:T(8,128)(2,1)}, bf16[1024,128]{1,0:T(8,128)(2,1)}, bf16[1024,128]{1,0:T(8,128)(2,1)}, bf16[1024,128]{1,0:T(8,128)(2,1)}, f3...) custom-call(bf16[512,1536]{1,0:T(8,128)(2,1)} %bitcast.20.mine, ...), custom_call_target="tpu_custom_call" | custom-call | flops 1000000 | bytes 100000 | tf_op jit(solution)/shard_map/pallas_call | solution.py:323
  78.4 7.1 %collective-permute-done.9 = bf16[192,1920]{1,0:T(8,128)(2,1)} collective-permute-done((bf16[192,1920]{1,0:T(8,128)(2,1)}, bf16[192,1920]{1,0:T(8,128)(2,1)}, u32[]{:S(2)}, u32[]{:S(2)}) %collective-permute-start.9) | collective-permute-done | bytes 737312 | tf_op jit(solution)/shard_map/ppermute | solution.py:483
  87.1 3.2 collective-permute-done.10
  90.4 3.0 add_convert_fusion.3
  93.3 4.6 %all-to-all-start.2 = ((bf16[8,64,1536]{2,1,0:T(8,128)(2,1)}), bf16[8,64,1536]{2,1,0:T(8,128)(2,1)S(1)}, u32[]{:S(2)}, u32[]{:S(2)}) async-start(bf16[8,64,1536]{2,1,0:T(8,128)(2,1)} %bitcast.87), calls=%async_computation.2 | async-start | bytes 3145728 | tf_op jit(solution)/shard_map/all_to_all | solution.py:54
  98.8 20.0 %all-to-all-done.2 = bf16[8,64,1536]{2,1,0:T(8,128)(2,1)S(1)} async-done(((bf16[8,64,1536]{2,1,0:T(8,128)(2,1)}), bf16[8,64,1536]{2,1,0:T(8,128)(2,1)S(1)}, u32[]{:S(2)}, u32[]{:S(2)}) %all-to-all-start.2) | async-done | bytes 1572896 | tf_op jit(solution)/shard_map/all_to_all | solution.py:54
  121.5 3.6 all-to-all-start.3
  126.7 18.2 %all-to-all-done.3 = bf16[8,64,1536]{2,1,0:T(8,128)(2,1)S(1)} async-done(((bf16[8,64,1536]{2,1,0:T(8,128)(2,1)}), bf16[8,64,1536]{2,1,0:T(8,128)(2,1)S(1)}, u32[]{:S(2)}, u32[]{:S(2)}) %all-to-all-start.3) | async-done | bytes 1572896 | tf_op jit(solution)/shard_map/all_to_all | solution.py:50
  154.2 7.8 %shard_map.188 = (bf16[512,640]{1,0:T(8,128)(2,1)S(1)}, bf16[512,1280]{1,0:T(8,128)(2,1)S(1)}, bf16[512,1536]{1,0:T(8,128)(2,1)S(1)}) custom-call(s32[1]{0:T(128)} %bitcast.23.hi, bf16[512,1536]{1,0:T(8,128)(2,1)} %collective-permute-done.11.rows.left_other, bf16[512,1536]{1,0:T(8,128)(2,1)} %collective-permute-done.12.grad.left_other, ...), custom_call_target="tpu_custom_call" | custom-call | flops 1000000 | bytes 100000 | tf_op jit(solution)/shard_map/pallas_call | solution.py:369
  162.6 6.3 %shard_map.187 = (bf16[512,640]{1,0:T(8,128)(2,1)S(1)}, bf16[512,1280]{1,0:T(8,128)(2,1)S(1)}, bf16[512,1536]{1,0:T(8,128)(2,1)S(1)}) custom-call(s32[1]{0:T(128)} %bitcast.23.hi, bf16[512,1536]{1,0:T(8,128)(2,1)S(1)} %bitcast.79, bf16[512,1536]{1,0:T(8,128)(2,1)S(1)} %bitcast.82, bf16[768,1920]{1,0:T(8,128)(2,1)S(1)} %copy-done.3, ...), custom_call_target="tpu_custom_call" | custom-call | flops 1000000 | bytes 100000 | tf_op jit(solution)/shard_map/pallas_call | solution.py:369
  170.4 5.7 %shard_map.189 = bf16[1536,1280]{1,0:T(8,128)(2,1)S(1)} custom-call(bf16[512,1536]{1,0:T(8,128)(2,1)S(1)} %bitcast.80, bf16[512,1536]{1,0:T(8,128)(2,1)} %collective-permute-done.11.rows.left_other, bf16[512,1280]{1,0:T(8,128)(2,1)S(1)} %get-tuple-element.124.right_mine, bf16[512,1280]{1,0:T(8,128)(2,1)S(1)} %get-tuple-element.125.right_other), custom_call_target="tpu_custom_call" | custom-call | flops 1000000 | bytes 100000 | tf_op jit(solution)/shard_map/pallas_call | solution.py:345
  178.1 4.3 %all-to-all-start.4 = ((bf16[8,64,1536]{2,1,0:T(8,128)(2,1)}), bf16[8,64,1536]{2,1,0:T(8,128)(2,1)}, u32[]{:S(2)}, u32[]{:S(2)}) async-start(bf16[8,64,1536]{2,1,0:T(8,128)(2,1)} %bitcast.86), calls=%async_computation.4 | async-start | bytes 3145728 | tf_op jit(solution)/shard_map/all_to_all | solution.py:54
  186.5 5.3 %shard_map.190 = bf16[1536,640]{1,0:T(8,128)(2,1)} custom-call(bf16[512,1536]{1,0:T(8,128)(2,1)S(1)} %bitcast.83, bf16[512,1536]{1,0:T(8,128)(2,1)} %collective-permute-done.12.grad.left_other, bf16[512,640]{1,0:T(8,128)(2,1)S(1)} %copy-done.18, bf16[512,640]{1,0:T(8,128)(2,1)S(1)} %copy-done.15), custom_call_target="tpu_custom_call" | custom-call | flops 1000000 | bytes 100000 | tf_op jit(solution)/shard_map/pallas_call | solution.py:345
  208.2 6.0 %collective-permute-done.14 = bf16[64,1536]{1,0:T(8,128)(2,1)S(1)} collective-permute-done((bf16[64,1536]{1,0:T(8,128)(2,1)S(1)}, bf16[64,1536]{1,0:T(8,128)(2,1)S(1)}, u32[]{:S(2)}, u32[]{:S(2)}) %collective-permute-start.14) | collective-permute-done | bytes 196640 | tf_op jit(solution)/shard_map/ppermute | solution.py:520
  216.5 4.4 %all-to-all-start.5 = ((bf16[4,2,64,1536]{3,2,1,0:T(8,128)(2,1)}), bf16[4,2,64,1536]{3,2,1,0:T(8,128)(2,1)}, u32[]{:S(2)}, u32[]{:S(2)}) async-start(bf16[4,2,64,1536]{3,2,1,0:T(8,128)(2,1)} %broadcast_in_dim.130), calls=%async_computation.5 | async-start | bytes 3145728 | tf_op jit(solution)/shard_map/all_to_all | solution.py:58
  225.9 15.3 %all-to-all-done.5 = bf16[4,2,64,1536]{3,2,1,0:T(8,128)(2,1)} async-done(((bf16[4,2,64,1536]{3,2,1,0:T(8,128)(2,1)}), bf16[4,2,64,1536]{3,2,1,0:T(8,128)(2,1)}, u32[]{:S(2)}, u32[]{:S(2)}) %all-to-all-start.5) | async-done | bytes 1572896 | tf_op jit(solution)/shard_map/all_to_all | solution.py:58
  242.6 3.6 all-to-all-start.6
  248.0 14.9 %shard_map.192 = (bf16[512,1536]{1,0:T(8,128)(2,1)}, bf16[512,1536]{1,0:T(8,128)(2,1)}, bf16[1664,512]{1,0:T(8,128)(2,1)}) custom-call(bf16[512,1536]{1,0:T(8,128)(2,1)} %bitcast.30.branch_mine, bf16[512,1536]{1,0:T(8,128)(2,1)} %collective-permute-done.17.branch_other, bf16[512,1536]{1,0:T(8,128)(2,1)} %bitcast.20.mine, ...), custom_call_target="tpu_custom_call" | custom-call | flops 1000000 | bytes 100000 | tf_op jit(solution)/shard_map/pallas_call | solution.py:338
  262.9 4.2 %all-to-all-done.6 = bf16[4,128,1536]{2,1,0:T(8,128)(2,1)S(1)} async-done(((bf16[4,128,1536]{2,1,0:T(8,128)(2,1)}), bf16[4,128,1536]{2,1,0:T(8,128)(2,1)S(1)}, u32[]{:S(2)}, u32[]{:S(2)}) %all-to-all-start.6) | async-done | bytes 1572896 | tf_op jit(solution)/shard_map/all_to_all | solution.py:58
  270.1 3.8 all-to-all-start.7
  273.9 3.7 add_convert_fusion
  281.7 3.2 collective-permute-start.20
  286.6 9.4 %all-to-all-done.7 = bf16[8,208,512]{2,1,0:T(8,128)(2,1)S(1)} async-done(((bf16[8,208,512]{2,1,0:T(8,128)(2,1)}), bf16[8,208,512]{2,1,0:T(8,128)(2,1)S(1)}, u32[]{:S(2)}, u32[]{:S(2)}) %all-to-all-start.7) | async-done | bytes 1703968 | tf_op jit(solution)/shard_map/all_to_all | solution.py:54
  296.0 5.2 %collective-permute-done.20 = bf16[192,640]{1,0:T(8,128)(2,1)} collective-permute-done((bf16[192,640]{1,0:T(8,128)(2,1)}, bf16[192,640]{1,0:T(8,128)(2,1)}, u32[]{:S(2)}, u32[]{:S(2)}) %collective-permute-start.20) | collective-permute-done | bytes 245792 | tf_op jit(solution)/shard_map/ppermute | solution.py:91
  307.5 5.7 %collective-permute-done.22 = bf16[64,1536]{1,0:T(8,128)(2,1)} collective-permute-done((bf16[64,1536]{1,0:T(8,128)(2,1)}, bf16[64,1536]{1,0:T(8,128)(2,1)}, u32[]{:S(2)}, u32[]{:S(2)}) %collective-permute-start.22) | collective-permute-done | bytes 196640 | tf_op jit(solution)/shard_map/ppermute | solution.py:557
  313.2 3.7 all-to-all-start.8
  328.9 5.4 %shard_map.193 = f32[192,2,4480]{2,1,0:T(2,128)} custom-call(bf16[8,192,1280]{2,1,0:T(8,128)(2,1)S(1)} %copy-done.13), custom_call_target="tpu_custom_call" | custom-call | flops 1000000 | bytes 100000 | tf_op jit(solution)/shard_map/pallas_call | solution.py:561
  334.4 24.3 %all-to-all-done.8.parts = bf16[8,400,512]{2,1,0:T(8,128)(2,1)S(1)} async-done(((bf16[8,400,512]{2,1,0:T(8,128)(2,1)}), bf16[8,400,512]{2,1,0:T(8,128)(2,1)S(1)}, u32[]{:S(2)}, u32[]{:S(2)}) %all-to-all-start.8) | async-done | bytes 3276832 | tf_op jit(solution)/shard_map/all_to_all | solution.py:54
  360.9 11.3 %all-gather.13.cloned.1.call-done.parts = bf16[8,192,640]{2,1,0:T(8,128)(2,1)} async-done(((bf16[2,192,640]{2,1,0:T(8,128)(2,1)}), bf16[8,192,640]{2,1,0:T(8,128)(2,1)}) %all-gather.13.cloned.1.call-update) | async-done | bytes 1966096 | tf_op jit(solution)/shard_map/all_gather | solution.py:99
  (292 shorter events, 135.4 us)
Async XLA Ops:
  11.6 36.5 %collective-permute-start = (bf16[208,512]{1,0:T(8,128)(2,1)}, bf16[208,512]{1,0:T(8,128)(2,1)}, u32[]{:S(2)}, u32[]{:S(2)}) collective-permute-start(bf16[208,512]{1,0:T(8,128)(2,1)} %maximum_maximum_fusion), channel_id=1, source_target_pairs={{0,16},{16,32},{32,48},{48,0},{64,80},{80,96},{96,112},{112,64},{1... | collective-permute-start | bytes 638984 | tf_op jit(solution)/shard_map/ppermute | solution.py:72
  13.7 35.5 %collective-permute-start.1 = (bf16[208,512]{1,0:T(8,128)(2,1)}, bf16[208,512]{1,0:T(8,128)(2,1)}, u32[]{:S(2)}, u32[]{:S(2)}) collective-permute-start(bf16[208,512]{1,0:T(8,128)(2,1)} %maximum_maximum_fusion), channel_id=1, source_target_pairs={{0,48},{16,0},{32,16},{48,32},{64,112},{80,64},{96,80},{112,96},{1... | collective-permute-start | bytes 638984 | tf_op jit(solution)/shard_map/ppermute | solution.py:72
  15.2 35.0 %collective-permute-start.2 = (bf16[208,512]{1,0:T(8,128)(2,1)}, bf16[208,512]{1,0:T(8,128)(2,1)}, u32[]{:S(2)}, u32[]{:S(2)}) collective-permute-start(bf16[208,512]{1,0:T(8,128)(2,1)} %maximum_maximum_fusion), channel_id=1, source_target_pairs={{0,32},{16,48},{32,0},{48,16},{64,96},{80,112},{96,64},{112,80},{1... | collective-permute-start | bytes 638984 | tf_op jit(solution)/shard_map/ppermute | solution.py:72
  16.8 28.5 %collective-permute-start.3 = (bf16[208,512]{1,0:T(8,128)(2,1)}, bf16[208,512]{1,0:T(8,128)(2,1)}, u32[]{:S(2)}, u32[]{:S(2)}) collective-permute-start(bf16[208,512]{1,0:T(8,128)(2,1)} %maximum_maximum_fusion), channel_id=1, source_target_pairs={{0,64},{16,80},{32,96},{48,112},{64,0},{80,16},{96,32},{112,48},{1... | collective-permute-start | bytes 638984 | tf_op jit(solution)/shard_map/ppermute | solution.py:452
  21.2 22.9 %collective-permute-start.7 = (bf16[64,1536]{1,0:T(8,128)(2,1)}, bf16[64,1536]{1,0:T(8,128)(2,1)}, u32[]{:S(2)}, u32[]{:S(2)}) collective-permute-start(bf16[64,1536]{1,0:T(8,128)(2,1)} %dynamic-slice_convert_fusion), channel_id=1, source_target_pairs={{0,2},{2,0},{4,6},{6,4},{8,10},{10,8},{12,14},{14,12},{1,3},{3,1},... | collective-permute-start | bytes 589832 | tf_op jit(solution)/shard_map/ppermute | solution.py:478
  26.1 30.4 %all-to-all-start = ((bf16[8,64,1536]{2,1,0:T(8,128)(2,1)}), bf16[8,64,1536]{2,1,0:T(8,128)(2,1)}, u32[]{:S(2)}, u32[]{:S(2)}) async-start(bf16[8,64,1536]{2,1,0:T(8,128)(2,1)} %broadcast_in_dim.109), calls=%async_computation | async-start | bytes 3145728 | tf_op jit(solution)/shard_map/all_to_all | solution.py:50
  32.1 116.4 %all-gather.7.cloned.1.call-start = ((), (), s32[]{:S(2)}) async-start(), calls=%async_computation.11 | async-start | bytes 3686400 | tf_op jit(solution)/shard_map/all_gather | solution.py:78
  45.8 7.9 %collective-permute-start.5 = (bf16[208,512]{1,0:T(8,128)(2,1)}, bf16[208,512]{1,0:T(8,128)(2,1)S(1)}, u32[]{:S(2)}, u32[]{:S(2)}) collective-permute-start(bf16[208,512]{1,0:T(8,128)(2,1)} %collective-permute-done.3), channel_id=1, source_target_pairs={{0,48},{16,0},{32,16},{48,32},{64,112},{80,64},{96,80},{112,96},{1... | collective-permute-start | bytes 638984 | tf_op jit(solution)/shard_map/ppermute | solution.py:72
  48.1 8.4 %collective-permute-start.6 = (bf16[208,512]{1,0:T(8,128)(2,1)}, bf16[208,512]{1,0:T(8,128)(2,1)S(1)}, u32[]{:S(2)}, u32[]{:S(2)}) collective-permute-start(bf16[208,512]{1,0:T(8,128)(2,1)} %collective-permute-done.3), channel_id=1, source_target_pairs={{0,32},{16,48},{32,0},{48,16},{64,96},{80,112},{96,64},{112,80},{1... | collective-permute-start | bytes 638984 | tf_op jit(solution)/shard_map/ppermute | solution.py:72
  57.9 10.2 %collective-permute-start.8 = (bf16[512,1536]{1,0:T(8,128)(2,1)}, bf16[512,1536]{1,0:T(8,128)(2,1)}, u32[]{:S(2)}, u32[]{:S(2)}) collective-permute-start(bf16[512,1536]{1,0:T(8,128)(2,1)} %bitcast.20.mine), channel_id=1, source_target_pairs={{0,1},{1,0},{2,3},{3,2},{4,5},{5,4},{6,7},{7,6},{8,9},{9,8},{10,11... | collective-permute-start | bytes 4718600 | tf_op jit(solution)/shard_map/ppermute | solution.py:104
  61.1 25.0 %all-to-all-start.1 = ((bf16[4,2,64,1536]{3,2,1,0:T(8,128)(2,1)}), bf16[4,2,64,1536]{3,2,1,0:T(8,128)(2,1)S(1)}, u32[]{:S(2)}, u32[]{:S(2)}) async-start(bf16[4,2,64,1536]{3,2,1,0:T(8,128)(2,1)} %broadcast_in_dim.122), calls=%async_computation.1 | async-start | bytes 3145728 | tf_op jit(solution)/shard_map/all_to_all | solution.py:58
  65.4 20.1 %collective-permute-start.9 = (bf16[192,1920]{1,0:T(8,128)(2,1)}, bf16[192,1920]{1,0:T(8,128)(2,1)}, u32[]{:S(2)}, u32[]{:S(2)}) collective-permute-start(bf16[192,1920]{1,0:T(8,128)(2,1)} %pad_maximum_fusion.4), channel_id=1, source_target_pairs={{0,64},{16,80},{32,96},{48,112},{64,0},{80,16},{96,32},{112,48},{1... | collective-permute-start | bytes 2211848 | tf_op jit(solution)/shard_map/ppermute | solution.py:483
  93.3 25.5 %all-to-all-start.2 = ((bf16[8,64,1536]{2,1,0:T(8,128)(2,1)}), bf16[8,64,1536]{2,1,0:T(8,128)(2,1)S(1)}, u32[]{:S(2)}, u32[]{:S(2)}) async-start(bf16[8,64,1536]{2,1,0:T(8,128)(2,1)} %bitcast.87), calls=%async_computation.2 | async-start | bytes 3145728 | tf_op jit(solution)/shard_map/all_to_all | solution.py:54
  98.0 50.5 %all-gather.9.cloned.1.call-start = ((), (), s32[]{:S(2)}) async-start(), calls=%async_computation.12 | async-start | bytes 3686400 | tf_op jit(solution)/shard_map/all_gather | solution.py:78
  121.5 23.4 %all-to-all-start.3 = ((bf16[8,64,1536]{2,1,0:T(8,128)(2,1)}), bf16[8,64,1536]{2,1,0:T(8,128)(2,1)S(1)}, u32[]{:S(2)}, u32[]{:S(2)}) async-start(bf16[8,64,1536]{2,1,0:T(8,128)(2,1)} %broadcast_in_dim.129), calls=%async_computation.3 | async-start | bytes 3145728 | tf_op jit(solution)/shard_map/all_to_all | solution.py:50
  125.1 95.9 %reduce-scatter.3.cloned.1.call-start = ((), (), s32[]{:S(2)}) async-start(), calls=%async_computation.13 | async-start | bytes 4915200 | tf_op jit(solution)/shard_map/reduce_scatter | solution.py:82
  125.1 23.3 %collective-permute-start.12 = (bf16[512,1536]{1,0:T(8,128)(2,1)S(1)}, bf16[512,1536]{1,0:T(8,128)(2,1)}, u32[]{:S(2)}, u32[]{:S(2)}) collective-permute-start(bf16[512,1536]{1,0:T(8,128)(2,1)S(1)} %bitcast.81), channel_id=1, source_target_pairs={{0,1},{1,0},{2,3},{3,2},{4,5},{5,4},{6,7},{7,6},{8,9},{9,8},{10,11... | collective-permute-start | bytes 4718600 | tf_op jit(solution)/shard_map/ppermute | solution.py:104
  162.0 6.9 %collective-permute-start.13 = (bf16[512,1536]{1,0:T(8,128)(2,1)S(1)}, bf16[512,1536]{1,0:T(8,128)(2,1)S(1)}, u32[]{:S(2)}, u32[]{:S(2)}) collective-permute-start(bf16[512,1536]{1,0:T(8,128)(2,1)S(1)} %get-tuple-element.116), channel_id=1, source_target_pairs={{0,1},{1,0},{2,3},{3,2},{4,5},{5,4},{6,7},{7,6},{8,9},{9,8},{10,11... | collective-permute-start | bytes 4718600 | tf_op jit(solution)/shard_map/ppermute | solution.py:108
  178.1 25.7 %all-to-all-start.4 = ((bf16[8,64,1536]{2,1,0:T(8,128)(2,1)}), bf16[8,64,1536]{2,1,0:T(8,128)(2,1)}, u32[]{:S(2)}, u32[]{:S(2)}) async-start(bf16[8,64,1536]{2,1,0:T(8,128)(2,1)} %bitcast.86), calls=%async_computation.4 | async-start | bytes 3145728 | tf_op jit(solution)/shard_map/all_to_all | solution.py:54
  182.4 95.2 %reduce-scatter.5.cloned.1.call-start = ((), (), s32[]{:S(2)}) async-start(), calls=%async_computation.14 | async-start | bytes 2457600 | tf_op jit(solution)/shard_map/reduce_scatter | solution.py:82
  203.8 20.6 %collective-permute-start.16 = (bf16[512,1536]{1,0:T(8,128)(2,1)}, bf16[512,1536]{1,0:T(8,128)(2,1)S(1)}, u32[]{:S(2)}, u32[]{:S(2)}) collective-permute-start(bf16[512,1536]{1,0:T(8,128)(2,1)} %copy-done.23), channel_id=1, source_target_pairs={{0,1},{1,0},{2,3},{3,2},{4,5},{5,4},{6,7},{7,6},{8,9},{9,8},{10,11... | collective-permute-start | bytes 4718600 | tf_op jit(solution)/shard_map/ppermute | solution.py:108
  216.5 24.6 %all-to-all-start.5 = ((bf16[4,2,64,1536]{3,2,1,0:T(8,128)(2,1)}), bf16[4,2,64,1536]{3,2,1,0:T(8,128)(2,1)}, u32[]{:S(2)}, u32[]{:S(2)}) async-start(bf16[4,2,64,1536]{3,2,1,0:T(8,128)(2,1)} %broadcast_in_dim.130), calls=%async_computation.5 | async-start | bytes 3145728 | tf_op jit(solution)/shard_map/all_to_all | solution.py:58
  223.3 17.9 %collective-permute-start.15 = (bf16[192,1280]{1,0:T(8,128)(2,1)}, bf16[192,1280]{1,0:T(8,128)(2,1)}, u32[]{:S(2)}, u32[]{:S(2)}) collective-permute-start(bf16[192,1280]{1,0:T(8,128)(2,1)} %get-tuple-element.194), channel_id=1, source_target_pairs={{0,64},{16,80},{32,96},{48,112},{64,0},{80,16},{96,32},{112,48},{1... | collective-permute-start | bytes 1474568 | tf_op jit(solution)/shard_map/ppermute | solution.py:91
  242.6 24.4 %all-to-all-start.6 = ((bf16[4,128,1536]{2,1,0:T(8,128)(2,1)}), bf16[4,128,1536]{2,1,0:T(8,128)(2,1)S(1)}, u32[]{:S(2)}, u32[]{:S(2)}) async-start(bf16[4,128,1536]{2,1,0:T(8,128)(2,1)} %bitcast.85), calls=%async_computation.7 | async-start | bytes 3145728 | tf_op jit(solution)/shard_map/all_to_all | solution.py:58
  246.2 80.6 %all-gather.11.cloned.1.call-start = ((), (), s32[]{:S(2)}) async-start(), calls=%async_computation.15 | async-start | bytes 4915200 | tf_op jit(solution)/shard_map/all_gather | solution.py:99
  247.4 15.4 %collective-permute-start.18 = (bf16[192,1280]{1,0:T(8,128)(2,1)S(1)}, bf16[192,1280]{1,0:T(8,128)(2,1)S(1)}, u32[]{:S(2)}, u32[]{:S(2)}) collective-permute-start(bf16[192,1280]{1,0:T(8,128)(2,1)S(1)} %add_convert_fusion.4), channel_id=1, source_target_pairs={{0,2},{2,0},{4,6},{6,4},{8,10},{10,8},{12,14},{14,12},{1,3},{3,1},... | collective-permute-start | bytes 1474568 | tf_op jit(solution)/shard_map/ppermute | solution.py:529
  270.1 25.9 %all-to-all-start.7 = ((bf16[8,208,512]{2,1,0:T(8,128)(2,1)}), bf16[8,208,512]{2,1,0:T(8,128)(2,1)S(1)}, u32[]{:S(2)}, u32[]{:S(2)}) async-start(bf16[8,208,512]{2,1,0:T(8,128)(2,1)} %bitcast.89), calls=%async_computation.8 | async-start | bytes 3407872 | tf_op jit(solution)/shard_map/all_to_all | solution.py:54
  281.7 19.6 %collective-permute-start.20 = (bf16[192,640]{1,0:T(8,128)(2,1)}, bf16[192,640]{1,0:T(8,128)(2,1)}, u32[]{:S(2)}, u32[]{:S(2)}) collective-permute-start(bf16[192,640]{1,0:T(8,128)(2,1)} %get-tuple-element.202), channel_id=1, source_target_pairs={{0,64},{16,80},{32,96},{48,112},{64,0},{80,16},{96,32},{112,48},{1... | collective-permute-start | bytes 737288 | tf_op jit(solution)/shard_map/ppermute | solution.py:91
  302.5 10.7 %collective-permute-start.21 = (bf16[192,640]{1,0:T(8,128)(2,1)S(1)}, bf16[192,640]{1,0:T(8,128)(2,1)}, u32[]{:S(2)}, u32[]{:S(2)}) collective-permute-start(bf16[192,640]{1,0:T(8,128)(2,1)S(1)} %add_convert_fusion.5), channel_id=1, source_target_pairs={{0,2},{2,0},{4,6},{6,4},{8,10},{10,8},{12,14},{14,12},{1,3},{3,1},... | collective-permute-start | bytes 737288 | tf_op jit(solution)/shard_map/ppermute | solution.py:556
  303.0 10.1 %collective-permute-start.22 = (bf16[64,1536]{1,0:T(8,128)(2,1)}, bf16[64,1536]{1,0:T(8,128)(2,1)}, u32[]{:S(2)}, u32[]{:S(2)}) collective-permute-start(bf16[64,1536]{1,0:T(8,128)(2,1)} %select_convert_fusion), channel_id=1, source_target_pairs={{0,2},{2,0},{4,6},{6,4},{8,10},{10,8},{12,14},{14,12},{1,3},{3,1},... | collective-permute-start | bytes 589832 | tf_op jit(solution)/shard_map/ppermute | solution.py:557
  313.2 45.5 %all-to-all-start.8 = ((bf16[8,400,512]{2,1,0:T(8,128)(2,1)}), bf16[8,400,512]{2,1,0:T(8,128)(2,1)S(1)}, u32[]{:S(2)}, u32[]{:S(2)}) async-start(bf16[8,400,512]{2,1,0:T(8,128)(2,1)} %pad_maximum_fusion), calls=%async_computation.10 | async-start | bytes 6553600 | tf_op jit(solution)/shard_map/all_to_all | solution.py:54
  316.9 55.3 %all-gather.13.cloned.1.call-start = ((), (), s32[]{:S(2)}) async-start(), calls=%async_computation.16 | async-start | bytes 2457600 | tf_op jit(solution)/shard_map/all_gather | solution.py:99
  (66 other events, 431.7 us)
Sparse Core Ops, SparseCore 0:
  61.3 36.4 all-gather.6
  100.5 37.1 all-gather.8
  178.2 40.6 reduce-scatter.2
  221.8 28.3 reduce-scatter.4
  269.4 43.0 all-gather.10
  319.6 52.4 all-gather.12

commit v7 on v6

--- a/solution.py
+++ b/solution.py
@@ -582,10 +582,6 @@
             ((16, 4 * HEAD), f32),
         ],
     )
-    sums, rest, down_part = tie(sums, rest, down_part)
-    grad_down_weight = assemble(
-        down_grad_kernel, down_part, [((shard, down_weight.shape[0]), f32)]
-    )[0]
     split_at = qcols + HEAD
     own_bias = lax.dynamic_slice(sums, (0, f * (split_at // 8)), (1, split_at // 8))
     own_value = lax.dynamic_slice(sums, (0, split_at + f * (HEAD // 8)), (1, HEAD // 8))
@@ -596,6 +592,12 @@
         ]
     )
     gain_sums = gain_sums + lax.ppermute(gain_sums, "tp", TP_SWAP)
+    gain_sums, grad_tokens, own_bias, own_value, down_part = tie(
+        gain_sums, grad_tokens, own_bias, own_value, down_part
+    )
+    grad_down_weight = assemble(
+        down_grad_kernel, down_part, [((shard, down_weight.shape[0]), f32)]
+    )[0]
 
     return (
         output,

time: 396 us -> 390 us (0.985)
  the two profiles are of different devices: /device:TPU:1 before, /device:TPU:3 now
where the time goes in v7:
time: 390 us; the launch traced here: 382 us
  waiting for transfers between devices  125 us (32%)
  starting transfers between devices  85.7 us (22%)
  Pallas kernels  61.5 us (16%)
  other arithmetic  51.5 us (13%)
  local copies, waits for them, and re-layouts  43.7 us (11%)
  between operations  15.3 us (4%)
    all_to_all x4, waiting for transfers between devices, spread(): return lax.all_to_all(part, axis, 0, 0, tiled=True)  54.7 us
    unnamed x110, local copies, waits for them, and re-layouts  24.3 us
    all_to_all x3, waiting for transfers between devices, spread_along_z(): lax.all_to_all(part, 'ctx', 0, 0, tiled=True, axis_index_groups=Z_GROUPS)  18.5 us
    all_to_all x4, starting transfers between devices, spread(): return lax.all_to_all(part, axis, 0, 0, tiled=True)  18 us
    all_to_all x2, waiting for transfers between devices, gather(): return lax.all_to_all(copies, axis, 0, 0, tiled=True)  17.1 us
    pallas_call x1, Pallas kernels, attention_grad(): local_call(attention_grad_kernel, outs, scratch, VMEM_BYTES)  14.9 us
    ppermute x2, starting transfers between devices, both_halves(): other = lax.ppermute(own, 'tp', TP_SWAP)  14.1 us
    pallas_call x2, Pallas kernels, feed_forward(): pl.pallas_call(ffn_kernel, grid_spec=pltpu.PrefetchScalarGridSpec(num_sca...  14.1 us
  transfers between devices with their start and end apart: 41, of which 16 were waited for; matrix products, arithmetic and copies ran while one was open for 17% of the time, Pallas kernels for 12%

profile of v7, /device:TPU:3, one launch (start us, length us, event | category | flops | bytes accessed | tf_op | source)
XLA Modules:
  0.0 382.5 jit_solution(13788041843986872418)
XLA Ops:
  25.2 6.3 %all-to-all-start = ((bf16[8,64,1536]{2,1,0:T(8,128)(2,1)}), bf16[8,64,1536]{2,1,0:T(8,128)(2,1)}, u32[]{:S(2)}, u32[]{:S(2)}) async-start(bf16[8,64,1536]{2,1,0:T(8,128)(2,1)} %broadcast_in_dim.109), calls=%async_computation | async-start | bytes 3145728 | tf_op jit(solution)/shard_map/all_to_all | solution.py:50
  57.4 3.1 collective-permute-start.8
  60.5 4.0 %all-to-all-start.1 = ((bf16[4,2,64,1536]{3,2,1,0:T(8,128)(2,1)}), bf16[4,2,64,1536]{3,2,1,0:T(8,128)(2,1)S(1)}, u32[]{:S(2)}, u32[]{:S(2)}) async-start(bf16[4,2,64,1536]{3,2,1,0:T(8,128)(2,1)} %broadcast_in_dim.122), calls=%async_computation.1 | async-start | bytes 3145728 | tf_op jit(solution)/shard_map/all_to_all | solution.py:58
  66.6 10.2 %shard_map.186 = (bf16[1024,128]{1,0:T(8,128)(2,1)}, bf16[1024,128]{1,0:T(8,128)(2,1)}, bf16[1024,128]{1,0:T(8,128)(2,1)}, bf16[1024,128]{1,0:T(8,128)(2,1)}, f3...) custom-call(bf16[512,1536]{1,0:T(8,128)(2,1)} %bitcast.20.mine, ...), custom_call_target="tpu_custom_call" | custom-call | flops 1000000 | bytes 100000 | tf_op jit(solution)/shard_map/pallas_call | solution.py:323
  76.8 7.8 %collective-permute-done.9 = bf16[192,1920]{1,0:T(8,128)(2,1)} collective-permute-done((bf16[192,1920]{1,0:T(8,128)(2,1)}, bf16[192,1920]{1,0:T(8,128)(2,1)}, u32[]{:S(2)}, u32[]{:S(2)}) %collective-permute-start.9) | collective-permute-done | bytes 737312 | tf_op jit(solution)/shard_map/ppermute | solution.py:483
  86.2 3.2 collective-permute-done.10
  92.4 4.9 %all-to-all-start.2 = ((bf16[8,64,1536]{2,1,0:T(8,128)(2,1)}), bf16[8,64,1536]{2,1,0:T(8,128)(2,1)S(1)}, u32[]{:S(2)}, u32[]{:S(2)}) async-start(bf16[8,64,1536]{2,1,0:T(8,128)(2,1)} %bitcast.87), calls=%async_computation.2 | async-start | bytes 3145728 | tf_op jit(solution)/shard_map/all_to_all | solution.py:54
  98.1 19.1 %all-to-all-done.2 = bf16[8,64,1536]{2,1,0:T(8,128)(2,1)S(1)} async-done(((bf16[8,64,1536]{2,1,0:T(8,128)(2,1)}), bf16[8,64,1536]{2,1,0:T(8,128)(2,1)S(1)}, u32[]{:S(2)}, u32[]{:S(2)}) %all-to-all-start.2) | async-done | bytes 1572896 | tf_op jit(solution)/shard_map/all_to_all | solution.py:54
  119.9 4.4 %all-to-all-start.3 = ((bf16[8,64,1536]{2,1,0:T(8,128)(2,1)}), bf16[8,64,1536]{2,1,0:T(8,128)(2,1)S(1)}, u32[]{:S(2)}, u32[]{:S(2)}) async-start(bf16[8,64,1536]{2,1,0:T(8,128)(2,1)} %broadcast_in_dim.129), calls=%async_computation.3 | async-start | bytes 3145728 | tf_op jit(solution)/shard_map/all_to_all | solution.py:50
  126.2 17.1 %all-to-all-done.3 = bf16[8,64,1536]{2,1,0:T(8,128)(2,1)S(1)} async-done(((bf16[8,64,1536]{2,1,0:T(8,128)(2,1)}), bf16[8,64,1536]{2,1,0:T(8,128)(2,1)S(1)}, u32[]{:S(2)}, u32[]{:S(2)}) %all-to-all-start.3) | async-done | bytes 1572896 | tf_op jit(solution)/shard_map/all_to_all | solution.py:50
  152.6 7.8 %shard_map.188 = (bf16[512,640]{1,0:T(8,128)(2,1)S(1)}, bf16[512,1280]{1,0:T(8,128)(2,1)S(1)}, bf16[512,1536]{1,0:T(8,128)(2,1)S(1)}) custom-call(s32[1]{0:T(128)} %bitcast.23.hi, bf16[512,1536]{1,0:T(8,128)(2,1)} %collective-permute-done.11.rows.left_other, bf16[512,1536]{1,0:T(8,128)(2,1)} %collective-permute-done.12.grad.left_other, ...), custom_call_target="tpu_custom_call" | custom-call | flops 1000000 | bytes 100000 | tf_op jit(solution)/shard_map/pallas_call | solution.py:369
  161.0 6.3 %shard_map.187 = (bf16[512,640]{1,0:T(8,128)(2,1)S(1)}, bf16[512,1280]{1,0:T(8,128)(2,1)S(1)}, bf16[512,1536]{1,0:T(8,128)(2,1)S(1)}) custom-call(s32[1]{0:T(128)} %bitcast.23.hi, bf16[512,1536]{1,0:T(8,128)(2,1)S(1)} %bitcast.79, bf16[512,1536]{1,0:T(8,128)(2,1)S(1)} %bitcast.82, bf16[768,1920]{1,0:T(8,128)(2,1)S(1)} %copy-done.3, ...), custom_call_target="tpu_custom_call" | custom-call | flops 1000000 | bytes 100000 | tf_op jit(solution)/shard_map/pallas_call | solution.py:369
  168.9 5.7 %shard_map.189 = bf16[1536,1280]{1,0:T(8,128)(2,1)S(1)} custom-call(bf16[512,1536]{1,0:T(8,128)(2,1)S(1)} %bitcast.80, bf16[512,1536]{1,0:T(8,128)(2,1)} %collective-permute-done.11.rows.left_other, bf16[512,1280]{1,0:T(8,128)(2,1)S(1)} %get-tuple-element.126.right_mine, bf16[512,1280]{1,0:T(8,128)(2,1)S(1)} %get-tuple-element.127.right_other), custom_call_target="tpu_custom_call" | custom-call | flops 1000000 | bytes 100000 | tf_op jit(solution)/shard_map/pallas_call | solution.py:345
  176.5 5.1 %all-to-all-start.4 = ((bf16[8,64,1536]{2,1,0:T(8,128)(2,1)}), bf16[8,64,1536]{2,1,0:T(8,128)(2,1)}, u32[]{:S(2)}, u32[]{:S(2)}) async-start(bf16[8,64,1536]{2,1,0:T(8,128)(2,1)} %bitcast.86), calls=%async_computation.4 | async-start | bytes 3145728 | tf_op jit(solution)/shard_map/all_to_all | solution.py:54
  185.6 5.3 %shard_map.190 = bf16[1536,640]{1,0:T(8,128)(2,1)} custom-call(bf16[512,1536]{1,0:T(8,128)(2,1)S(1)} %bitcast.83, bf16[512,1536]{1,0:T(8,128)(2,1)} %collective-permute-done.12.grad.left_other, bf16[512,640]{1,0:T(8,128)(2,1)S(1)} %copy-done.18, bf16[512,640]{1,0:T(8,128)(2,1)S(1)} %copy-done.15), custom_call_target="tpu_custom_call" | custom-call | flops 1000000 | bytes 100000 | tf_op jit(solution)/shard_map/pallas_call | solution.py:345
  206.8 5.7 %collective-permute-done.14 = bf16[64,1536]{1,0:T(8,128)(2,1)S(1)} collective-permute-done((bf16[64,1536]{1,0:T(8,128)(2,1)S(1)}, bf16[64,1536]{1,0:T(8,128)(2,1)S(1)}, u32[]{:S(2)}, u32[]{:S(2)}) %collective-permute-start.14) | collective-permute-done | bytes 196640 | tf_op jit(solution)/shard_map/ppermute | solution.py:520
  213.9 4.4 %all-to-all-start.5 = ((bf16[4,2,64,1536]{3,2,1,0:T(8,128)(2,1)}), bf16[4,2,64,1536]{3,2,1,0:T(8,128)(2,1)}, u32[]{:S(2)}, u32[]{:S(2)}) async-start(bf16[4,2,64,1536]{3,2,1,0:T(8,128)(2,1)} %broadcast_in_dim.130), calls=%async_computation.5 | async-start | bytes 3145728 | tf_op jit(solution)/shard_map/all_to_all | solution.py:58
  223.7 14.7 %all-to-all-done.5 = bf16[4,2,64,1536]{3,2,1,0:T(8,128)(2,1)} async-done(((bf16[4,2,64,1536]{3,2,1,0:T(8,128)(2,1)}), bf16[4,2,64,1536]{3,2,1,0:T(8,128)(2,1)}, u32[]{:S(2)}, u32[]{:S(2)}) %all-to-all-start.5) | async-done | bytes 1572896 | tf_op jit(solution)/shard_map/all_to_all | solution.py:58
  240.0 3.6 all-to-all-start.6
  245.9 14.9 %shard_map.192 = (bf16[512,1536]{1,0:T(8,128)(2,1)}, bf16[512,1536]{1,0:T(8,128)(2,1)}, bf16[1664,512]{1,0:T(8,128)(2,1)}) custom-call(bf16[512,1536]{1,0:T(8,128)(2,1)} %bitcast.30.branch_mine, bf16[512,1536]{1,0:T(8,128)(2,1)} %collective-permute-done.17.branch_other, bf16[512,1536]{1,0:T(8,128)(2,1)} %bitcast.20.mine, ...), custom_call_target="tpu_custom_call" | custom-call | flops 1000000 | bytes 100000 | tf_op jit(solution)/shard_map/pallas_call | solution.py:338
  261.1 3.3 all-to-all-done.6
  266.6 3.6 all-to-all-start.7
  270.2 3.4 add_convert_fusion
  277.8 3.0 collective-permute-start.20
  282.6 9.6 %all-to-all-done.7 = bf16[8,208,512]{2,1,0:T(8,128)(2,1)S(1)} async-done(((bf16[8,208,512]{2,1,0:T(8,128)(2,1)}), bf16[8,208,512]{2,1,0:T(8,128)(2,1)S(1)}, u32[]{:S(2)}, u32[]{:S(2)}) %all-to-all-start.7) | async-done | bytes 1703968 | tf_op jit(solution)/shard_map/all_to_all | solution.py:54
  292.2 4.7 %collective-permute-done.20 = bf16[192,640]{1,0:T(8,128)(2,1)} collective-permute-done((bf16[192,640]{1,0:T(8,128)(2,1)}, bf16[192,640]{1,0:T(8,128)(2,1)}, u32[]{:S(2)}, u32[]{:S(2)}) %collective-permute-start.20) | collective-permute-done | bytes 245792 | tf_op jit(solution)/shard_map/ppermute | solution.py:91
  303.1 5.1 %collective-permute-done.22 = bf16[64,1536]{1,0:T(8,128)(2,1)} collective-permute-done((bf16[64,1536]{1,0:T(8,128)(2,1)}, bf16[64,1536]{1,0:T(8,128)(2,1)}, u32[]{:S(2)}, u32[]{:S(2)}) %collective-permute-start.22) | collective-permute-done | bytes 196640 | tf_op jit(solution)/shard_map/ppermute | solution.py:557
  308.2 4.4 %all-to-all-start.8 = ((bf16[8,400,512]{2,1,0:T(8,128)(2,1)}), bf16[8,400,512]{2,1,0:T(8,128)(2,1)S(1)}, u32[]{:S(2)}, u32[]{:S(2)}) async-start(bf16[8,400,512]{2,1,0:T(8,128)(2,1)} %pad_maximum_fusion), calls=%async_computation.10 | async-start | bytes 6553600 | tf_op jit(solution)/shard_map/all_to_all | solution.py:54
  314.6 3.2 collective-permute-start.23
  324.1 5.4 %shard_map.193 = f32[192,2,4480]{2,1,0:T(2,128)} custom-call(bf16[8,192,1280]{2,1,0:T(8,128)(2,1)S(1)} %copy-done.13), custom_call_target="tpu_custom_call" | custom-call | flops 1000000 | bytes 100000 | tf_op jit(solution)/shard_map/pallas_call | solution.py:561
  329.6 23.9 %all-to-all-done.8.parts = bf16[8,400,512]{2,1,0:T(8,128)(2,1)S(1)} async-done(((bf16[8,400,512]{2,1,0:T(8,128)(2,1)}), bf16[8,400,512]{2,1,0:T(8,128)(2,1)S(1)}, u32[]{:S(2)}, u32[]{:S(2)}) %all-to-all-start.8) | async-done | bytes 3276832 | tf_op jit(solution)/shard_map/all_to_all | solution.py:54
  355.0 10.9 %collective-permute-start.25 = (f32[64,1536]{1,0:T(8,128)S(1)}, f32[64,1536]{1,0:T(8,128)S(1)}, u32[]{:S(2)}, u32[]{:S(2)}) collective-permute-start(f32[64,1536]{1,0:T(8,128)S(1)} %subtract_add_fusion), channel_id=1, source_target_pairs={{0,1},{1,0},{2,3},{3,2},{4,5},{5,4},{6,7},{7,6},{8,9},{9,8},{10,11... | collective-permute-start | bytes 1179656 | tf_op jit(solution)/shard_map/ppermute | solution.py:115
  (286 shorter events, 132.9 us)
Async XLA Ops:
  11.6 35.7 %collective-permute-start = (bf16[208,512]{1,0:T(8,128)(2,1)}, bf16[208,512]{1,0:T(8,128)(2,1)}, u32[]{:S(2)}, u32[]{:S(2)}) collective-permute-start(bf16[208,512]{1,0:T(8,128)(2,1)} %maximum_maximum_fusion), channel_id=1, source_target_pairs={{0,16},{16,32},{32,48},{48,0},{64,80},{80,96},{96,112},{112,64},{1... | collective-permute-start | bytes 638984 | tf_op jit(solution)/shard_map/ppermute | solution.py:72
  12.9 35.6 %collective-permute-start.1 = (bf16[208,512]{1,0:T(8,128)(2,1)}, bf16[208,512]{1,0:T(8,128)(2,1)}, u32[]{:S(2)}, u32[]{:S(2)}) collective-permute-start(bf16[208,512]{1,0:T(8,128)(2,1)} %maximum_maximum_fusion), channel_id=1, source_target_pairs={{0,48},{16,0},{32,16},{48,32},{64,112},{80,64},{96,80},{112,96},{1... | collective-permute-start | bytes 638984 | tf_op jit(solution)/shard_map/ppermute | solution.py:72
  14.4 35.0 %collective-permute-start.2 = (bf16[208,512]{1,0:T(8,128)(2,1)}, bf16[208,512]{1,0:T(8,128)(2,1)}, u32[]{:S(2)}, u32[]{:S(2)}) collective-permute-start(bf16[208,512]{1,0:T(8,128)(2,1)} %maximum_maximum_fusion), channel_id=1, source_target_pairs={{0,32},{16,48},{32,0},{48,16},{64,96},{80,112},{96,64},{112,80},{1... | collective-permute-start | bytes 638984 | tf_op jit(solution)/shard_map/ppermute | solution.py:72
  16.0 28.6 %collective-permute-start.3 = (bf16[208,512]{1,0:T(8,128)(2,1)}, bf16[208,512]{1,0:T(8,128)(2,1)}, u32[]{:S(2)}, u32[]{:S(2)}) collective-permute-start(bf16[208,512]{1,0:T(8,128)(2,1)} %maximum_maximum_fusion), channel_id=1, source_target_pairs={{0,64},{16,80},{32,96},{48,112},{64,0},{80,16},{96,32},{112,48},{1... | collective-permute-start | bytes 638984 | tf_op jit(solution)/shard_map/ppermute | solution.py:452
  19.5 23.8 %collective-permute-start.7 = (bf16[64,1536]{1,0:T(8,128)(2,1)}, bf16[64,1536]{1,0:T(8,128)(2,1)}, u32[]{:S(2)}, u32[]{:S(2)}) collective-permute-start(bf16[64,1536]{1,0:T(8,128)(2,1)} %dynamic-slice_convert_fusion), channel_id=1, source_target_pairs={{0,2},{2,0},{4,6},{6,4},{8,10},{10,8},{12,14},{14,12},{1,3},{3,1},... | collective-permute-start | bytes 589832 | tf_op jit(solution)/shard_map/ppermute | solution.py:478
  25.2 30.8 %all-to-all-start = ((bf16[8,64,1536]{2,1,0:T(8,128)(2,1)}), bf16[8,64,1536]{2,1,0:T(8,128)(2,1)}, u32[]{:S(2)}, u32[]{:S(2)}) async-start(bf16[8,64,1536]{2,1,0:T(8,128)(2,1)} %broadcast_in_dim.109), calls=%async_computation | async-start | bytes 3145728 | tf_op jit(solution)/shard_map/all_to_all | solution.py:50
  31.5 115.4 %all-gather.7.cloned.1.call-start = ((), (), s32[]{:S(2)}) async-start(), calls=%async_computation.11 | async-start | bytes 3686400 | tf_op jit(solution)/shard_map/all_gather | solution.py:78
  47.3 8.6 %collective-permute-start.6 = (bf16[208,512]{1,0:T(8,128)(2,1)}, bf16[208,512]{1,0:T(8,128)(2,1)S(1)}, u32[]{:S(2)}, u32[]{:S(2)}) collective-permute-start(bf16[208,512]{1,0:T(8,128)(2,1)} %collective-permute-done.3), channel_id=1, source_target_pairs={{0,32},{16,48},{32,0},{48,16},{64,96},{80,112},{96,64},{112,80},{1... | collective-permute-start | bytes 638984 | tf_op jit(solution)/shard_map/ppermute | solution.py:72
  57.4 9.2 %collective-permute-start.8 = (bf16[512,1536]{1,0:T(8,128)(2,1)}, bf16[512,1536]{1,0:T(8,128)(2,1)}, u32[]{:S(2)}, u32[]{:S(2)}) collective-permute-start(bf16[512,1536]{1,0:T(8,128)(2,1)} %bitcast.20.mine), channel_id=1, source_target_pairs={{0,1},{1,0},{2,3},{3,2},{4,5},{5,4},{6,7},{7,6},{8,9},{9,8},{10,11... | collective-permute-start | bytes 4718600 | tf_op jit(solution)/shard_map/ppermute | solution.py:104
  60.5 24.5 %all-to-all-start.1 = ((bf16[4,2,64,1536]{3,2,1,0:T(8,128)(2,1)}), bf16[4,2,64,1536]{3,2,1,0:T(8,128)(2,1)S(1)}, u32[]{:S(2)}, u32[]{:S(2)}) async-start(bf16[4,2,64,1536]{3,2,1,0:T(8,128)(2,1)} %broadcast_in_dim.122), calls=%async_computation.1 | async-start | bytes 3145728 | tf_op jit(solution)/shard_map/all_to_all | solution.py:58
  64.5 20.1 %collective-permute-start.9 = (bf16[192,1920]{1,0:T(8,128)(2,1)}, bf16[192,1920]{1,0:T(8,128)(2,1)}, u32[]{:S(2)}, u32[]{:S(2)}) collective-permute-start(bf16[192,1920]{1,0:T(8,128)(2,1)} %pad_maximum_fusion.4), channel_id=1, source_target_pairs={{0,64},{16,80},{32,96},{48,112},{64,0},{80,16},{96,32},{112,48},{1... | collective-permute-start | bytes 2211848 | tf_op jit(solution)/shard_map/ppermute | solution.py:483
  92.4 24.8 %all-to-all-start.2 = ((bf16[8,64,1536]{2,1,0:T(8,128)(2,1)}), bf16[8,64,1536]{2,1,0:T(8,128)(2,1)S(1)}, u32[]{:S(2)}, u32[]{:S(2)}) async-start(bf16[8,64,1536]{2,1,0:T(8,128)(2,1)} %bitcast.87), calls=%async_computation.2 | async-start | bytes 3145728 | tf_op jit(solution)/shard_map/all_to_all | solution.py:54
  97.3 49.6 %all-gather.9.cloned.1.call-start = ((), (), s32[]{:S(2)}) async-start(), calls=%async_computation.12 | async-start | bytes 3686400 | tf_op jit(solution)/shard_map/all_gather | solution.py:78
  119.9 23.4 %all-to-all-start.3 = ((bf16[8,64,1536]{2,1,0:T(8,128)(2,1)}), bf16[8,64,1536]{2,1,0:T(8,128)(2,1)S(1)}, u32[]{:S(2)}, u32[]{:S(2)}) async-start(bf16[8,64,1536]{2,1,0:T(8,128)(2,1)} %broadcast_in_dim.129), calls=%async_computation.3 | async-start | bytes 3145728 | tf_op jit(solution)/shard_map/all_to_all | solution.py:50
  124.3 94.6 %reduce-scatter.3.cloned.1.call-start = ((), (), s32[]{:S(2)}) async-start(), calls=%async_computation.13 | async-start | bytes 4915200 | tf_op jit(solution)/shard_map/reduce_scatter | solution.py:82
  124.3 22.6 %collective-permute-start.12 = (bf16[512,1536]{1,0:T(8,128)(2,1)S(1)}, bf16[512,1536]{1,0:T(8,128)(2,1)}, u32[]{:S(2)}, u32[]{:S(2)}) collective-permute-start(bf16[512,1536]{1,0:T(8,128)(2,1)S(1)} %bitcast.81), channel_id=1, source_target_pairs={{0,1},{1,0},{2,3},{3,2},{4,5},{5,4},{6,7},{7,6},{8,9},{9,8},{10,11... | collective-permute-start | bytes 4718600 | tf_op jit(solution)/shard_map/ppermute | solution.py:104
  176.5 25.7 %all-to-all-start.4 = ((bf16[8,64,1536]{2,1,0:T(8,128)(2,1)}), bf16[8,64,1536]{2,1,0:T(8,128)(2,1)}, u32[]{:S(2)}, u32[]{:S(2)}) async-start(bf16[8,64,1536]{2,1,0:T(8,128)(2,1)} %bitcast.86), calls=%async_computation.4 | async-start | bytes 3145728 | tf_op jit(solution)/shard_map/all_to_all | solution.py:54
  202.2 20.0 %collective-permute-start.16 = (bf16[512,1536]{1,0:T(8,128)(2,1)}, bf16[512,1536]{1,0:T(8,128)(2,1)S(1)}, u32[]{:S(2)}, u32[]{:S(2)}) collective-permute-start(bf16[512,1536]{1,0:T(8,128)(2,1)} %copy-done.23), channel_id=1, source_target_pairs={{0,1},{1,0},{2,3},{3,2},{4,5},{5,4},{6,7},{7,6},{8,9},{9,8},{10,11... | collective-permute-start | bytes 4718600 | tf_op jit(solution)/shard_map/ppermute | solution.py:108
  213.9 24.5 %all-to-all-start.5 = ((bf16[4,2,64,1536]{3,2,1,0:T(8,128)(2,1)}), bf16[4,2,64,1536]{3,2,1,0:T(8,128)(2,1)}, u32[]{:S(2)}, u32[]{:S(2)}) async-start(bf16[4,2,64,1536]{3,2,1,0:T(8,128)(2,1)} %broadcast_in_dim.130), calls=%async_computation.5 | async-start | bytes 3145728 | tf_op jit(solution)/shard_map/all_to_all | solution.py:58
  218.3 55.4 %reduce-scatter.5.cloned.1.call-start = ((), (), s32[]{:S(2)}) async-start(), calls=%async_computation.14 | async-start | bytes 2457600 | tf_op jit(solution)/shard_map/reduce_scatter | solution.py:82
  221.1 17.4 %collective-permute-start.15 = (bf16[192,1280]{1,0:T(8,128)(2,1)}, bf16[192,1280]{1,0:T(8,128)(2,1)}, u32[]{:S(2)}, u32[]{:S(2)}) collective-permute-start(bf16[192,1280]{1,0:T(8,128)(2,1)} %get-tuple-element.198), channel_id=1, source_target_pairs={{0,64},{16,80},{32,96},{48,112},{64,0},{80,16},{96,32},{112,48},{1... | collective-permute-start | bytes 1474568 | tf_op jit(solution)/shard_map/ppermute | solution.py:91
  240.0 24.4 %all-to-all-start.6 = ((bf16[4,128,1536]{2,1,0:T(8,128)(2,1)}), bf16[4,128,1536]{2,1,0:T(8,128)(2,1)S(1)}, u32[]{:S(2)}, u32[]{:S(2)}) async-start(bf16[4,128,1536]{2,1,0:T(8,128)(2,1)} %bitcast.84), calls=%async_computation.7 | async-start | bytes 3145728 | tf_op jit(solution)/shard_map/all_to_all | solution.py:58
  243.6 78.4 %all-gather.11.cloned.1.call-start = ((), (), s32[]{:S(2)}) async-start(), calls=%async_computation.15 | async-start | bytes 4915200 | tf_op jit(solution)/shard_map/all_gather | solution.py:99
  244.8 16.3 %collective-permute-start.18 = (bf16[192,1280]{1,0:T(8,128)(2,1)S(1)}, bf16[192,1280]{1,0:T(8,128)(2,1)S(1)}, u32[]{:S(2)}, u32[]{:S(2)}) collective-permute-start(bf16[192,1280]{1,0:T(8,128)(2,1)S(1)} %add_convert_fusion.4), channel_id=1, source_target_pairs={{0,2},{2,0},{4,6},{6,4},{8,10},{10,8},{12,14},{14,12},{1,3},{3,1},... | collective-permute-start | bytes 1474568 | tf_op jit(solution)/shard_map/ppermute | solution.py:529
  260.8 9.4 %collective-permute-start.19 = (bf16[512,1536]{1,0:T(8,128)(2,1)}, bf16[512,1536]{1,0:T(8,128)(2,1)}, u32[]{:S(2)}, u32[]{:S(2)}) collective-permute-start(bf16[512,1536]{1,0:T(8,128)(2,1)} %get-tuple-element.154), channel_id=1, source_target_pairs={{0,1},{1,0},{2,3},{3,2},{4,5},{5,4},{6,7},{7,6},{8,9},{9,8},{10,11... | collective-permute-start | bytes 4718600 | tf_op jit(solution)/shard_map/ppermute | solution.py:108
  266.6 25.5 %all-to-all-start.7 = ((bf16[8,208,512]{2,1,0:T(8,128)(2,1)}), bf16[8,208,512]{2,1,0:T(8,128)(2,1)S(1)}, u32[]{:S(2)}, u32[]{:S(2)}) async-start(bf16[8,208,512]{2,1,0:T(8,128)(2,1)} %bitcast.89), calls=%async_computation.8 | async-start | bytes 3407872 | tf_op jit(solution)/shard_map/all_to_all | solution.py:54
  277.8 19.1 %collective-permute-start.20 = (bf16[192,640]{1,0:T(8,128)(2,1)}, bf16[192,640]{1,0:T(8,128)(2,1)}, u32[]{:S(2)}, u32[]{:S(2)}) collective-permute-start(bf16[192,640]{1,0:T(8,128)(2,1)} %get-tuple-element.206), channel_id=1, source_target_pairs={{0,64},{16,80},{32,96},{48,112},{64,0},{80,16},{96,32},{112,48},{1... | collective-permute-start | bytes 737288 | tf_op jit(solution)/shard_map/ppermute | solution.py:91
  298.2 10.1 %collective-permute-start.21 = (bf16[192,640]{1,0:T(8,128)(2,1)S(1)}, bf16[192,640]{1,0:T(8,128)(2,1)}, u32[]{:S(2)}, u32[]{:S(2)}) collective-permute-start(bf16[192,640]{1,0:T(8,128)(2,1)S(1)} %add_convert_fusion.5), channel_id=1, source_target_pairs={{0,2},{2,0},{4,6},{6,4},{8,10},{10,8},{12,14},{14,12},{1,3},{3,1},... | collective-permute-start | bytes 737288 | tf_op jit(solution)/shard_map/ppermute | solution.py:556
  299.3 8.9 %collective-permute-start.22 = (bf16[64,1536]{1,0:T(8,128)(2,1)}, bf16[64,1536]{1,0:T(8,128)(2,1)}, u32[]{:S(2)}, u32[]{:S(2)}) collective-permute-start(bf16[64,1536]{1,0:T(8,128)(2,1)} %select_convert_fusion), channel_id=1, source_target_pairs={{0,2},{2,0},{4,6},{6,4},{8,10},{10,8},{12,14},{14,12},{1,3},{3,1},... | collective-permute-start | bytes 589832 | tf_op jit(solution)/shard_map/ppermute | solution.py:557
  308.2 45.2 %all-to-all-start.8 = ((bf16[8,400,512]{2,1,0:T(8,128)(2,1)}), bf16[8,400,512]{2,1,0:T(8,128)(2,1)S(1)}, u32[]{:S(2)}, u32[]{:S(2)}) async-start(bf16[8,400,512]{2,1,0:T(8,128)(2,1)} %pad_maximum_fusion), calls=%async_computation.10 | async-start | bytes 6553600 | tf_op jit(solution)/shard_map/all_to_all | solution.py:54
  312.6 58.1 %all-gather.13.cloned.1.call-start = ((), (), s32[]{:S(2)}) async-start(), calls=%async_computation.16 | async-start | bytes 2457600 | tf_op jit(solution)/shard_map/all_gather | solution.py:99
  355.0 14.7 %collective-permute-start.25 = (f32[64,1536]{1,0:T(8,128)S(1)}, f32[64,1536]{1,0:T(8,128)S(1)}, u32[]{:S(2)}, u32[]{:S(2)}) collective-permute-start(f32[64,1536]{1,0:T(8,128)S(1)} %subtract_add_fusion), channel_id=1, source_target_pairs={{0,1},{1,0},{2,3},{3,2},{4,5},{5,4},{6,7},{7,6},{8,9},{9,8},{10,11... | collective-permute-start | bytes 1179656 | tf_op jit(solution)/shard_map/ppermute | solution.py:115
  (63 other events, 386.8 us)
Sparse Core Ops, SparseCore 0:
  60.7 36.1 all-gather.6
  99.8 36.9 all-gather.8
  176.6 41.3 reduce-scatter.2
  221.8 28.4 reduce-scatter.4
  266.7 43.8 all-gather.10
  320.0 47.6 all-gather.12
